TPU v7x, 128 devices: a whole 4x4x4 slice. The times are simulated.
128 devices in a mesh: dp: 8 (over z_lo, y), ctx: 16 (over x, z_hi, core).
Axes of the slice: x: 4, y: 4, z: 4 (z_hi: 2, z_lo: 2; z = z_hi * 2 + z_lo), core: 2. Of those that a mesh axis runs over, the one named last changes fastest.
Arguments:
- tokens: bfloat16 [32, 4096, 768], P('dp', 'ctx'), may hold values from -6 to 6
- w_qkv: bfloat16 [768, 2304], replicated, may hold values from -0.21650635 to 0.21650635
- w_out: bfloat16 [768, 768], replicated, may hold values from -0.21875 to 0.21875
- ln_gain: float32 [768], replicated, may hold values from 0.25 to 1.75
- cache: bfloat16 [16384, 768], P(('dp', 'ctx')), may hold values from -0.5051815 to 0.5051815
- positive: int32 [32], replicated, may hold values from 0 to 16383
- lengths: int32 [32], P('dp'), may hold values from 2048 to 4096, as said below
Outputs:
- hidden: bfloat16 [32, 4096, 768], P('dp', 'ctx')
- loss: float32 [], replicated
- grad_out: float32 [768, 768], P(('dp', 'ctx'))
Inputs may be any that keep to these rules, and one draw needn't show every extreme that they name: `lengths`: some document has exactly 4096 valid tokens in every draw.
All inputs are finite; a program needn't handle non-finite values.
Results may differ from a plain program's by a relative error of at most 0.003.
The roundings to bfloat16 on the way count: a program that leaves them out, or rounds other values in their place, can miss the bound.
Values may be sent and summed in bfloat16 or wider, within the bound.
No kernel may reach another device: no remote copies, remote signals or barrier semaphores. Data moves between devices by JAX's collectives and lax.ppermute only.
A program may use at most 128 MiB of HBM per device.

v0:
```python
import functools
import math

import jax
import jax.numpy as jnp
from jax import lax
from jax.experimental import pallas as pl
from jax.experimental.pallas import tpu as pltpu
from jax.sharding import PartitionSpec as P

H = 12
WIN = 256
TAU = 0.02
FAR = 1e32
NT = (((1,), (1,)), ((), ()))
TN = (((0,), (0,)), ((), ()))
HIGHEST = lax.Precision.HIGHEST
VMEM = pl.BlockSpec(memory_space=pltpu.VMEM)
SMEM = pl.BlockSpec(memory_space=pltpu.SMEM)
ANY = pl.BlockSpec(memory_space=pl.ANY)


def swap(value, axis, bits):
    return lax.ppermute(value, axis, [(i, i ^ bits) for i in range(lax.axis_size(axis))])


def from_x(value, k):
    size = lax.axis_size("ctx")
    return lax.ppermute(value, "ctx", [((c + 4 * k) % size, c) for c in range(size)])


def from_y(value, k):
    return lax.ppermute(value, "dp", [((d & 4) | ((d + k) & 3), d) for d in range(lax.axis_size("dp"))])


def from_z(value, k):
    n_dp, n_ctx = lax.axis_size("dp"), lax.axis_size("ctx")
    pairs = []
    for d in range(n_dp):
        for c in range(n_ctx):
            z = ((c & 2) + (d >> 2) + k) & 3
            pairs.append((((z & 1) * 4 + (d & 3)) * n_ctx + (c & ~2) + (z & 2), d * n_ctx + c))
    return lax.ppermute(value, ("dp", "ctx"), pairs)


def from_plane(value, k, last):
    n_dp, n_ctx = lax.axis_size("dp"), lax.axis_size("ctx")
    pairs = []
    for d in range(n_dp):
        for c in range(n_ctx):
            along_y = (c & 1 == 1) == last
            source = ((d & 4) | ((d + k) & 3), c) if along_y else (d, (c + 4 * k) % n_ctx)
            pairs.append((source[0] * n_ctx + source[1], d * n_ctx + c))
    return lax.ppermute(value, ("dp", "ctx"), pairs)


def around(value, fetch):
    return [value] + [fetch(value, k) for k in (1, 2, 3)]


def here():
    return lax.axis_index("dp"), lax.axis_index("ctx")


def in_hbm(value):
    return pltpu.with_memory_space_constraint(value, pltpu.HBM)


def call(kernel, out_shape, in_specs, out_specs, limit=16, flops=0, moved=0, **keywords):
    return pl.pallas_call(
        kernel,
        out_shape=out_shape,
        in_specs=in_specs,
        out_specs=out_specs,
        compiler_params=pltpu.CompilerParams(vmem_limit_bytes=limit * 2**20),
        cost_estimate=pl.CostEstimate(flops=flops, bytes_accessed=moved, transcendentals=0),
        **keywords,
    )


def f32(*shape):
    return jax.ShapeDtypeStruct(shape, jnp.float32)


def bf16(*shape):
    return jax.ShapeDtypeStruct(shape, jnp.bfloat16)


def slopes_of(heads):
    largest = 2 ** int(math.floor(math.log2(heads)))
    listed = [2.0 ** (-8.0 * (h + 1) / largest) for h in range(largest)]
    return listed + [2.0 ** (-4.0 * (2 * m + 1) / largest) for m in range(heads - largest)]


def thirds(value):
    high = value.astype(jnp.bfloat16)
    rest = value - high.astype(jnp.float32)
    middle = rest.astype(jnp.bfloat16)
    low = (rest - middle.astype(jnp.float32)).astype(jnp.bfloat16)
    parts = [p.astype(jnp.float32) for p in (high, middle, low)]
    return jnp.concatenate(parts, axis=0).astype(jnp.bfloat16)


def folded(products):
    rows = products.shape[0] // 3
    return products[0:rows] + products[rows : 2 * rows] + products[2 * rows :]


def attend_kernel(first, *refs):
    far = refs[3]
    lax.fori_loop(0, far.shape[0], lambda index, _: attend_doc(first + index, index, *refs), None)


def attend_doc(
    doc, index, lengths, tok, near, far, qk, v_turned, w, w_v_turned, w_out, gain, *refs
):
    hidden, mixed_all, normed, rstd_out, pool, keys, values, dist, hidden_here, sem = refs[-10:]
    docs, tb, width = tok.shape
    ext = tb + 2 * WIN
    own = pl.ds(pl.multiple_of(doc * tb, tb), tb)
    mixed = mixed_all.at[:, own]
    ctx = lax.axis_index("ctx")
    start, length = ctx * tb, lengths[doc]
    right = lax.rem(ctx, 2) == 0
    ends = far[index], near[doc]
    rows = jnp.concatenate([jnp.where(right, *ends), jnp.where(right, *ends[::-1])], axis=0)
    new = jnp.dot(rows, w[:, width : 2 * width], preferred_element_type=jnp.float32).astype(jnp.bfloat16)
    keys[0:WIN] = new[0:WIN]
    keys[WIN : WIN + tb] = qk[doc, :, width:]
    keys[WIN + tb :] = new[WIN:]
    new = lax.dot_general(w_v_turned[...], rows, NT, preferred_element_type=jnp.float32).astype(jnp.bfloat16)
    values[:, 0:WIN] = new[:, 0:WIN]
    values[:, WIN : WIN + tb] = v_turned[:, own]
    values[:, WIN + tb :] = new[:, WIN:]
    j = lax.broadcasted_iota(jnp.int32, (ext, tb), 0) - WIN
    away = jnp.abs(lax.broadcasted_iota(jnp.int32, (ext, tb), 1) - j)
    kpos = start + j
    seen = (away <= WIN) & (((kpos >= 0) & (kpos < length)) | (away == 0))
    dist[...] = jnp.where(seen, away.astype(jnp.float32), FAR)
    half = lax.broadcasted_iota(jnp.int32, (tb, 128), 1) < 64
    slopes = slopes_of(H)
    lanes = 128
    span = lanes + 2 * WIN

    def scores_of(pair):
        cols = pl.ds(pair * 128, 128)
        query, zero = qk[doc, :, cols] * jnp.bfloat16(0.125), jnp.bfloat16(0)
        both = jnp.concatenate([jnp.where(half, query, zero), jnp.where(half, zero, query)], axis=0)
        return lax.dot_general(keys[:, cols], both, NT, preferred_element_type=jnp.float32)

    upcoming = scores_of(0)
    for pair in range(H // 2):
        scores = upcoming
        if pair + 1 < H // 2:
            upcoming = scores_of(pair + 1)
        for part in range(2):
            columns = []
            for low in range(0, tb, lanes):
                score = scores[low : low + span, part * tb + low : part * tb + low + lanes]
                score = score - slopes[2 * pair + part] * dist[pl.ds(low, span), pl.ds(low, lanes)]
                expo = jnp.exp(score - jnp.max(score, axis=0, keepdims=True))
                weights = (expo * (1.0 / jnp.sum(expo, axis=0, keepdims=True))).astype(jnp.bfloat16)
                above, below = low, ext - span - low
                pieces = [weights]
                if above:
                    pieces = [jnp.zeros((above, lanes), jnp.bfloat16)] + pieces
                if below:
                    pieces = pieces + [jnp.zeros((below, lanes), jnp.bfloat16)]
                columns.append(jnp.concatenate(pieces, axis=0))
            weights = jnp.concatenate(columns, axis=1)
            head = pl.ds(pair * 128 + part * 64, 64)
            mixed[head, :] = jnp.dot(values[head, :], weights, preferred_element_type=jnp.float32).astype(jnp.bfloat16)
    summed = tok[doc].astype(jnp.float32) + lax.dot_general(
        mixed[...], w_out[...], TN, preferred_element_type=jnp.float32
    )
    centred = summed - jnp.mean(summed, axis=1, keepdims=True)
    rstd = lax.rsqrt(jnp.mean(centred * centred, axis=1, keepdims=True) + 1e-05)
    unit = centred * rstd
    hidden_f = unit * gain[...].reshape(1, width)
    hidden_here[...] = hidden_f.astype(jnp.bfloat16)
    leaving = pltpu.make_async_copy(hidden_here, hidden.at[doc], sem)
    leaving.start()
    normed[doc] = unit.astype(jnp.bfloat16)
    rstd_out[doc] = jnp.broadcast_to(rstd, rstd_out.shape[1:])
    keep = start + lax.broadcasted_iota(jnp.int32, (tb, 1), 0) < length
    pool[doc] = jnp.sum(jnp.where(keep, hidden_f, 0.0), axis=0, keepdims=True) / length.astype(jnp.float32)
    leaving.wait()


def attend(first, before, lengths, tokens, near, far, qk, v_turned, w_qkv, w_v_turned, w_out, gain):
    docs, tb, width = tokens.shape
    ext = tb + 2 * WIN
    out_shape = (bf16(docs, tb, width), bf16(width, docs * tb), bf16(docs, tb, width), f32(docs, tb, 128), f32(docs, 1, width))
    out_specs = (ANY,) + (VMEM,) * 4
    operands = [lengths, tokens, near, far, qk, v_turned, w_qkv, w_v_turned, w_out, gain]
    in_specs = [SMEM] + [VMEM] * 9
    aliases = {}
    if before is not None:
        aliases = {len(operands) + k: k for k in range(len(out_shape))}
        operands = operands + list(before)
        in_specs = in_specs + list(out_specs)
    return call(
        functools.partial(attend_kernel, first),
        out_shape,
        in_specs,
        out_specs,
        limit=24,
        flops=5 * 2 * far.shape[0] * tb * ext * width,
        moved=4 * 2**20,
        scratch_shapes=[
            pltpu.VMEM((ext, width), jnp.bfloat16),
            pltpu.VMEM((width, ext), jnp.bfloat16),
            pltpu.VMEM((ext, tb), jnp.float32),
            pltpu.VMEM((tb, width), jnp.bfloat16),
            pltpu.SemaphoreType.DMA,
        ],
        input_output_aliases=aliases,
        name="attend",
    )(*operands)


def prepare_kernel(tok, w, qk, v_turned, w_v_turned, *later):
    width = tok.shape[2]
    for index, late in enumerate(later):

        @pl.when(pl.program_id(0) == index + 2)
        def _():
            late[...] = tok[...]

    @pl.when(pl.program_id(0) == 0)
    def _():
        w_v_turned[...] = w[:, 2 * width :].T

    rows = tok[0]
    qk[0] = jnp.dot(rows, w[:, 0 : 2 * width], preferred_element_type=jnp.float32).astype(jnp.bfloat16)
    v_turned[...] = lax.dot_general(w_v_turned[...], rows, NT, preferred_element_type=jnp.float32).astype(jnp.bfloat16)


def prepare(tokens, w_qkv):
    docs, tb, width = tokens.shape
    return call(
        prepare_kernel,
        (bf16(docs, tb, 2 * width), bf16(width, docs * tb), bf16(width, width)) + (bf16(1, tb, width),) * (docs - 2),
        [
            pl.BlockSpec((1, tb, width), lambda i: (i, 0, 0)),
            pl.BlockSpec(w_qkv.shape, lambda i: (0, 0), pipeline_mode=pl.Buffered(1)),
        ],
        (
            pl.BlockSpec((1, tb, 2 * width), lambda i: (i, 0, 0)),
            pl.BlockSpec((width, tb), lambda i: (0, i)),
            pl.BlockSpec((width, width), lambda i: (0, 0)),
        )
        + (pl.BlockSpec((1, tb, width), lambda i: (0, 0, 0)),) * (docs - 2),
        flops=2 * docs * tb * width * 3 * width,
        moved=11 * 2**20,
        grid=(docs,),
        name="prepare",
    )(tokens, w_qkv)


def row_ids(k, shape, dim):
    dp, ctx = here()
    place = lax.broadcasted_iota(jnp.int32, shape, dim)
    return (((dp & 4) | ((dp + k) & 3)) * 16 + ctx) * shape[dim] + place


def stack_kernel(pool, target, out):
    docs = pool.shape[0]
    for doc in range(docs):
        out[doc : doc + 1, :] = pool[doc]
    out[docs:, :] = target[...]


def add_kernel(*refs):
    terms = [ref[...] for ref in refs[:-1]]
    if len(terms) == 4:
        terms = [terms[0] + terms[2], terms[1] + terms[3]]
    refs[-1][...] = terms[0] + terms[1]


def add(terms):
    return call(add_kernel, f32(*terms[0].shape), [VMEM] * len(terms), VMEM, limit=4, name="add")(*terms)


def merge_kernel(docs, width, *refs):
    refs[-1][...] = merge(docs, width, [ref[...] for ref in refs[:-1]])


def merged(docs, width, states):
    kernel = functools.partial(merge_kernel, docs, width)
    return call(kernel, f32(*states[0].shape), [VMEM] * len(states), VMEM, limit=4, name="merge")(*states)


def target_kernel(docs, positive, *refs):
    pieces, out = refs[:4], refs[4]
    dp, _ = here()
    total = jnp.zeros(out.shape, jnp.float32)
    for k, piece in enumerate(pieces):
        shape = (out.shape[0], piece.shape[0])
        doc = lax.broadcasted_iota(jnp.int32, shape, 0)
        wanted = jnp.zeros(shape, jnp.int32)
        for d in range(2 * docs):
            wanted = jnp.where(doc == d, positive[(d // docs * 4 + (dp & 3)) * docs + d % docs], wanted)
        hit = (row_ids(k, shape, 1) == wanted).astype(jnp.float32).astype(jnp.bfloat16)
        total = total + jnp.dot(hit, piece[...], preferred_element_type=jnp.float32)
    out[...] = total


def turn_kernel(mixed, out):
    width = out.shape[0]
    rows = 128
    lax.fori_loop(0, width // rows, lambda index, _: turn_rows(index * rows, rows, mixed, out), None)


def turn_rows(low, rows, mixed, out):
    width = out.shape[0]
    place = low + lax.broadcasted_iota(jnp.int32, (rows, 1), 0)
    dp, ctx = here()
    each = width // 128
    core = (ctx & 1) ^ (place // (64 * each))
    first, second = place // (16 * each) % 4, place // (4 * each) % 4
    y = ((dp & 3) + jnp.where(core == 0, first, second)) & 3
    x = ((ctx >> 2) + jnp.where(core == 0, second, first)) & 3
    z = ((ctx & 2) + (dp >> 2) + place // each % 4) & 3
    block = ((z & 1) * 4 + y) * 16 + x * 4 + (z >> 1) * 2 + core
    chosen = block * each + place % each == lax.broadcasted_iota(jnp.int32, (rows, width), 1)
    chosen = jnp.where(chosen, 1.0, 0.0).astype(jnp.bfloat16)
    here_rows = pl.ds(pl.multiple_of(low, rows), rows)
    out[here_rows, :] = jnp.dot(chosen, mixed[...], preferred_element_type=jnp.float32).astype(jnp.bfloat16)


def norm_kernel(s0, s1, s2, s3, emb_out, rinv_out, target_out):
    docs = s0.shape[0] // 3
    dp, _ = here()
    own, other = s0[0:docs] + s2[0:docs], s1[0:docs] + s3[0:docs]
    second = dp >= 4
    pooled = jnp.concatenate([jnp.where(second, other, own), jnp.where(second, own, other)], axis=0)
    rinv = lax.rsqrt(jnp.sum(pooled * pooled, axis=1, keepdims=True) + 1e-06)
    emb_out[...] = pooled * rinv
    rinv_out[...] = jnp.broadcast_to(rinv, rinv_out.shape)
    target_out[...] = (s0[docs:] + s2[docs:]) + (s1[docs:] + s3[docs:])


def as_row(column):
    size = column.shape[0]
    same = lax.broadcasted_iota(jnp.int32, (size, size), 0) == lax.broadcasted_iota(jnp.int32, (size, size), 1)
    return jnp.sum(jnp.where(same, column, 0.0), axis=0, keepdims=True)


def score_kernel(docs, positive, e0, e1, e2, e3, t0, t1, t2, t3, everyone, state, expos):
    all_docs, width = everyone.shape
    dp, _ = here()
    y = dp & 3
    group = e0.shape[0]
    for k, piece in enumerate((e0, e1, e2, e3)):
        everyone[pl.ds(pl.multiple_of(((y + k) & 3) * group, group), group), :] = piece[...]
    tables = (t0, t1, t2, t3)
    rows = t0.shape[0]
    emb = thirds(everyone[...])
    scores = [folded(lax.dot_general(emb, t[...], NT, preferred_element_type=jnp.float32)) / TAU for t in tables]
    tops = [jnp.max(s, axis=1, keepdims=True) for s in scores]
    top = jnp.maximum(jnp.maximum(tops[0], tops[2]), jnp.maximum(tops[1], tops[3]))
    row = lax.broadcasted_iota(jnp.int32, (all_docs, rows), 0)
    wanted = jnp.zeros((all_docs, rows), jnp.int32)
    for doc in range(all_docs):
        z, rest = divmod(doc, all_docs // 2)
        wanted = jnp.where(row == rest // docs * group + z * docs + rest % docs, positive[doc], wanted)
    totals, found = [], jnp.zeros((all_docs, 1), jnp.float32)
    for k, s in enumerate(scores):
        expo = jnp.exp(s - top)
        expos[:, k * rows : (k + 1) * rows] = expo
        totals.append(jnp.sum(expo, axis=1, keepdims=True))
        hit = row_ids(k, (all_docs, rows), 1) == wanted
        found = found + jnp.sum(jnp.where(hit, s, 0.0), axis=1, keepdims=True)
    total = (totals[0] + totals[2]) + (totals[1] + totals[3])
    mine = thirds(expos[pl.ds(pl.multiple_of(y * group, group), group), :])
    mix = jnp.zeros((group, width), jnp.float32)
    for k, t in enumerate(tables):
        mix = mix + folded(jnp.dot(mine[:, k * rows : (k + 1) * rows], t[...], preferred_element_type=jnp.float32))
    column = lax.broadcasted_iota(jnp.int32, (group, all_docs), 1)
    own = column == lax.broadcasted_iota(jnp.int32, (group, all_docs), 0) + y * group
    total_row, top_row, found_row = as_row(total), as_row(top), as_row(found)
    state[...] = jnp.zeros_like(state)
    state[0:group, 0:width] = mix
    for place, values in ((width, total_row), (width + 128, top_row)):
        value = jnp.sum(jnp.where(own, values, 0.0), axis=1, keepdims=True)
        state[0:group, place : place + 128] = jnp.broadcast_to(value, (group, 128))
    for index, values in enumerate((total_row, top_row, found_row)):
        state[group + index : group + index + 1, 0:all_docs] = values


def merge(docs, width, states):
    row = lax.broadcasted_iota(jnp.int32, states[0].shape, 0)
    column = lax.broadcasted_iota(jnp.int32, states[0].shape, 1)
    place = width + 128
    by_row = [s[:, place : place + 1] for s in states]
    by_lane = [s[docs + 1 : docs + 2, :] for s in states]
    top_row = functools.reduce(jnp.maximum, by_row)
    top_lane = functools.reduce(jnp.maximum, by_lane)
    terms = [
        s * jnp.exp(jnp.where(row == docs, b - top_lane, a - top_row)) for s, a, b in zip(states, by_row, by_lane)
    ]
    if len(terms) == 4:
        terms = [terms[0] + terms[2], terms[1] + terms[3]]
    joined = jnp.where((row < docs) & (column >= place), top_row, terms[0] + terms[1])
    return jnp.where(row == docs + 1, top_lane, joined)


def batch_kernel(emb, everyone, product_out, stats):
    everything = everyone[...]
    all_docs = everything.shape[0]
    own = lax.dot_general(emb[...], everything, NT, precision=HIGHEST, preferred_element_type=jnp.float32) / TAU
    product = lax.dot_general(everything, everything, NT, precision=HIGHEST, preferred_element_type=jnp.float32) / TAU
    wide = (all_docs, all_docs)
    same = lax.broadcasted_iota(jnp.int32, wide, 0) == lax.broadcasted_iota(jnp.int32, wide, 1)
    product = jnp.where(same, -1e30, product)
    top = jnp.max(product, axis=0, keepdims=True)
    total = jnp.sum(jnp.exp(product - top), axis=0, keepdims=True)
    product_out[...] = own
    stats[...] = jnp.concatenate([top, total] * 4, axis=0)


def grad_kernel(
    lengths, s0, s1, s2, s3, emb, rinv, everyone, target, product, stats, gain, normed, rstd, turned,
    send_out, d_summed, loss_out,
):
    docs, tb, width = normed.shape
    all_docs, group = everyone.shape[0], emb.shape[0]
    dp, _ = here()
    mine = lambda a: jnp.where(dp >= 4, a[docs:group], a[0:docs])
    own, others = mine(emb), everyone[...]
    now = merge(group, width, [s[...] for s in (s0, s1, s2, s3)])
    total, top, found = (now[group + k : group + k + 1, 0:all_docs] for k in range(3))
    batch_top, batch_total = stats[0:1], stats[1:2]
    peak = jnp.maximum(top, batch_top)
    lse_row = peak + jnp.log(total * jnp.exp(top - peak) + batch_total * jnp.exp(batch_top - peak))
    loss_out[...] = jnp.broadcast_to(jnp.sum(lse_row - found, axis=1, keepdims=True) / all_docs, loss_out.shape)
    column = lax.broadcasted_iota(jnp.int32, (docs, all_docs), 1)
    first = (dp & 3) * group + (dp >> 2) * docs
    same = column == lax.broadcasted_iota(jnp.int32, (docs, all_docs), 0) + first
    lse = jnp.sum(jnp.where(same, lse_row, 0.0), axis=1, keepdims=True)
    scores = mine(product)
    g_batch = jnp.where(same, 0.0, jnp.exp(scores - lse) + jnp.exp(scores - lse_row)) / all_docs
    shares = mine(now)
    mix = shares[:, 0:width] * jnp.exp(shares[:, width + 128 : width + 129] - lse)
    from_batch = jnp.dot(g_batch, others, precision=HIGHEST, preferred_element_type=jnp.float32)
    d_emb = ((mix - mine(target)) / all_docs + from_batch) / TAU
    d_pooled = (d_emb - own * jnp.sum(own * d_emb, axis=1, keepdims=True)) * mine(rinv)[:, 0:1]
    for doc in range(docs):
        dy = d_pooled[doc : doc + 1] / lengths[doc].astype(jnp.float32) * gain[...].reshape(1, width)
        level = dy - jnp.mean(dy, axis=1, keepdims=True)
        unit = normed[doc].astype(jnp.float32)
        along = jnp.mean(unit * dy, axis=1, keepdims=True)
        keep = lax.axis_index("ctx") * tb + lax.broadcasted_iota(jnp.int32, (tb, 1), 0) < lengths[doc]
        scale = jnp.where(keep, rstd[doc, :, 0:1], 0.0)
        d_summed[doc * tb : (doc + 1) * tb, :] = (scale * (level - unit * along)).astype(jnp.bfloat16)
    product_rows(turned, width // 2, d_summed, send_out)


def product_rows(turned, low, d_summed, out):
    rows = 128

    def some(index, _):
        source = pl.ds(pl.multiple_of(low + index * rows, rows), rows)
        here_rows = pl.ds(pl.multiple_of(index * rows, rows), rows)
        out[here_rows, :] = jnp.dot(turned[source, :], d_summed[...], preferred_element_type=jnp.float32)

    lax.fori_loop(0, out.shape[0] // rows, some, None)


def keep_kernel(turned, d_summed, out):
    product_rows(turned, 0, d_summed, out)


def sum_kernel(count, *refs):
    terms, outs = refs[:count], refs[count:]
    total = terms[0][...].astype(jnp.float32)
    for term in terms[1:]:
        total = total + term[...].astype(jnp.float32)
    rows = outs[0].shape[0]
    for index, out in enumerate(outs):
        out[...] = total[index * rows : (index + 1) * rows].astype(out.dtype)


def sum_and_split(terms, kind):
    rows, width = terms[0].shape
    piece = (rows // 4, width)
    shapes = (f32(*piece),) + (jax.ShapeDtypeStruct(piece, kind),) * 3
    return call(
        functools.partial(sum_kernel, len(terms)), shapes, [VMEM] * len(terms), (VMEM,) * 4, limit=8, name="sum_split"
    )(*terms)


def shards(tokens, w_qkv, w_out, ln_gain, cache, positive, lengths):
    docs, tb, width = tokens.shape
    n_ctx, n_dp = lax.axis_size("ctx"), lax.axis_size("dp")
    all_docs = n_dp * docs
    ring = [(i, (i + 2 * (i % 2) - 1) % n_ctx) for i in range(n_ctx)]
    fetch = lambda part: lax.ppermute(part, "ctx", ring)
    early = fetch(tokens[0:2])
    near = swap(tokens, "ctx", 1)
    tables = around(cache, from_y)
    qk, v_turned, w_v_turned, third, fourth = prepare(in_hbm(tokens), in_hbm(w_qkv))
    target = call(
        functools.partial(target_kernel, docs), f32(2 * docs, width), [SMEM] + [VMEM] * 4, VMEM, name="target"
    )(positive, *tables)
    early, third = lax.optimization_barrier((early, third))
    third = fetch(third)
    early, target = lax.optimization_barrier((early, target))
    gain = ln_gain
    fixed = (lengths, tokens, near), (qk, v_turned, w_qkv, w_v_turned, w_out, gain)
    *done, pool = attend(0, None, *fixed[0], early, *fixed[1])
    pool, fourth = lax.optimization_barrier((pool, fourth))
    fourth = fetch(fourth)
    done = attend(2, [*done, pool], *fixed[0], third, *fixed[1])
    done = attend(3, done, *fixed[0], fourth, *fixed[1])
    hidden, mixed, normed, rstd, pool = done

    turned = call(
        turn_kernel,
        bf16(width, docs * tb),
        [VMEM],
        VMEM,
        flops=2 * docs * tb * width * width,
        moved=4 * 2**20,
        name="turn",
    )(mixed)

    group = 2 * docs
    sums = call(stack_kernel, f32(docs + group, width), [VMEM, VMEM], VMEM, limit=4, name="stack")(
        pool, target
    )
    sums = add([sums, swap(sums, "ctx", 1)])
    sums = add(around(sums, from_x))
    emb, rinv, target = call(
        norm_kernel,
        (f32(group, width), f32(group, 128), f32(group, width)),
        [VMEM] * 4,
        (VMEM,) * 3,
        limit=4,
        name="norm",
    )(*around(sums, from_z))
    embs = around(emb, from_y)
    everyone, state = call(
        functools.partial(score_kernel, docs),
        (f32(all_docs, width), f32(2 * group, width + 256)),
        [SMEM] + [VMEM] * 8,
        (VMEM, VMEM),
        moved=2 * 2**20,
        scratch_shapes=[pltpu.VMEM((all_docs, n_dp * cache.shape[0]), jnp.float32)],
        name="score",
    )(positive, *embs, *tables)
    product, stats = call(
        batch_kernel,
        (f32(group, all_docs), f32(8, all_docs)),
        [VMEM, VMEM],
        (VMEM, VMEM),
        limit=4,
        name="batch",
    )(emb, everyone)
    state = merged(group, width, [state, swap(state, "ctx", 1)])
    state = merged(group, width, around(state, from_x))
    half = width // 2
    send, d_summed, loss = call(
        grad_kernel,
        (f32(half, width), bf16(docs * tb, width), f32(8, 128)),
        [SMEM] + [VMEM] * 14,
        (VMEM,) * 3,
        flops=docs * tb * width * width,
        moved=8 * 2**20,
        name="grad",
    )(
        lengths, *around(state, from_z), emb, rinv, everyone, target, product, stats, gain, normed, rstd, turned,
    )
    keep = call(
        keep_kernel,
        f32(half, width),
        [VMEM, VMEM],
        VMEM,
        flops=docs * tb * width * width,
        moved=2**20,
        name="keep",
    )(turned, d_summed)
    keep, *sends = sum_and_split([keep, swap(send, "ctx", 1)], jnp.bfloat16)
    got = [from_plane(piece, -(k + 1), False) for k, piece in enumerate(sends)]
    keep, *sends = sum_and_split([keep] + got, jnp.float32)
    got = [from_plane(piece, -(k + 1), True) for k, piece in enumerate(sends)]
    keep, *sends = sum_and_split([keep] + got, jnp.float32)
    got = [from_z(piece, -(k + 1)) for k, piece in enumerate(sends)]
    return (hidden, loss[0, 0], add([keep] + got))


def solution(mesh):
    placed = (P("dp", "ctx", None), P(), P(), P(), P(("dp", "ctx"), None), P(), P("dp"))
    return jax.shard_map(
        shards,
        mesh=mesh,
        in_specs=placed,
        out_specs=(P("dp", "ctx", None), P(), P(("dp", "ctx"), None)),
        check_vma=False,
    )
```

profile of v0, /device:TPU:0, one launch (start us, length us, event | category | flops | bytes accessed | tf_op | source)
XLA Modules:
  0.0 135.0 jit_solution(10799470895345311320)
XLA Ops:
  0.7 1.2 slice.6
  2.0 6.3 %collective-permute-start.1 = (bf16[2,256,768]{2,1,0:T(8,128)(2,1)S(1)}, bf16[2,256,768]{2,1,0:T(8,128)(2,1)S(1)}, u32[]{:S(2)}, u32[]{:S(2)}) collective-permute-start(bf16[2,256,768]{2,1,0:T(8,128)(2,1)S(1)} %slice.6), channel_id=1, source_target_pairs={{0,15},{1,2},{2,1},{3,4},{4,3},{5,6},{6,5},{7,8},{8,7},{9,10},{10,... | collective-permute-start | bytes 2359304 | tf_op jit(solution)/shard_map/ppermute | solution.py:499
  8.3 1.6 %collective-permute-start.4 = (bf16[128,768]{1,0:T(8,128)(2,1)S(1)}, bf16[128,768]{1,0:T(8,128)(2,1)S(1)}, u32[]{:S(2)}, u32[]{:S(2)}) collective-permute-start(bf16[128,768]{1,0:T(8,128)(2,1)S(1)} %copy-done.3), channel_id=1, source_target_pairs={{48,0},{0,16},{16,32},{32,48},{112,64},{64,80},{80,96},{96,112},{4... | collective-permute-start | bytes 589832 | tf_op jit(solution)/shard_map/ppermute | solution.py:33
  9.9 2.9 %collective-permute-start.3 = (bf16[128,768]{1,0:T(8,128)(2,1)S(1)}, bf16[128,768]{1,0:T(8,128)(2,1)S(1)}, u32[]{:S(2)}, u32[]{:S(2)}) collective-permute-start(bf16[128,768]{1,0:T(8,128)(2,1)S(1)} %copy-done.3), channel_id=1, source_target_pairs={{32,0},{48,16},{0,32},{16,48},{96,64},{112,80},{64,96},{80,112},{3... | collective-permute-start | bytes 589832 | tf_op jit(solution)/shard_map/ppermute | solution.py:33
  12.8 1.3 collective-permute-start.2
  14.1 7.2 %prepare.1 = (bf16[4,256,1536]{2,1,0:T(8,128)(2,1)S(1)}, bf16[768,1024]{1,0:T(8,128)(2,1)S(1)}, bf16[768,768]{1,0:T(8,128)(2,1)S(1)}, bf16[1,256,768]{2,1,0:T(8,128)(2,1)S(1)}, bf16[1,256,768]{2,1,0:T(8,128)(2,1)S(1)}) custom-call(bf16[4,256,768]{2,1,0:T(8,128)(2,1)} %refs_1_.5, bf16[768,2304]{1,0:T(8,128)(2,1)} %refs_6_.5), custom_call_target="tpu_custom_call" | custom-call | flops 3623878656 | bytes 11534336 | tf_op jit(solution)/shard_map/prepare/pallas_call | solution.py:241
  22.1 1.3 collective-permute-start.6
  23.5 12.6 %attend.3 = (bf16[4,256,768]{2,1,0:T(8,128)(2,1)}, bf16[768,1024]{1,0:T(8,128)(2,1)S(1)}, bf16[4,256,768]{2,1,0:T(8,128)(2,1)S(1)}, f32[4,256,128]{2,1,0:T(8,128)S(1)}, f32[4,1,768]{2,1,0:T(1,128)S(1)}) custom-call(s32[4]{0:T(128)S(1)} %copy-done.5, bf16[4,256,768]{2,1,0:T(8,128)(2,1)S(1)} %copy-done.1, ...), custom_call_target="tpu_custom_call" | custom-call | flops 3019898880 | bytes 4194304 | tf_op jit(solution)/shard_map/attend/pallas_call | solution.py:202
  36.1 4.5 %collective-permute-start.5 = (bf16[1,256,768]{2,1,0:T(8,128)(2,1)S(1)}, bf16[1,256,768]{2,1,0:T(8,128)(2,1)S(1)}, u32[]{:S(2)}, u32[]{:S(2)}) collective-permute-start(bf16[1,256,768]{2,1,0:T(8,128)(2,1)S(1)} %get-tuple-element.59), channel_id=1, source_target_pairs={{0,15},{1,2},{2,1},{3,4},{4,3},{5,6},{6,5},{7,8},{8,7},{9,10},{10,... | collective-permute-start | bytes 1179656 | tf_op jit(solution)/shard_map/ppermute | solution.py:499
  40.5 6.6 %attend.4 = (bf16[4,256,768]{2,1,0:T(8,128)(2,1)}, bf16[768,1024]{1,0:T(8,128)(2,1)S(1)}, bf16[4,256,768]{2,1,0:T(8,128)(2,1)S(1)}, f32[4,256,128]{2,1,0:T(8,128)S(1)}, f32[4,1,768]{2,1,0:T(1,128)S(1)}) custom-call(s32[4]{0:T(128)S(1)} %copy-done.5, ...), custom_call_target="tpu_custom_call", output_to_operand_aliasing={{0}: (10, {}), {1}: (11, {}), {2}: (12, {}), {3}: (13, {}),... | custom-call | flops 1509949440 | bytes 4194304 | tf_op jit(solution)/shard_map/attend/pallas_call | solution.py:202
  47.1 6.6 %attend.5 = (bf16[4,256,768]{2,1,0:T(8,128)(2,1)}, bf16[768,1024]{1,0:T(8,128)(2,1)S(1)}, bf16[4,256,768]{2,1,0:T(8,128)(2,1)S(1)}, f32[4,256,128]{2,1,0:T(8,128)S(1)}, f32[4,1,768]{2,1,0:T(1,128)S(1)}) custom-call(s32[4]{0:T(128)S(1)} %copy-done.5, ...), custom_call_target="tpu_custom_call", output_to_operand_aliasing={{0}: (10, {}), {1}: (11, {}), {2}: (12, {}), {3}: (13, {}),... | custom-call | flops 1509949440 | bytes 4194304 | tf_op jit(solution)/shard_map/attend/pallas_call | solution.py:202
  53.7 6.2 %collective-permute-start.7 = (f32[12,768]{1,0:T(8,128)S(1)}, f32[12,768]{1,0:T(8,128)S(1)}, u32[]{:S(2)}, u32[]{:S(2)}) collective-permute-start(f32[12,768]{1,0:T(8,128)S(1)} %stack.1.refs_0_), channel_id=1, source_target_pairs={{0,1},{1,0},{2,3},{3,2},{4,5},{5,4},{6,7},{7,6},{8,9},{9,8},{10,11... | collective-permute-start | bytes 110600 | tf_op jit(solution)/shard_map/ppermute | solution.py:24
  60.0 0.9 collective-permute-done.7.refs_1_
  60.8 1.5 %collective-permute-start.10 = (f32[12,768]{1,0:T(8,128)S(1)}, f32[12,768]{1,0:T(8,128)S(1)}, u32[]{:S(2)}, u32[]{:S(2)}) collective-permute-start(f32[12,768]{1,0:T(8,128)S(1)} %add.3.refs_0_), channel_id=1, source_target_pairs={{12,0},{13,1},{14,2},{15,3},{0,4},{1,5},{2,6},{3,7},{4,8},{5,9},{6... | collective-permute-start | bytes 110600 | tf_op jit(solution)/shard_map/ppermute | solution.py:29
  62.3 1.6 %collective-permute-start.9 = (f32[12,768]{1,0:T(8,128)S(1)}, f32[12,768]{1,0:T(8,128)S(1)}, u32[]{:S(2)}, u32[]{:S(2)}) collective-permute-start(f32[12,768]{1,0:T(8,128)S(1)} %add.3.refs_0_), channel_id=1, source_target_pairs={{8,0},{9,1},{10,2},{11,3},{12,4},{13,5},{14,6},{15,7},{0,8},{1,9},... | collective-permute-start | bytes 110600 | tf_op jit(solution)/shard_map/ppermute | solution.py:29
  64.0 2.5 %collective-permute-start.8 = (f32[12,768]{1,0:T(8,128)S(1)}, f32[12,768]{1,0:T(8,128)S(1)}, u32[]{:S(2)}, u32[]{:S(2)}) collective-permute-start(f32[12,768]{1,0:T(8,128)S(1)} %add.3.refs_0_), channel_id=1, source_target_pairs={{4,0},{5,1},{6,2},{7,3},{8,4},{9,5},{10,6},{11,7},{12,8},{13,9},{1... | collective-permute-start | bytes 110600 | tf_op jit(solution)/shard_map/ppermute | solution.py:29
  66.5 1.4 %collective-permute-done.9.refs_2_ = f32[12,768]{1,0:T(8,128)S(1)} collective-permute-done((f32[12,768]{1,0:T(8,128)S(1)}, f32[12,768]{1,0:T(8,128)S(1)}, u32[]{:S(2)}, u32[]{:S(2)}) %collective-permute-start.9) | collective-permute-done | bytes 36896 | tf_op jit(solution)/shard_map/ppermute | solution.py:29
  68.3 1.1 collective-permute-start.13
  69.4 2.5 %collective-permute-start.12 = (f32[12,768]{1,0:T(8,128)S(1)}, f32[12,768]{1,0:T(8,128)S(1)}, u32[]{:S(2)}, u32[]{:S(2)}) collective-permute-start(f32[12,768]{1,0:T(8,128)S(1)} %add.4.s0), channel_id=1, source_target_pairs={{2,0},{3,1},{0,2},{1,3},{6,4},{7,5},{4,6},{5,7},{10,8},{11,9},{8,1... | collective-permute-start | bytes 110600 | tf_op jit(solution)/shard_map/ppermute | solution.py:43
  72.4 1.2 collective-permute-done.13.s3
  73.6 1.3 collective-permute-done.12.s2
  75.0 0.9 collective-permute-done.11.s1
  76.0 1.2 collective-permute-start.16
  77.2 3.5 %collective-permute-start.15 = (f32[8,768]{1,0:T(8,128)S(1)}, f32[8,768]{1,0:T(8,128)S(1)}, u32[]{:S(2)}, u32[]{:S(2)}) collective-permute-start(f32[8,768]{1,0:T(8,128)S(1)} %get-tuple-element.74.e0.emb), channel_id=1, source_target_pairs={{32,0},{48,16},{0,32},{16,48},{96,64},{112,80},{64,96},{80,112},{3... | collective-permute-start | bytes 73736 | tf_op jit(solution)/shard_map/ppermute | solution.py:33
  81.5 1.3 collective-permute-done.15.e2
  82.7 1.8 %collective-permute-done.14.e1 = f32[8,768]{1,0:T(8,128)S(1)} collective-permute-done((f32[8,768]{1,0:T(8,128)S(1)}, f32[8,768]{1,0:T(8,128)S(1)}, u32[]{:S(2)}, u32[]{:S(2)}) %collective-permute-start.14) | collective-permute-done | bytes 24608 | tf_op jit(solution)/shard_map/ppermute | solution.py:33
  84.5 1.3 score.1
  85.9 1.2 collective-permute-done.17.refs_1_
  88.0 3.7 %collective-permute-start.19 = (f32[16,1024]{1,0:T(8,128)S(1)}, f32[16,1024]{1,0:T(8,128)S(1)}, u32[]{:S(2)}, u32[]{:S(2)}) collective-permute-start(f32[16,1024]{1,0:T(8,128)S(1)} %merge.2.refs_0_), channel_id=1, source_target_pairs={{8,0},{9,1},{10,2},{11,3},{12,4},{13,5},{14,6},{15,7},{0,8},{1,9},... | collective-permute-start | bytes 196616 | tf_op jit(solution)/shard_map/ppermute | solution.py:29
  91.8 1.0 collective-permute-done.20.refs_3_
  92.8 2.5 %collective-permute-done.19.refs_2_ = f32[16,1024]{1,0:T(8,128)S(1)} collective-permute-done((f32[16,1024]{1,0:T(8,128)S(1)}, f32[16,1024]{1,0:T(8,128)S(1)}, u32[]{:S(2)}, u32[]{:S(2)}) %collective-permute-start.19) | collective-permute-done | bytes 65568 | tf_op jit(solution)/shard_map/ppermute | solution.py:29
  96.1 1.1 collective-permute-start.23
  97.2 2.7 %collective-permute-start.22 = (f32[16,1024]{1,0:T(8,128)S(1)}, f32[16,1024]{1,0:T(8,128)S(1)}, u32[]{:S(2)}, u32[]{:S(2)}) collective-permute-start(f32[16,1024]{1,0:T(8,128)S(1)} %merge.3.s0), channel_id=1, source_target_pairs={{2,0},{3,1},{0,2},{1,3},{6,4},{7,5},{4,6},{5,7},{10,8},{11,9},{8,1... | collective-permute-start | bytes 196616 | tf_op jit(solution)/shard_map/ppermute | solution.py:43
  100.3 3.6 %turn.1.turned = bf16[768,1024]{1,0:T(8,128)(2,1)S(1)} custom-call(bf16[768,1024]{1,0:T(8,128)(2,1)S(1)} %get-tuple-element.83.mixed), custom_call_target="tpu_custom_call" | custom-call | flops 1207959552 | bytes 4194304 | tf_op jit(solution)/shard_map/turn/pallas_call | solution.py:519
  104.3 2.9 %grad.1 = (f32[384,768]{1,0:T(8,128)S(1)}, bf16[1024,768]{1,0:T(8,128)(2,1)S(1)}, f32[8,128]{1,0:T(8,128)S(1)}) custom-call(s32[4]{0:T(128)S(1)} %copy-done.5, f32[16,1024]{1,0:T(8,128)S(1)} %merge.3.s0, f32[16,1024]{1,0:T(8,128)S(1)} %collective-permute-done.21.s1, f32[16,1024]{1,0:T(8,128)S(1)} %collective-permute-done.22.s2, ...), custom_call_target="tpu_custom_call" | custom-call | flops 603979776 | bytes 8388608 | tf_op jit(solution)/shard_map/grad/pallas_call | solution.py:564
  107.4 1.2 keep.1.refs_0_
  108.5 1.7 %collective-permute-done.24.refs_1_ = f32[384,768]{1,0:T(8,128)S(1)} collective-permute-done((f32[384,768]{1,0:T(8,128)S(1)}, f32[384,768]{1,0:T(8,128)S(1)}, u32[]{:S(2)}, u32[]{:S(2)}) %collective-permute-start.24) | collective-permute-done | bytes 1179680 | tf_op jit(solution)/shard_map/ppermute | solution.py:24
  110.7 3.8 %collective-permute-start.26 = (bf16[96,768]{1,0:T(8,128)(2,1)S(1)}, bf16[96,768]{1,0:T(8,128)(2,1)S(1)}, u32[]{:S(2)}, u32[]{:S(2)}) collective-permute-start(bf16[96,768]{1,0:T(8,128)(2,1)S(1)} %get-tuple-element.89), channel_id=1, source_target_pairs={{32,0},{9,1},{34,2},{11,3},{36,4},{13,5},{38,6},{15,7},{40,8},{1,9... | collective-permute-start | bytes 442376 | tf_op jit(solution)/shard_map/ppermute | solution.py:54
  114.6 2.2 %collective-permute-done.25.refs_1_ = bf16[96,768]{1,0:T(8,128)(2,1)S(1)} collective-permute-done((bf16[96,768]{1,0:T(8,128)(2,1)S(1)}, bf16[96,768]{1,0:T(8,128)(2,1)S(1)}, u32[]{:S(2)}, u32[]{:S(2)}) %collective-permute-start.25) | collective-permute-done | bytes 147488 | tf_op jit(solution)/shard_map/ppermute | solution.py:54
  116.8 2.4 %collective-permute-done.26.refs_2_ = bf16[96,768]{1,0:T(8,128)(2,1)S(1)} collective-permute-done((bf16[96,768]{1,0:T(8,128)(2,1)S(1)}, bf16[96,768]{1,0:T(8,128)(2,1)S(1)}, u32[]{:S(2)}, u32[]{:S(2)}) %collective-permute-start.26) | collective-permute-done | bytes 147488 | tf_op jit(solution)/shard_map/ppermute | solution.py:54
  119.8 3.0 %collective-permute-start.29 = (f32[24,768]{1,0:T(8,128)S(1)}, f32[24,768]{1,0:T(8,128)S(1)}, u32[]{:S(2)}, u32[]{:S(2)}) collective-permute-start(f32[24,768]{1,0:T(8,128)S(1)} %get-tuple-element.93), channel_id=1, source_target_pairs={{8,0},{33,1},{10,2},{35,3},{12,4},{37,5},{14,6},{39,7},{0,8},{41,9... | collective-permute-start | bytes 221192 | tf_op jit(solution)/shard_map/ppermute | solution.py:54
  122.8 1.2 collective-permute-start.30
  123.9 2.2 %collective-permute-done.28.refs_1_ = f32[24,768]{1,0:T(8,128)S(1)} collective-permute-done((f32[24,768]{1,0:T(8,128)S(1)}, f32[24,768]{1,0:T(8,128)S(1)}, u32[]{:S(2)}, u32[]{:S(2)}) %collective-permute-start.28) | collective-permute-done | bytes 73760 | tf_op jit(solution)/shard_map/ppermute | solution.py:54
  126.1 1.0 collective-permute-done.30.refs_3_
  127.1 1.6 %collective-permute-start.31 = (f32[6,768]{1,0:T(8,128)S(1)}, f32[6,768]{1,0:T(8,128)S(1)}, u32[]{:S(2)}, u32[]{:S(2)}) collective-permute-start(f32[6,768]{1,0:T(8,128)S(1)} %get-tuple-element.96), channel_id=1, source_target_pairs={{66,0},{67,1},{64,2},{65,3},{70,4},{71,5},{68,6},{69,7},{74,8},{75... | collective-permute-start | bytes 55304 | tf_op jit(solution)/shard_map/ppermute | solution.py:43
  128.8 1.8 %collective-permute-start.32 = (f32[6,768]{1,0:T(8,128)S(1)}, f32[6,768]{1,0:T(8,128)S(1)}, u32[]{:S(2)}, u32[]{:S(2)}) collective-permute-start(f32[6,768]{1,0:T(8,128)S(1)} %get-tuple-element.97), channel_id=1, source_target_pairs={{2,0},{3,1},{0,2},{1,3},{6,4},{7,5},{4,6},{5,7},{10,8},{11,9},{8,1... | collective-permute-start | bytes 55304 | tf_op jit(solution)/shard_map/ppermute | solution.py:43
  130.6 1.3 collective-permute-start.33
  132.4 1.7 %collective-permute-done.32.refs_2_ = f32[6,768]{1,0:T(8,128)S(1)} collective-permute-done((f32[6,768]{1,0:T(8,128)S(1)}, f32[6,768]{1,0:T(8,128)S(1)}, u32[]{:S(2)}, u32[]{:S(2)}) %collective-permute-start.32) | collective-permute-done | bytes 18464 | tf_op jit(solution)/shard_map/ppermute | solution.py:43
  (56 shorter events, 8.0 us)
Async XLA Ops:
  0.6 7.7 %copy-start.3 = (bf16[128,768]{1,0:T(8,128)(2,1)S(1)}, bf16[128,768]{1,0:T(8,128)(2,1)}, u32[]{:S(2)}) copy-start(bf16[128,768]{1,0:T(8,128)(2,1)} %t0.1) | copy-start | bytes 589828
  0.6 22.8 %collective-permute-start = (bf16[4,256,768]{2,1,0:T(8,128)(2,1)}, bf16[4,256,768]{2,1,0:T(8,128)(2,1)S(1)}, u32[]{:S(2)}, u32[]{:S(2)}) collective-permute-start(bf16[4,256,768]{2,1,0:T(8,128)(2,1)} %refs_1_.5), channel_id=1, source_target_pairs={{0,1},{1,0},{2,3},{3,2},{4,5},{5,4},{6,7},{7,6},{8,9},{9,8},{10,11... | collective-permute-start | bytes 4718600 | tf_op jit(solution)/shard_map/ppermute | solution.py:24
  1.9 19.5 %copy-start.6 = (s32[32]{0:T(128)S(1)}, s32[32]{0:T(128)}, u32[]{:S(2)}) copy-start(s32[32]{0:T(128)} %positive.3) | copy-start | bytes 388
  1.9 21.5 %copy-start.4 = (f32[768]{0:T(1024)S(1)}, f32[768]{0:T(1024)}, u32[]{:S(2)}) copy-start(f32[768]{0:T(1024)} %gain.1) | copy-start | bytes 9220
  1.9 21.5 %copy-start.5 = (s32[4]{0:T(128)S(1)}, s32[4]{0:T(128)}, u32[]{:S(2)}) copy-start(s32[4]{0:T(128)} %lengths.1) | copy-start | bytes 52
  2.0 20.2 %collective-permute-start.1 = (bf16[2,256,768]{2,1,0:T(8,128)(2,1)S(1)}, bf16[2,256,768]{2,1,0:T(8,128)(2,1)S(1)}, u32[]{:S(2)}, u32[]{:S(2)}) collective-permute-start(bf16[2,256,768]{2,1,0:T(8,128)(2,1)S(1)} %slice.6), channel_id=1, source_target_pairs={{0,15},{1,2},{2,1},{3,4},{4,3},{5,6},{6,5},{7,8},{8,7},{9,10},{10,... | collective-permute-start | bytes 2359304 | tf_op jit(solution)/shard_map/ppermute | solution.py:499
  8.3 13.1 %collective-permute-start.4 = (bf16[128,768]{1,0:T(8,128)(2,1)S(1)}, bf16[128,768]{1,0:T(8,128)(2,1)S(1)}, u32[]{:S(2)}, u32[]{:S(2)}) collective-permute-start(bf16[128,768]{1,0:T(8,128)(2,1)S(1)} %copy-done.3), channel_id=1, source_target_pairs={{48,0},{0,16},{16,32},{32,48},{112,64},{64,80},{80,96},{96,112},{4... | collective-permute-start | bytes 589832 | tf_op jit(solution)/shard_map/ppermute | solution.py:33
  9.9 11.5 %collective-permute-start.3 = (bf16[128,768]{1,0:T(8,128)(2,1)S(1)}, bf16[128,768]{1,0:T(8,128)(2,1)S(1)}, u32[]{:S(2)}, u32[]{:S(2)}) collective-permute-start(bf16[128,768]{1,0:T(8,128)(2,1)S(1)} %copy-done.3), channel_id=1, source_target_pairs={{32,0},{48,16},{0,32},{16,48},{96,64},{112,80},{64,96},{80,112},{3... | collective-permute-start | bytes 589832 | tf_op jit(solution)/shard_map/ppermute | solution.py:33
  12.8 8.6 %collective-permute-start.2 = (bf16[128,768]{1,0:T(8,128)(2,1)S(1)}, bf16[128,768]{1,0:T(8,128)(2,1)S(1)}, u32[]{:S(2)}, u32[]{:S(2)}) collective-permute-start(bf16[128,768]{1,0:T(8,128)(2,1)S(1)} %copy-done.3), channel_id=1, source_target_pairs={{16,0},{32,16},{48,32},{0,48},{80,64},{96,80},{112,96},{64,112},{1... | collective-permute-start | bytes 589832 | tf_op jit(solution)/shard_map/ppermute | solution.py:33
  14.1 9.3 %copy-start = (bf16[768,2304]{1,0:T(8,128)(2,1)S(1)}, bf16[768,2304]{1,0:T(8,128)(2,1)}, u32[]{:S(2)}) copy-start(bf16[768,2304]{1,0:T(8,128)(2,1)} %refs_6_.5) | copy-start | bytes 10616836
  14.1 9.3 %copy-start.1 = (bf16[4,256,768]{2,1,0:T(8,128)(2,1)S(1)}, bf16[4,256,768]{2,1,0:T(8,128)(2,1)}, u32[]{:S(2)}) copy-start(bf16[4,256,768]{2,1,0:T(8,128)(2,1)} %refs_1_.5) | copy-start | bytes 4718596
  14.1 9.3 %copy-start.2 = (bf16[768,768]{1,0:T(8,128)(2,1)S(1)}, bf16[768,768]{1,0:T(8,128)(2,1)}, u32[]{:S(2)}) copy-start(bf16[768,768]{1,0:T(8,128)(2,1)} %refs_8_.5) | copy-start | bytes 3538948
  22.1 18.4 %collective-permute-start.6 = (bf16[1,256,768]{2,1,0:T(8,128)(2,1)S(1)}, bf16[1,256,768]{2,1,0:T(8,128)(2,1)S(1)}, u32[]{:S(2)}, u32[]{:S(2)}) collective-permute-start(bf16[1,256,768]{2,1,0:T(8,128)(2,1)S(1)} %get-tuple-element.60), channel_id=1, source_target_pairs={{0,15},{1,2},{2,1},{3,4},{4,3},{5,6},{6,5},{7,8},{8,7},{9,10},{10,... | collective-permute-start | bytes 1179656 | tf_op jit(solution)/shard_map/ppermute | solution.py:499
  36.1 11.1 %collective-permute-start.5 = (bf16[1,256,768]{2,1,0:T(8,128)(2,1)S(1)}, bf16[1,256,768]{2,1,0:T(8,128)(2,1)S(1)}, u32[]{:S(2)}, u32[]{:S(2)}) collective-permute-start(bf16[1,256,768]{2,1,0:T(8,128)(2,1)S(1)} %get-tuple-element.59), channel_id=1, source_target_pairs={{0,15},{1,2},{2,1},{3,4},{4,3},{5,6},{6,5},{7,8},{8,7},{9,10},{10,... | collective-permute-start | bytes 1179656 | tf_op jit(solution)/shard_map/ppermute | solution.py:499
  53.7 7.1 %collective-permute-start.7 = (f32[12,768]{1,0:T(8,128)S(1)}, f32[12,768]{1,0:T(8,128)S(1)}, u32[]{:S(2)}, u32[]{:S(2)}) collective-permute-start(f32[12,768]{1,0:T(8,128)S(1)} %stack.1.refs_0_), channel_id=1, source_target_pairs={{0,1},{1,0},{2,3},{3,2},{4,5},{5,4},{6,7},{7,6},{8,9},{9,8},{10,11... | collective-permute-start | bytes 110600 | tf_op jit(solution)/shard_map/ppermute | solution.py:24
  60.8 5.7 %collective-permute-start.10 = (f32[12,768]{1,0:T(8,128)S(1)}, f32[12,768]{1,0:T(8,128)S(1)}, u32[]{:S(2)}, u32[]{:S(2)}) collective-permute-start(f32[12,768]{1,0:T(8,128)S(1)} %add.3.refs_0_), channel_id=1, source_target_pairs={{12,0},{13,1},{14,2},{15,3},{0,4},{1,5},{2,6},{3,7},{4,8},{5,9},{6... | collective-permute-start | bytes 110600 | tf_op jit(solution)/shard_map/ppermute | solution.py:29
  62.3 5.6 %collective-permute-start.9 = (f32[12,768]{1,0:T(8,128)S(1)}, f32[12,768]{1,0:T(8,128)S(1)}, u32[]{:S(2)}, u32[]{:S(2)}) collective-permute-start(f32[12,768]{1,0:T(8,128)S(1)} %add.3.refs_0_), channel_id=1, source_target_pairs={{8,0},{9,1},{10,2},{11,3},{12,4},{13,5},{14,6},{15,7},{0,8},{1,9},... | collective-permute-start | bytes 110600 | tf_op jit(solution)/shard_map/ppermute | solution.py:29
  64.0 4.3 %collective-permute-start.8 = (f32[12,768]{1,0:T(8,128)S(1)}, f32[12,768]{1,0:T(8,128)S(1)}, u32[]{:S(2)}, u32[]{:S(2)}) collective-permute-start(f32[12,768]{1,0:T(8,128)S(1)} %add.3.refs_0_), channel_id=1, source_target_pairs={{4,0},{5,1},{6,2},{7,3},{8,4},{9,5},{10,6},{11,7},{12,8},{13,9},{1... | collective-permute-start | bytes 110600 | tf_op jit(solution)/shard_map/ppermute | solution.py:29
  68.3 5.4 %collective-permute-start.13 = (f32[12,768]{1,0:T(8,128)S(1)}, f32[12,768]{1,0:T(8,128)S(1)}, u32[]{:S(2)}, u32[]{:S(2)}) collective-permute-start(f32[12,768]{1,0:T(8,128)S(1)} %add.4.s0), channel_id=1, source_target_pairs={{66,0},{67,1},{64,2},{65,3},{70,4},{71,5},{68,6},{69,7},{74,8},{75... | collective-permute-start | bytes 110600 | tf_op jit(solution)/shard_map/ppermute | solution.py:43
  69.4 5.6 %collective-permute-start.12 = (f32[12,768]{1,0:T(8,128)S(1)}, f32[12,768]{1,0:T(8,128)S(1)}, u32[]{:S(2)}, u32[]{:S(2)}) collective-permute-start(f32[12,768]{1,0:T(8,128)S(1)} %add.4.s0), channel_id=1, source_target_pairs={{2,0},{3,1},{0,2},{1,3},{6,4},{7,5},{4,6},{5,7},{10,8},{11,9},{8,1... | collective-permute-start | bytes 110600 | tf_op jit(solution)/shard_map/ppermute | solution.py:43
  71.8 4.1 %collective-permute-start.11 = (f32[12,768]{1,0:T(8,128)S(1)}, f32[12,768]{1,0:T(8,128)S(1)}, u32[]{:S(2)}, u32[]{:S(2)}) collective-permute-start(f32[12,768]{1,0:T(8,128)S(1)} %add.4.s0), channel_id=1, source_target_pairs={{64,0},{65,1},{66,2},{67,3},{68,4},{69,5},{70,6},{71,7},{72,8},{73... | collective-permute-start | bytes 110600 | tf_op jit(solution)/shard_map/ppermute | solution.py:43
  76.0 5.4 %collective-permute-start.16 = (f32[8,768]{1,0:T(8,128)S(1)}, f32[8,768]{1,0:T(8,128)S(1)}, u32[]{:S(2)}, u32[]{:S(2)}) collective-permute-start(f32[8,768]{1,0:T(8,128)S(1)} %get-tuple-element.74.e0.emb), channel_id=1, source_target_pairs={{48,0},{0,16},{16,32},{32,48},{112,64},{64,80},{80,96},{96,112},{4... | collective-permute-start | bytes 73736 | tf_op jit(solution)/shard_map/ppermute | solution.py:33
  77.2 5.5 %collective-permute-start.15 = (f32[8,768]{1,0:T(8,128)S(1)}, f32[8,768]{1,0:T(8,128)S(1)}, u32[]{:S(2)}, u32[]{:S(2)}) collective-permute-start(f32[8,768]{1,0:T(8,128)S(1)} %get-tuple-element.74.e0.emb), channel_id=1, source_target_pairs={{32,0},{48,16},{0,32},{16,48},{96,64},{112,80},{64,96},{80,112},{3... | collective-permute-start | bytes 73736 | tf_op jit(solution)/shard_map/ppermute | solution.py:33
  80.7 3.8 %collective-permute-start.14 = (f32[8,768]{1,0:T(8,128)S(1)}, f32[8,768]{1,0:T(8,128)S(1)}, u32[]{:S(2)}, u32[]{:S(2)}) collective-permute-start(f32[8,768]{1,0:T(8,128)S(1)} %get-tuple-element.74.e0.emb), channel_id=1, source_target_pairs={{16,0},{32,16},{48,32},{0,48},{80,64},{96,80},{112,96},{64,112},{1... | collective-permute-start | bytes 73736 | tf_op jit(solution)/shard_map/ppermute | solution.py:33
  85.8 1.3 collective-permute-start.17
  87.2 5.5 %collective-permute-start.20 = (f32[16,1024]{1,0:T(8,128)S(1)}, f32[16,1024]{1,0:T(8,128)S(1)}, u32[]{:S(2)}, u32[]{:S(2)}) collective-permute-start(f32[16,1024]{1,0:T(8,128)S(1)} %merge.2.refs_0_), channel_id=1, source_target_pairs={{12,0},{13,1},{14,2},{15,3},{0,4},{1,5},{2,6},{3,7},{4,8},{5,9},{6... | collective-permute-start | bytes 196616 | tf_op jit(solution)/shard_map/ppermute | solution.py:29
  88.0 7.2 %collective-permute-start.19 = (f32[16,1024]{1,0:T(8,128)S(1)}, f32[16,1024]{1,0:T(8,128)S(1)}, u32[]{:S(2)}, u32[]{:S(2)}) collective-permute-start(f32[16,1024]{1,0:T(8,128)S(1)} %merge.2.refs_0_), channel_id=1, source_target_pairs={{8,0},{9,1},{10,2},{11,3},{12,4},{13,5},{14,6},{15,7},{0,8},{1,9},... | collective-permute-start | bytes 196616 | tf_op jit(solution)/shard_map/ppermute | solution.py:29
  91.8 4.3 %collective-permute-start.18 = (f32[16,1024]{1,0:T(8,128)S(1)}, f32[16,1024]{1,0:T(8,128)S(1)}, u32[]{:S(2)}, u32[]{:S(2)}) collective-permute-start(f32[16,1024]{1,0:T(8,128)S(1)} %merge.2.refs_0_), channel_id=1, source_target_pairs={{4,0},{5,1},{6,2},{7,3},{8,4},{9,5},{10,6},{11,7},{12,8},{13,9},{1... | collective-permute-start | bytes 196616 | tf_op jit(solution)/shard_map/ppermute | solution.py:29
  96.1 8.2 %collective-permute-start.23 = (f32[16,1024]{1,0:T(8,128)S(1)}, f32[16,1024]{1,0:T(8,128)S(1)}, u32[]{:S(2)}, u32[]{:S(2)}) collective-permute-start(f32[16,1024]{1,0:T(8,128)S(1)} %merge.3.s0), channel_id=1, source_target_pairs={{66,0},{67,1},{64,2},{65,3},{70,4},{71,5},{68,6},{69,7},{74,8},{75... | collective-permute-start | bytes 196616 | tf_op jit(solution)/shard_map/ppermute | solution.py:43
  97.2 7.1 %collective-permute-start.22 = (f32[16,1024]{1,0:T(8,128)S(1)}, f32[16,1024]{1,0:T(8,128)S(1)}, u32[]{:S(2)}, u32[]{:S(2)}) collective-permute-start(f32[16,1024]{1,0:T(8,128)S(1)} %merge.3.s0), channel_id=1, source_target_pairs={{2,0},{3,1},{0,2},{1,3},{6,4},{7,5},{4,6},{5,7},{10,8},{11,9},{8,1... | collective-permute-start | bytes 196616 | tf_op jit(solution)/shard_map/ppermute | solution.py:43
  99.9 4.4 %collective-permute-start.21 = (f32[16,1024]{1,0:T(8,128)S(1)}, f32[16,1024]{1,0:T(8,128)S(1)}, u32[]{:S(2)}, u32[]{:S(2)}) collective-permute-start(f32[16,1024]{1,0:T(8,128)S(1)} %merge.3.s0), channel_id=1, source_target_pairs={{64,0},{65,1},{66,2},{67,3},{68,4},{69,5},{70,6},{71,7},{72,8},{73... | collective-permute-start | bytes 196616 | tf_op jit(solution)/shard_map/ppermute | solution.py:43
  107.3 2.9 %collective-permute-start.24 = (f32[384,768]{1,0:T(8,128)S(1)}, f32[384,768]{1,0:T(8,128)S(1)}, u32[]{:S(2)}, u32[]{:S(2)}) collective-permute-start(f32[384,768]{1,0:T(8,128)S(1)} %get-tuple-element.86), channel_id=1, source_target_pairs={{0,1},{1,0},{2,3},{3,2},{4,5},{5,4},{6,7},{7,6},{8,9},{9,8},{10,11... | collective-permute-start | bytes 3538952 | tf_op jit(solution)/shard_map/ppermute | solution.py:24
  110.4 6.4 %collective-permute-start.25 = (bf16[96,768]{1,0:T(8,128)(2,1)S(1)}, bf16[96,768]{1,0:T(8,128)(2,1)S(1)}, u32[]{:S(2)}, u32[]{:S(2)}) collective-permute-start(bf16[96,768]{1,0:T(8,128)(2,1)S(1)} %get-tuple-element.88), channel_id=1, source_target_pairs={{48,0},{13,1},{50,2},{15,3},{52,4},{1,5},{54,6},{3,7},{56,8},{5,9}... | collective-permute-start | bytes 442376 | tf_op jit(solution)/shard_map/ppermute | solution.py:54
  110.7 8.5 %collective-permute-start.26 = (bf16[96,768]{1,0:T(8,128)(2,1)S(1)}, bf16[96,768]{1,0:T(8,128)(2,1)S(1)}, u32[]{:S(2)}, u32[]{:S(2)}) collective-permute-start(bf16[96,768]{1,0:T(8,128)(2,1)S(1)} %get-tuple-element.89), channel_id=1, source_target_pairs={{32,0},{9,1},{34,2},{11,3},{36,4},{13,5},{38,6},{15,7},{40,8},{1,9... | collective-permute-start | bytes 442376 | tf_op jit(solution)/shard_map/ppermute | solution.py:54
  114.5 5.1 %collective-permute-start.27 = (bf16[96,768]{1,0:T(8,128)(2,1)S(1)}, bf16[96,768]{1,0:T(8,128)(2,1)S(1)}, u32[]{:S(2)}, u32[]{:S(2)}) collective-permute-start(bf16[96,768]{1,0:T(8,128)(2,1)S(1)} %get-tuple-element.90), channel_id=1, source_target_pairs={{16,0},{5,1},{18,2},{7,3},{20,4},{9,5},{22,6},{11,7},{24,8},{13,9}... | collective-permute-start | bytes 442376 | tf_op jit(solution)/shard_map/ppermute | solution.py:54
  119.7 6.4 %collective-permute-start.28 = (f32[24,768]{1,0:T(8,128)S(1)}, f32[24,768]{1,0:T(8,128)S(1)}, u32[]{:S(2)}, u32[]{:S(2)}) collective-permute-start(f32[24,768]{1,0:T(8,128)S(1)} %get-tuple-element.92), channel_id=1, source_target_pairs={{12,0},{49,1},{14,2},{51,3},{0,4},{53,5},{2,6},{55,7},{4,8},{57,9}... | collective-permute-start | bytes 221192 | tf_op jit(solution)/shard_map/ppermute | solution.py:54
  119.8 6.3 %collective-permute-start.29 = (f32[24,768]{1,0:T(8,128)S(1)}, f32[24,768]{1,0:T(8,128)S(1)}, u32[]{:S(2)}, u32[]{:S(2)}) collective-permute-start(f32[24,768]{1,0:T(8,128)S(1)} %get-tuple-element.93), channel_id=1, source_target_pairs={{8,0},{33,1},{10,2},{35,3},{12,4},{37,5},{14,6},{39,7},{0,8},{41,9... | collective-permute-start | bytes 221192 | tf_op jit(solution)/shard_map/ppermute | solution.py:54
  122.8 4.4 %collective-permute-start.30 = (f32[24,768]{1,0:T(8,128)S(1)}, f32[24,768]{1,0:T(8,128)S(1)}, u32[]{:S(2)}, u32[]{:S(2)}) collective-permute-start(f32[24,768]{1,0:T(8,128)S(1)} %get-tuple-element.94), channel_id=1, source_target_pairs={{4,0},{17,1},{6,2},{19,3},{8,4},{21,5},{10,6},{23,7},{12,8},{25,9}... | collective-permute-start | bytes 221192 | tf_op jit(solution)/shard_map/ppermute | solution.py:54
  127.1 5.2 %collective-permute-start.31 = (f32[6,768]{1,0:T(8,128)S(1)}, f32[6,768]{1,0:T(8,128)S(1)}, u32[]{:S(2)}, u32[]{:S(2)}) collective-permute-start(f32[6,768]{1,0:T(8,128)S(1)} %get-tuple-element.96), channel_id=1, source_target_pairs={{66,0},{67,1},{64,2},{65,3},{70,4},{71,5},{68,6},{69,7},{74,8},{75... | collective-permute-start | bytes 55304 | tf_op jit(solution)/shard_map/ppermute | solution.py:43
  128.8 5.3 %collective-permute-start.32 = (f32[6,768]{1,0:T(8,128)S(1)}, f32[6,768]{1,0:T(8,128)S(1)}, u32[]{:S(2)}, u32[]{:S(2)}) collective-permute-start(f32[6,768]{1,0:T(8,128)S(1)} %get-tuple-element.97), channel_id=1, source_target_pairs={{2,0},{3,1},{0,2},{1,3},{6,4},{7,5},{4,6},{5,7},{10,8},{11,9},{8,1... | collective-permute-start | bytes 55304 | tf_op jit(solution)/shard_map/ppermute | solution.py:43
  130.6 3.8 %collective-permute-start.33 = (f32[6,768]{1,0:T(8,128)S(1)}, f32[6,768]{1,0:T(8,128)S(1)}, u32[]{:S(2)}, u32[]{:S(2)}) collective-permute-start(f32[6,768]{1,0:T(8,128)S(1)} %get-tuple-element.98), channel_id=1, source_target_pairs={{64,0},{65,1},{66,2},{67,3},{68,4},{69,5},{70,6},{71,7},{72,8},{73... | collective-permute-start | bytes 55304 | tf_op jit(solution)/shard_map/ppermute | solution.py:43
where the time goes:
time: 135 us
  starting transfers between devices  61.5 us (46%)
  Pallas kernels  44.3 us (33%)
  waiting for transfers between devices  26.6 us (20%)
  local copies, waits for them, and re-layouts  1.73 us (1%)
    pallas_call x3, Pallas kernels, attend(): call(functools.partial(attend_kernel, first), out_shape, in_specs, out_sp...  25.7 us
    ppermute x9, starting transfers between devices, from_z(): return lax.ppermute(value, ('dp', 'ctx'), pairs)  13.1 us
    ppermute x3, starting transfers between devices, shards(): fetch = lambda part: lax.ppermute(part, 'ctx', ring)  12.1 us
    ppermute x6, starting transfers between devices, from_y(): lax.ppermute(value, 'dp', [(d & 4 | d + k & 3, d) for d in range(lax.axis...  11.3 us
    ppermute x6, starting transfers between devices, from_x(): lax.ppermute(value, 'ctx', [((c + 4 * k) % size, c) for c in range(size)])  10.2 us
    ppermute x6, starting transfers between devices, from_plane(): return lax.ppermute(value, ('dp', 'ctx'), pairs)  8.4 us
    ppermute x6, waiting for transfers between devices, from_plane(): return lax.ppermute(value, ('dp', 'ctx'), pairs)  8.22 us
    pallas_call x1, Pallas kernels, prepare(): call(prepare_kernel, (bf16(docs, tb, 2 * width), bf16(width, docs * tb),...  7.25 us
  transfers between devices with their start and end apart: 34, of which 20 were waited for; matrix products, arithmetic and copies ran while one was open for 1% of the time, Pallas kernels for 24%

commit v1 on v0

--- a/solution.py
+++ b/solution.py
@@ -112,7 +112,7 @@
 
 
 def attend_doc(
-    doc, index, lengths, tok, near, far, qk, v_turned, w, w_v_turned, w_out, gain, *refs
+    doc, index, lengths, tok, near_k, far, near_v, qk, v_turned, w, w_v_turned, w_out, gain, *refs
 ):
     hidden, mixed_all, normed, rstd_out, pool, keys, values, dist, hidden_here, sem = refs[-10:]
     docs, tb, width = tok.shape
@@ -121,17 +121,20 @@
     mixed = mixed_all.at[:, own]
     ctx = lax.axis_index("ctx")
     start, length = ctx * tb, lengths[doc]
-    right = lax.rem(ctx, 2) == 0
-    ends = far[index], near[doc]
-    rows = jnp.concatenate([jnp.where(right, *ends), jnp.where(right, *ends[::-1])], axis=0)
-    new = jnp.dot(rows, w[:, width : 2 * width], preferred_element_type=jnp.float32).astype(jnp.bfloat16)
-    keys[0:WIN] = new[0:WIN]
+    odd = lax.rem(ctx, 2)
+    near_at = pl.ds(pl.multiple_of((1 - odd) * (WIN + tb), 128), WIN)
+    far_at = pl.ds(pl.multiple_of(odd * (WIN + tb), 128), WIN)
+    rows = far[index]
+    keys[far_at, :] = jnp.dot(
+        rows, w[:, width : 2 * width], preferred_element_type=jnp.float32
+    ).astype(jnp.bfloat16)
+    keys[near_at, :] = near_k[doc]
     keys[WIN : WIN + tb] = qk[doc, :, width:]
-    keys[WIN + tb :] = new[WIN:]
-    new = lax.dot_general(w_v_turned[...], rows, NT, preferred_element_type=jnp.float32).astype(jnp.bfloat16)
-    values[:, 0:WIN] = new[:, 0:WIN]
+    values[:, far_at] = lax.dot_general(
+        w_v_turned[...], rows, NT, preferred_element_type=jnp.float32
+    ).astype(jnp.bfloat16)
+    values[:, near_at] = near_v[:, own]
     values[:, WIN : WIN + tb] = v_turned[:, own]
-    values[:, WIN + tb :] = new[:, WIN:]
     j = lax.broadcasted_iota(jnp.int32, (ext, tb), 0) - WIN
     away = jnp.abs(lax.broadcasted_iota(jnp.int32, (ext, tb), 1) - j)
     kpos = start + j
@@ -187,13 +190,13 @@
     leaving.wait()
 
 
-def attend(first, before, lengths, tokens, near, far, qk, v_turned, w_qkv, w_v_turned, w_out, gain):
+def attend(first, before, lengths, tokens, near_k, far, near_v, qk, v_turned, w_qkv, w_v_turned, w_out, gain):
     docs, tb, width = tokens.shape
     ext = tb + 2 * WIN
     out_shape = (bf16(docs, tb, width), bf16(width, docs * tb), bf16(docs, tb, width), f32(docs, tb, 128), f32(docs, 1, width))
     out_specs = (ANY,) + (VMEM,) * 4
-    operands = [lengths, tokens, near, far, qk, v_turned, w_qkv, w_v_turned, w_out, gain]
-    in_specs = [SMEM] + [VMEM] * 9
+    operands = [lengths, tokens, near_k, far, near_v, qk, v_turned, w_qkv, w_v_turned, w_out, gain]
+    in_specs = [SMEM] + [VMEM] * 10
     aliases = {}
     if before is not None:
         aliases = {len(operands) + k: k for k in range(len(out_shape))}
@@ -219,13 +222,22 @@
     )(*operands)
 
 
-def prepare_kernel(tok, w, qk, v_turned, w_v_turned, *later):
+def near_kernel(near, w, w_v_turned, near_k, near_v):
+    docs, tb, width = near.shape
+
+    def some(doc, _):
+        rows = near[doc]
+        own = pl.ds(pl.multiple_of(doc * tb, tb), tb)
+        near_k[doc] = jnp.dot(rows, w[:, width : 2 * width], preferred_element_type=jnp.float32).astype(jnp.bfloat16)
+        near_v[:, own] = lax.dot_general(
+            w_v_turned[...], rows, NT, preferred_element_type=jnp.float32
+        ).astype(jnp.bfloat16)
+
+    lax.fori_loop(0, docs, some, None)
+
+
+def prepare_kernel(tok, w, qk, v_turned, w_v_turned):
     width = tok.shape[2]
-    for index, late in enumerate(later):
-
-        @pl.when(pl.program_id(0) == index + 2)
-        def _():
-            late[...] = tok[...]
 
     @pl.when(pl.program_id(0) == 0)
     def _():
@@ -240,7 +252,7 @@
     docs, tb, width = tokens.shape
     return call(
         prepare_kernel,
-        (bf16(docs, tb, 2 * width), bf16(width, docs * tb), bf16(width, width)) + (bf16(1, tb, width),) * (docs - 2),
+        (bf16(docs, tb, 2 * width), bf16(width, docs * tb), bf16(width, width)),
         [
             pl.BlockSpec((1, tb, width), lambda i: (i, 0, 0)),
             pl.BlockSpec(w_qkv.shape, lambda i: (0, 0), pipeline_mode=pl.Buffered(1)),
@@ -249,8 +261,7 @@
             pl.BlockSpec((1, tb, 2 * width), lambda i: (i, 0, 0)),
             pl.BlockSpec((width, tb), lambda i: (0, i)),
             pl.BlockSpec((width, width), lambda i: (0, 0)),
-        )
-        + (pl.BlockSpec((1, tb, width), lambda i: (0, 0, 0)),) * (docs - 2),
+        ),
         flops=2 * docs * tb * width * 3 * width,
         moved=11 * 2**20,
         grid=(docs,),
@@ -261,7 +272,7 @@
 def row_ids(k, shape, dim):
     dp, ctx = here()
     place = lax.broadcasted_iota(jnp.int32, shape, dim)
-    return (((dp & 4) | ((dp + k) & 3)) * 16 + ctx) * shape[dim] + place
+    return (((dp & 4) | ((dp + k) & 3)) * 16 + (ctx ^ (k // 4))) * shape[dim] + place
 
 
 def stack_kernel(pool, target, out):
@@ -347,19 +358,18 @@
     return jnp.sum(jnp.where(same, column, 0.0), axis=0, keepdims=True)
 
 
-def score_kernel(docs, positive, e0, e1, e2, e3, t0, t1, t2, t3, everyone, state, expos):
+def score_kernel(docs, positive, e0, e1, e2, e3, *refs):
+    tables, (everyone, state, expos) = refs[:8], refs[8:]
     all_docs, width = everyone.shape
     dp, _ = here()
     y = dp & 3
     group = e0.shape[0]
     for k, piece in enumerate((e0, e1, e2, e3)):
         everyone[pl.ds(pl.multiple_of(((y + k) & 3) * group, group), group), :] = piece[...]
-    tables = (t0, t1, t2, t3)
-    rows = t0.shape[0]
+    rows = tables[0].shape[0]
     emb = thirds(everyone[...])
     scores = [folded(lax.dot_general(emb, t[...], NT, preferred_element_type=jnp.float32)) / TAU for t in tables]
-    tops = [jnp.max(s, axis=1, keepdims=True) for s in scores]
-    top = jnp.maximum(jnp.maximum(tops[0], tops[2]), jnp.maximum(tops[1], tops[3]))
+    top = functools.reduce(jnp.maximum, [jnp.max(s, axis=1, keepdims=True) for s in scores])
     row = lax.broadcasted_iota(jnp.int32, (all_docs, rows), 0)
     wanted = jnp.zeros((all_docs, rows), jnp.int32)
     for doc in range(all_docs):
@@ -372,6 +382,7 @@
         totals.append(jnp.sum(expo, axis=1, keepdims=True))
         hit = row_ids(k, (all_docs, rows), 1) == wanted
         found = found + jnp.sum(jnp.where(hit, s, 0.0), axis=1, keepdims=True)
+    totals = [totals[k] + totals[k + 4] for k in range(4)]
     total = (totals[0] + totals[2]) + (totals[1] + totals[3])
     mine = thirds(expos[pl.ds(pl.multiple_of(y * group, group), group), :])
     mix = jnp.zeros((group, width), jnp.float32)
@@ -497,23 +508,31 @@
     all_docs = n_dp * docs
     ring = [(i, (i + 2 * (i % 2) - 1) % n_ctx) for i in range(n_ctx)]
     fetch = lambda part: lax.ppermute(part, "ctx", ring)
-    early = fetch(tokens[0:2])
+    early, middle, late = fetch(tokens[0:1]), fetch(tokens[1:3]), tokens[3:]
     near = swap(tokens, "ctx", 1)
     tables = around(cache, from_y)
-    qk, v_turned, w_v_turned, third, fourth = prepare(in_hbm(tokens), in_hbm(w_qkv))
+    qk, v_turned, w_v_turned = prepare(in_hbm(tokens), in_hbm(w_qkv))
+    near_k, near_v = call(
+        near_kernel,
+        (bf16(docs, tb, width), bf16(width, docs * tb)),
+        [VMEM] * 3,
+        (VMEM,) * 2,
+        flops=4 * docs * tb * width * width,
+        moved=4 * 2**20,
+        name="near",
+    )(near, w_qkv, w_v_turned)
+    gain = ln_gain
+    fixed = (lengths, tokens, near_k), (near_v, qk, v_turned, w_qkv, w_v_turned, w_out, gain)
+    *done, pool = attend(0, None, *fixed[0], early, *fixed[1])
+    pool, after, *tables = lax.optimization_barrier((pool, positive, *tables))
+    others = [swap(table, "ctx", 1) for table in tables]
     target = call(
         functools.partial(target_kernel, docs), f32(2 * docs, width), [SMEM] + [VMEM] * 4, VMEM, name="target"
-    )(positive, *tables)
-    early, third = lax.optimization_barrier((early, third))
-    third = fetch(third)
-    early, target = lax.optimization_barrier((early, target))
-    gain = ln_gain
-    fixed = (lengths, tokens, near), (qk, v_turned, w_qkv, w_v_turned, w_out, gain)
-    *done, pool = attend(0, None, *fixed[0], early, *fixed[1])
-    pool, fourth = lax.optimization_barrier((pool, fourth))
-    fourth = fetch(fourth)
-    done = attend(2, [*done, pool], *fixed[0], third, *fixed[1])
-    done = attend(3, done, *fixed[0], fourth, *fixed[1])
+    )(after, *tables)
+    middle, late, target, *others = lax.optimization_barrier((middle, late, target, *others))
+    late = fetch(late)
+    done = attend(1, [*done, pool], *fixed[0], middle, *fixed[1])
+    done = attend(3, done, *fixed[0], late, *fixed[1])
     hidden, mixed, normed, rstd, pool = done
 
     turned = call(
@@ -544,12 +563,12 @@
     everyone, state = call(
         functools.partial(score_kernel, docs),
         (f32(all_docs, width), f32(2 * group, width + 256)),
-        [SMEM] + [VMEM] * 8,
+        [SMEM] + [VMEM] * 12,
         (VMEM, VMEM),
         moved=2 * 2**20,
-        scratch_shapes=[pltpu.VMEM((all_docs, n_dp * cache.shape[0]), jnp.float32)],
+        scratch_shapes=[pltpu.VMEM((all_docs, 8 * cache.shape[0]), jnp.float32)],
         name="score",
-    )(positive, *embs, *tables)
+    )(positive, *embs, *tables, *others)
     product, stats = call(
         batch_kernel,
         (f32(group, all_docs), f32(8, all_docs)),
@@ -558,7 +577,6 @@
         limit=4,
         name="batch",
     )(emb, everyone)
-    state = merged(group, width, [state, swap(state, "ctx", 1)])
     state = merged(group, width, around(state, from_x))
     half = width // 2
     send, d_summed, loss = call(

time: 135 us -> 131 us (0.970)
  starting transfers between devices: 61.5 us -> 56.5 us
  Pallas kernels: 44.3 us -> 45.8 us
    pallas_call x0 -> x1, Pallas kernels: none -> 3.13 us  [shards(): call(near_kernel, (bf16(docs, tb, width), bf16(width, docs * tb)), [VMEM]...]
    ppermute x6, starting transfers between devices: 10.2 us -> 7.88 us  [from_x(): lax.ppermute(value, 'ctx', [((c + 4 * k) % size, c) for c in range(size)])]
    pallas_call x3, Pallas kernels: 25.7 us -> 23.9 us  [attend(): call(functools.partial(attend_kernel, first), out_shape, in_specs, out_sp...]
    ppermute x6, starting transfers between devices: 11.3 us -> 9.77 us  [from_y(): lax.ppermute(value, 'dp', [(d & 4 | d + k & 3, d) for d in range(lax.axis...]
    ppermute x4 -> x7, starting transfers between devices: 6.47 us -> 5.87 us  [swap(): lax.ppermute(value, axis, [(i, i ^ bits) for i in range(lax.axis_size(axi...]
    ppermute x4 -> x7, waiting for transfers between devices: 3.8 us -> 3.54 us  [swap(): lax.ppermute(value, axis, [(i, i ^ bits) for i in range(lax.axis_size(axi...]
  transfers between devices with their start and end apart: 34 -> 37, of which waited for: 20 -> 22; matrix products, arithmetic and copies ran while one was open for 1% -> 1% of each run, Pallas kernels for 24% -> 26%
where the time goes in v1:
time: 131 us
  starting transfers between devices  56.5 us (43%)
  Pallas kernels  45.8 us (35%)
  waiting for transfers between devices  25.9 us (20%)
  local copies, waits for them, and re-layouts  1.77 us (1%)
    pallas_call x3, Pallas kernels, attend(): call(functools.partial(attend_kernel, first), out_shape, in_specs, out_sp...  23.9 us
    ppermute x9, starting transfers between devices, from_z(): return lax.ppermute(value, ('dp', 'ctx'), pairs)  12.9 us
    ppermute x3, starting transfers between devices, shards(): fetch = lambda part: lax.ppermute(part, 'ctx', ring)  11.2 us
    ppermute x6, starting transfers between devices, from_y(): lax.ppermute(value, 'dp', [(d & 4 | d + k & 3, d) for d in range(lax.axis...  9.77 us
    ppermute x6, starting transfers between devices, from_plane(): return lax.ppermute(value, ('dp', 'ctx'), pairs)  8.91 us
    ppermute x6, waiting for transfers between devices, from_plane(): return lax.ppermute(value, ('dp', 'ctx'), pairs)  8.09 us
    ppermute x6, starting transfers between devices, from_x(): lax.ppermute(value, 'ctx', [((c + 4 * k) % size, c) for c in range(size)])  7.88 us
    ppermute x6, waiting for transfers between devices, from_x(): lax.ppermute(value, 'ctx', [((c + 4 * k) % size, c) for c in range(size)])  7.29 us
  transfers between devices with their start and end apart: 37, of which 22 were waited for; matrix products, arithmetic and copies ran while one was open for 1% of the time, Pallas kernels for 26%

profile of v1, /device:TPU:0, one launch (start us, length us, event | category | flops | bytes accessed | tf_op | source)
XLA Modules:
  0.0 131.0 jit_solution(971707824695625073)
XLA Ops:
  0.7 3.4 %collective-permute-start.4 = (bf16[128,768]{1,0:T(8,128)(2,1)}, bf16[128,768]{1,0:T(8,128)(2,1)S(1)}, u32[]{:S(2)}, u32[]{:S(2)}) collective-permute-start(bf16[128,768]{1,0:T(8,128)(2,1)} %refs_0_.7), channel_id=1, source_target_pairs={{32,0},{48,16},{0,32},{16,48},{96,64},{112,80},{64,96},{80,112},{3... | collective-permute-start | bytes 589832 | tf_op jit(solution)/shard_map/ppermute | solution.py:33
  4.1 1.1 collective-permute-start.3
  5.1 1.2 fusion
  6.3 5.6 %collective-permute-start.2 = (bf16[1,256,768]{2,1,0:T(8,128)(2,1)S(1)}, bf16[1,256,768]{2,1,0:T(8,128)(2,1)S(1)}, u32[]{:S(2)}, u32[]{:S(2)}) collective-permute-start(bf16[1,256,768]{2,1,0:T(8,128)(2,1)S(1)} %get-tuple-element.113), channel_id=1, source_target_pairs={{0,15},{1,2},{2,1},{3,4},{4,3},{5,6},{6,5},{7,8},{8,7},{9,10},{10,... | collective-permute-start | bytes 1179656 | tf_op jit(solution)/shard_map/ppermute | solution.py:510
  12.1 7.2 %prepare.1 = (bf16[4,256,1536]{2,1,0:T(8,128)(2,1)S(1)}, bf16[768,1024]{1,0:T(8,128)(2,1)S(1)}, bf16[768,768]{1,0:T(8,128)(2,1)S(1)}) custom-call(bf16[4,256,768]{2,1,0:T(8,128)(2,1)} %refs_1_.5, bf16[768,2304]{1,0:T(8,128)(2,1)} %refs_7_.5), custom_call_target="tpu_custom_call" | custom-call | flops 3623878656 | bytes 11534336 | tf_op jit(solution)/shard_map/prepare/pallas_call | solution.py:253
  19.3 1.0 collective-permute-start.5
  20.4 3.1 %near.1 = (bf16[4,256,768]{2,1,0:T(8,128)(2,1)S(1)}, bf16[768,1024]{1,0:T(8,128)(2,1)S(1)}) custom-call(bf16[4,256,768]{2,1,0:T(8,128)(2,1)S(1)} %collective-permute-done.near, bf16[768,2304]{1,0:T(8,128)(2,1)S(1)} %copy-done, bf16[768,768]{1,0:T(8,128)(2,1)S(1)} %get-tuple-element.58.w_v_turned.refs_8_), custom_call_target="tpu_custom_call" | custom-call | flops 2415919104 | bytes 4194304 | tf_op jit(solution)/shard_map/near/pallas_call | solution.py:515
  23.6 6.1 %attend.3 = (bf16[4,256,768]{2,1,0:T(8,128)(2,1)}, bf16[768,1024]{1,0:T(8,128)(2,1)S(1)}, bf16[4,256,768]{2,1,0:T(8,128)(2,1)S(1)}, f32[4,256,128]{2,1,0:T(8,128)S(1)}, f32[4,1,768]{2,1,0:T(1,128)S(1)}) custom-call(s32[4]{0:T(128)S(1)} %copy-done.6, bf16[4,256,768]{2,1,0:T(8,128)(2,1)S(1)} %copy-done.2, bf16[4,256,768]{2,1,0:T(8,128)(2,1)S(1)} %get-tuple-element.59.refs_2_, ...), custom_call_target="tpu_custom_call" | custom-call | flops 1509949440 | bytes 4194304 | tf_op jit(solution)/shard_map/attend/pallas_call | solution.py:205
  29.7 5.0 %collective-permute-start.6 = (bf16[128,768]{1,0:T(8,128)(2,1)S(1)}, bf16[128,768]{1,0:T(8,128)(2,1)S(1)}, u32[]{:S(2)}, u32[]{:S(2)}) collective-permute-start(bf16[128,768]{1,0:T(8,128)(2,1)S(1)} %copy-done.4), channel_id=1, source_target_pairs={{0,1},{1,0},{2,3},{3,2},{4,5},{5,4},{6,7},{7,6},{8,9},{9,8},{10,11... | collective-permute-start | bytes 589832 | tf_op jit(solution)/shard_map/ppermute | solution.py:24
  36.7 5.5 %collective-permute-start.10 = (bf16[1,256,768]{2,1,0:T(8,128)(2,1)S(1)}, bf16[1,256,768]{2,1,0:T(8,128)(2,1)S(1)}, u32[]{:S(2)}, u32[]{:S(2)}) collective-permute-start(bf16[1,256,768]{2,1,0:T(8,128)(2,1)S(1)} %get-tuple-element.69), channel_id=1, source_target_pairs={{0,15},{1,2},{2,1},{3,4},{4,3},{5,6},{6,5},{7,8},{8,7},{9,10},{10,... | collective-permute-start | bytes 1179656 | tf_op jit(solution)/shard_map/ppermute | solution.py:510
  42.2 11.7 %attend.4 = (bf16[4,256,768]{2,1,0:T(8,128)(2,1)}, bf16[768,1024]{1,0:T(8,128)(2,1)S(1)}, bf16[4,256,768]{2,1,0:T(8,128)(2,1)S(1)}, f32[4,256,128]{2,1,0:T(8,128)S(1)}, f32[4,1,768]{2,1,0:T(1,128)S(1)}) custom-call(s32[4]{0:T(128)S(1)} %copy-done.6, ...), custom_call_target="tpu_custom_call", output_to_operand_aliasing={{0}: (11, {}), {1}: (12, {}), {2}: (13, {}), {3}: (14, {}),... | custom-call | flops 3019898880 | bytes 4194304 | tf_op jit(solution)/shard_map/attend/pallas_call | solution.py:205
  53.9 6.1 %attend.5 = (bf16[4,256,768]{2,1,0:T(8,128)(2,1)}, bf16[768,1024]{1,0:T(8,128)(2,1)S(1)}, bf16[4,256,768]{2,1,0:T(8,128)(2,1)S(1)}, f32[4,256,128]{2,1,0:T(8,128)S(1)}, f32[4,1,768]{2,1,0:T(1,128)S(1)}) custom-call(s32[4]{0:T(128)S(1)} %copy-done.6, ...), custom_call_target="tpu_custom_call", output_to_operand_aliasing={{0}: (11, {}), {1}: (12, {}), {2}: (13, {}), {3}: (14, {}),... | custom-call | flops 1509949440 | bytes 4194304 | tf_op jit(solution)/shard_map/attend/pallas_call | solution.py:205
  60.1 1.2 collective-permute-done.11.refs_1_
  61.4 2.3 %collective-permute-start.13 = (f32[12,768]{1,0:T(8,128)S(1)}, f32[12,768]{1,0:T(8,128)S(1)}, u32[]{:S(2)}, u32[]{:S(2)}) collective-permute-start(f32[12,768]{1,0:T(8,128)S(1)} %add.3.refs_0_), channel_id=1, source_target_pairs={{8,0},{9,1},{10,2},{11,3},{12,4},{13,5},{14,6},{15,7},{0,8},{1,9},... | collective-permute-start | bytes 110600 | tf_op jit(solution)/shard_map/ppermute | solution.py:29
  63.7 1.2 collective-permute-start.12
  64.9 2.5 %collective-permute-done.14.refs_3_ = f32[12,768]{1,0:T(8,128)S(1)} collective-permute-done((f32[12,768]{1,0:T(8,128)S(1)}, f32[12,768]{1,0:T(8,128)S(1)}, u32[]{:S(2)}, u32[]{:S(2)}) %collective-permute-start.14) | collective-permute-done | bytes 36896 | tf_op jit(solution)/shard_map/ppermute | solution.py:29
  68.1 1.1 collective-permute-start.17
  69.2 1.6 %collective-permute-start.16 = (f32[12,768]{1,0:T(8,128)S(1)}, f32[12,768]{1,0:T(8,128)S(1)}, u32[]{:S(2)}, u32[]{:S(2)}) collective-permute-start(f32[12,768]{1,0:T(8,128)S(1)} %add.4.s0), channel_id=1, source_target_pairs={{2,0},{3,1},{0,2},{1,3},{6,4},{7,5},{4,6},{5,7},{10,8},{11,9},{8,1... | collective-permute-start | bytes 110600 | tf_op jit(solution)/shard_map/ppermute | solution.py:43
  70.8 1.2 collective-permute-start.15
  72.0 1.5 %collective-permute-done.17.s3 = f32[12,768]{1,0:T(8,128)S(1)} collective-permute-done((f32[12,768]{1,0:T(8,128)S(1)}, f32[12,768]{1,0:T(8,128)S(1)}, u32[]{:S(2)}, u32[]{:S(2)}) %collective-permute-start.17) | collective-permute-done | bytes 36896 | tf_op jit(solution)/shard_map/ppermute | solution.py:43
  73.5 1.3 collective-permute-done.16.s2
  75.0 1.0 collective-permute-start.20
  76.8 2.5 %collective-permute-start.18 = (f32[8,768]{1,0:T(8,128)S(1)}, f32[8,768]{1,0:T(8,128)S(1)}, u32[]{:S(2)}, u32[]{:S(2)}) collective-permute-start(f32[8,768]{1,0:T(8,128)S(1)} %get-tuple-element.84.e0.emb), channel_id=1, source_target_pairs={{16,0},{32,16},{48,32},{0,48},{80,64},{96,80},{112,96},{64,112},{1... | collective-permute-start | bytes 73736 | tf_op jit(solution)/shard_map/ppermute | solution.py:33
  80.0 1.3 collective-permute-done.19.e2
  81.3 1.7 %score.1 = (f32[32,768]{1,0:T(8,128)S(1)}, f32[16,1024]{1,0:T(8,128)S(1)}) custom-call(s32[32]{0:T(128)S(1)} %copy-done.7, f32[8,768]{1,0:T(8,128)S(1)} %get-tuple-element.84.e0.emb, f32[8,768]{1,0:T(8,128)S(1)} %collective-permute-done.18.e1, f32[8,768]{1,0:T(8,128)S(1)} %collective-permute-done.19.e2, f32[8,768]{1,0:T(8,128)S(1)} %collective-permute-done.20.e3, ...), custom_call_target="tpu_custom_call" | custom-call | bytes 2097152 | tf_op jit(solution)/shard_map/score/pallas_call | solution.py:563
  83.0 1.6 %collective-permute-start.23 = (f32[16,1024]{1,0:T(8,128)S(1)}, f32[16,1024]{1,0:T(8,128)S(1)}, u32[]{:S(2)}, u32[]{:S(2)}) collective-permute-start(f32[16,1024]{1,0:T(8,128)S(1)} %get-tuple-element.89.refs_0_), channel_id=1, source_target_pairs={{12,0},{13,1},{14,2},{15,3},{0,4},{1,5},{2,6},{3,7},{4,8},{5,9},{6... | collective-permute-start | bytes 196616 | tf_op jit(solution)/shard_map/ppermute | solution.py:29
  84.6 2.6 %collective-permute-start.22 = (f32[16,1024]{1,0:T(8,128)S(1)}, f32[16,1024]{1,0:T(8,128)S(1)}, u32[]{:S(2)}, u32[]{:S(2)}) collective-permute-start(f32[16,1024]{1,0:T(8,128)S(1)} %get-tuple-element.89.refs_0_), channel_id=1, source_target_pairs={{8,0},{9,1},{10,2},{11,3},{12,4},{13,5},{14,6},{15,7},{0,8},{1,9},... | collective-permute-start | bytes 196616 | tf_op jit(solution)/shard_map/ppermute | solution.py:29
  87.4 1.2 collective-permute-done.23.refs_3_
  88.6 1.8 %collective-permute-done.22.refs_2_ = f32[16,1024]{1,0:T(8,128)S(1)} collective-permute-done((f32[16,1024]{1,0:T(8,128)S(1)}, f32[16,1024]{1,0:T(8,128)S(1)}, u32[]{:S(2)}, u32[]{:S(2)}) %collective-permute-start.22) | collective-permute-done | bytes 65568 | tf_op jit(solution)/shard_map/ppermute | solution.py:29
  90.4 1.1 collective-permute-done.21.refs_1_
  91.6 1.6 %collective-permute-start.26 = (f32[16,1024]{1,0:T(8,128)S(1)}, f32[16,1024]{1,0:T(8,128)S(1)}, u32[]{:S(2)}, u32[]{:S(2)}) collective-permute-start(f32[16,1024]{1,0:T(8,128)S(1)} %merge.1.s0), channel_id=1, source_target_pairs={{66,0},{67,1},{64,2},{65,3},{70,4},{71,5},{68,6},{69,7},{74,8},{75... | collective-permute-start | bytes 196616 | tf_op jit(solution)/shard_map/ppermute | solution.py:43
  93.1 2.6 %collective-permute-start.25 = (f32[16,1024]{1,0:T(8,128)S(1)}, f32[16,1024]{1,0:T(8,128)S(1)}, u32[]{:S(2)}, u32[]{:S(2)}) collective-permute-start(f32[16,1024]{1,0:T(8,128)S(1)} %merge.1.s0), channel_id=1, source_target_pairs={{2,0},{3,1},{0,2},{1,3},{6,4},{7,5},{4,6},{5,7},{10,8},{11,9},{8,1... | collective-permute-start | bytes 196616 | tf_op jit(solution)/shard_map/ppermute | solution.py:43
  96.2 3.6 %turn.1.turned = bf16[768,1024]{1,0:T(8,128)(2,1)S(1)} custom-call(bf16[768,1024]{1,0:T(8,128)(2,1)S(1)} %get-tuple-element.97.mixed), custom_call_target="tpu_custom_call" | custom-call | flops 1207959552 | bytes 4194304 | tf_op jit(solution)/shard_map/turn/pallas_call | solution.py:538
  100.2 2.9 %grad.1 = (f32[384,768]{1,0:T(8,128)S(1)}, bf16[1024,768]{1,0:T(8,128)(2,1)S(1)}, f32[8,128]{1,0:T(8,128)S(1)}) custom-call(s32[4]{0:T(128)S(1)} %copy-done.6, f32[16,1024]{1,0:T(8,128)S(1)} %merge.1.s0, f32[16,1024]{1,0:T(8,128)S(1)} %collective-permute-done.24.s1, f32[16,1024]{1,0:T(8,128)S(1)} %collective-permute-done.25.s2, ...), custom_call_target="tpu_custom_call" | custom-call | flops 603979776 | bytes 8388608 | tf_op jit(solution)/shard_map/grad/pallas_call | solution.py:582
  103.3 1.2 keep.1.refs_0_
  104.4 1.7 %collective-permute-done.27.refs_1_ = f32[384,768]{1,0:T(8,128)S(1)} collective-permute-done((f32[384,768]{1,0:T(8,128)S(1)}, f32[384,768]{1,0:T(8,128)S(1)}, u32[]{:S(2)}, u32[]{:S(2)}) %collective-permute-start.27) | collective-permute-done | bytes 1179680 | tf_op jit(solution)/shard_map/ppermute | solution.py:24
  106.3 1.7 %collective-permute-start.28 = (bf16[96,768]{1,0:T(8,128)(2,1)S(1)}, bf16[96,768]{1,0:T(8,128)(2,1)S(1)}, u32[]{:S(2)}, u32[]{:S(2)}) collective-permute-start(bf16[96,768]{1,0:T(8,128)(2,1)S(1)} %get-tuple-element.102), channel_id=1, source_target_pairs={{48,0},{13,1},{50,2},{15,3},{52,4},{1,5},{54,6},{3,7},{56,8},{5,9}... | collective-permute-start | bytes 442376 | tf_op jit(solution)/shard_map/ppermute | solution.py:54
  108.0 2.9 %collective-permute-start.29 = (bf16[96,768]{1,0:T(8,128)(2,1)S(1)}, bf16[96,768]{1,0:T(8,128)(2,1)S(1)}, u32[]{:S(2)}, u32[]{:S(2)}) collective-permute-start(bf16[96,768]{1,0:T(8,128)(2,1)S(1)} %get-tuple-element.103), channel_id=1, source_target_pairs={{32,0},{9,1},{34,2},{11,3},{36,4},{13,5},{38,6},{15,7},{40,8},{1,9... | collective-permute-start | bytes 442376 | tf_op jit(solution)/shard_map/ppermute | solution.py:54
  111.0 1.7 %collective-permute-done.28.refs_1_ = bf16[96,768]{1,0:T(8,128)(2,1)S(1)} collective-permute-done((bf16[96,768]{1,0:T(8,128)(2,1)S(1)}, bf16[96,768]{1,0:T(8,128)(2,1)S(1)}, u32[]{:S(2)}, u32[]{:S(2)}) %collective-permute-start.28) | collective-permute-done | bytes 147488 | tf_op jit(solution)/shard_map/ppermute | solution.py:54
  112.7 2.9 %collective-permute-done.29.refs_2_ = bf16[96,768]{1,0:T(8,128)(2,1)S(1)} collective-permute-done((bf16[96,768]{1,0:T(8,128)(2,1)S(1)}, bf16[96,768]{1,0:T(8,128)(2,1)S(1)}, u32[]{:S(2)}, u32[]{:S(2)}) %collective-permute-start.29) | collective-permute-done | bytes 147488 | tf_op jit(solution)/shard_map/ppermute | solution.py:54
  116.2 2.8 %collective-permute-start.32 = (f32[24,768]{1,0:T(8,128)S(1)}, f32[24,768]{1,0:T(8,128)S(1)}, u32[]{:S(2)}, u32[]{:S(2)}) collective-permute-start(f32[24,768]{1,0:T(8,128)S(1)} %get-tuple-element.107), channel_id=1, source_target_pairs={{8,0},{33,1},{10,2},{35,3},{12,4},{37,5},{14,6},{39,7},{0,8},{41,9... | collective-permute-start | bytes 221192 | tf_op jit(solution)/shard_map/ppermute | solution.py:54
  119.0 1.3 collective-permute-start.33
  120.3 2.2 %collective-permute-done.31.refs_1_ = f32[24,768]{1,0:T(8,128)S(1)} collective-permute-done((f32[24,768]{1,0:T(8,128)S(1)}, f32[24,768]{1,0:T(8,128)S(1)}, u32[]{:S(2)}, u32[]{:S(2)}) %collective-permute-start.31) | collective-permute-done | bytes 73760 | tf_op jit(solution)/shard_map/ppermute | solution.py:54
  122.5 0.9 collective-permute-done.33.refs_3_
  123.4 1.6 %collective-permute-start.34 = (f32[6,768]{1,0:T(8,128)S(1)}, f32[6,768]{1,0:T(8,128)S(1)}, u32[]{:S(2)}, u32[]{:S(2)}) collective-permute-start(f32[6,768]{1,0:T(8,128)S(1)} %get-tuple-element.110), channel_id=1, source_target_pairs={{66,0},{67,1},{64,2},{65,3},{70,4},{71,5},{68,6},{69,7},{74,8},{75... | collective-permute-start | bytes 55304 | tf_op jit(solution)/shard_map/ppermute | solution.py:43
  125.0 1.4 %collective-permute-start.35 = (f32[6,768]{1,0:T(8,128)S(1)}, f32[6,768]{1,0:T(8,128)S(1)}, u32[]{:S(2)}, u32[]{:S(2)}) collective-permute-start(f32[6,768]{1,0:T(8,128)S(1)} %get-tuple-element.111), channel_id=1, source_target_pairs={{2,0},{3,1},{0,2},{1,3},{6,4},{7,5},{4,6},{5,7},{10,8},{11,9},{8,1... | collective-permute-start | bytes 55304 | tf_op jit(solution)/shard_map/ppermute | solution.py:43
  126.4 1.4 %collective-permute-start.36 = (f32[6,768]{1,0:T(8,128)S(1)}, f32[6,768]{1,0:T(8,128)S(1)}, u32[]{:S(2)}, u32[]{:S(2)}) collective-permute-start(f32[6,768]{1,0:T(8,128)S(1)} %get-tuple-element.112), channel_id=1, source_target_pairs={{64,0},{65,1},{66,2},{67,3},{68,4},{69,5},{70,6},{71,7},{72,8},{73... | collective-permute-start | bytes 55304 | tf_op jit(solution)/shard_map/ppermute | solution.py:43
  128.5 1.9 %collective-permute-done.35.refs_2_ = f32[6,768]{1,0:T(8,128)S(1)} collective-permute-done((f32[6,768]{1,0:T(8,128)S(1)}, f32[6,768]{1,0:T(8,128)S(1)}, u32[]{:S(2)}, u32[]{:S(2)}) %collective-permute-start.35) | collective-permute-done | bytes 18464 | tf_op jit(solution)/shard_map/ppermute | solution.py:43
  (65 shorter events, 8.2 us)
Async XLA Ops:
  0.6 11.3 %copy-start.1 = (bf16[4,256,768]{2,1,0:T(8,128)(2,1)S(1)}, bf16[4,256,768]{2,1,0:T(8,128)(2,1)}, u32[]{:S(2)}) copy-start(bf16[4,256,768]{2,1,0:T(8,128)(2,1)} %refs_1_.5) | copy-start | bytes 4718596
  0.6 18.7 %collective-permute-start = (bf16[4,256,768]{2,1,0:T(8,128)(2,1)}, bf16[4,256,768]{2,1,0:T(8,128)(2,1)S(1)}, u32[]{:S(2)}, u32[]{:S(2)}) collective-permute-start(bf16[4,256,768]{2,1,0:T(8,128)(2,1)} %refs_1_.5), channel_id=1, source_target_pairs={{0,1},{1,0},{2,3},{3,2},{4,5},{5,4},{6,7},{7,6},{8,9},{9,8},{10,11... | collective-permute-start | bytes 4718600 | tf_op jit(solution)/shard_map/ppermute | solution.py:24
  0.7 29.0 %collective-permute-start.4 = (bf16[128,768]{1,0:T(8,128)(2,1)}, bf16[128,768]{1,0:T(8,128)(2,1)S(1)}, u32[]{:S(2)}, u32[]{:S(2)}) collective-permute-start(bf16[128,768]{1,0:T(8,128)(2,1)} %refs_0_.7), channel_id=1, source_target_pairs={{32,0},{48,16},{0,32},{16,48},{96,64},{112,80},{64,96},{80,112},{3... | collective-permute-start | bytes 589832 | tf_op jit(solution)/shard_map/ppermute | solution.py:33
  4.1 25.6 %collective-permute-start.3 = (bf16[128,768]{1,0:T(8,128)(2,1)}, bf16[128,768]{1,0:T(8,128)(2,1)S(1)}, u32[]{:S(2)}, u32[]{:S(2)}) collective-permute-start(bf16[128,768]{1,0:T(8,128)(2,1)} %refs_0_.7), channel_id=1, source_target_pairs={{16,0},{32,16},{48,32},{0,48},{80,64},{96,80},{112,96},{64,112},{1... | collective-permute-start | bytes 589832 | tf_op jit(solution)/shard_map/ppermute | solution.py:33
  6.3 17.2 %collective-permute-start.2 = (bf16[1,256,768]{2,1,0:T(8,128)(2,1)S(1)}, bf16[1,256,768]{2,1,0:T(8,128)(2,1)S(1)}, u32[]{:S(2)}, u32[]{:S(2)}) collective-permute-start(bf16[1,256,768]{2,1,0:T(8,128)(2,1)S(1)} %get-tuple-element.113), channel_id=1, source_target_pairs={{0,15},{1,2},{2,1},{3,4},{4,3},{5,6},{6,5},{7,8},{8,7},{9,10},{10,... | collective-permute-start | bytes 1179656 | tf_op jit(solution)/shard_map/ppermute | solution.py:510
  12.0 7.3 %copy-start.4 = (bf16[128,768]{1,0:T(8,128)(2,1)S(1)}, bf16[128,768]{1,0:T(8,128)(2,1)}, u32[]{:S(2)}) copy-start(bf16[128,768]{1,0:T(8,128)(2,1)} %refs_0_.7) | copy-start | bytes 589828
  12.0 8.4 %copy-start = (bf16[768,2304]{1,0:T(8,128)(2,1)S(1)}, bf16[768,2304]{1,0:T(8,128)(2,1)}, u32[]{:S(2)}) copy-start(bf16[768,2304]{1,0:T(8,128)(2,1)} %refs_7_.5) | copy-start | bytes 10616836
  12.0 24.0 %collective-permute-start.1 = (bf16[2,256,768]{2,1,0:T(8,128)(2,1)S(1)}, bf16[2,256,768]{2,1,0:T(8,128)(2,1)S(1)}, u32[]{:S(2)}, u32[]{:S(2)}) collective-permute-start(bf16[2,256,768]{2,1,0:T(8,128)(2,1)S(1)} %slice.12), channel_id=1, source_target_pairs={{0,15},{1,2},{2,1},{3,4},{4,3},{5,6},{6,5},{7,8},{8,7},{9,10},{10,... | collective-permute-start | bytes 2359304 | tf_op jit(solution)/shard_map/ppermute | solution.py:510
  19.3 10.4 %collective-permute-start.5 = (bf16[128,768]{1,0:T(8,128)(2,1)S(1)}, bf16[128,768]{1,0:T(8,128)(2,1)S(1)}, u32[]{:S(2)}, u32[]{:S(2)}) collective-permute-start(bf16[128,768]{1,0:T(8,128)(2,1)S(1)} %copy-done.4), channel_id=1, source_target_pairs={{48,0},{0,16},{16,32},{32,48},{112,64},{64,80},{80,96},{96,112},{4... | collective-permute-start | bytes 589832 | tf_op jit(solution)/shard_map/ppermute | solution.py:33
  20.4 3.2 %copy-start.2 = (bf16[4,256,768]{2,1,0:T(8,128)(2,1)S(1)}, bf16[4,256,768]{2,1,0:T(8,128)(2,1)}, u32[]{:S(2)}) copy-start(bf16[4,256,768]{2,1,0:T(8,128)(2,1)} %refs_1_.5) | copy-start | bytes 4718596
  20.4 3.2 %copy-start.3 = (bf16[768,768]{1,0:T(8,128)(2,1)S(1)}, bf16[768,768]{1,0:T(8,128)(2,1)}, u32[]{:S(2)}) copy-start(bf16[768,768]{1,0:T(8,128)(2,1)} %refs_9_.5) | copy-start | bytes 3538948
  20.4 3.2 %copy-start.5 = (f32[768]{0:T(1024)S(1)}, f32[768]{0:T(1024)}, u32[]{:S(2)}) copy-start(f32[768]{0:T(1024)} %gain.1) | copy-start | bytes 9220
  20.4 3.2 %copy-start.6 = (s32[4]{0:T(128)S(1)}, s32[4]{0:T(128)}, u32[]{:S(2)}) copy-start(s32[4]{0:T(128)} %lengths.1) | copy-start | bytes 52
  23.6 11.8 %copy-start.7 = (s32[32]{0:T(128)S(1)}, s32[32]{0:T(128)}, u32[]{:S(2)}) copy-start(s32[32]{0:T(128)} %positive.2) | copy-start | bytes 388
  29.7 6.4 %collective-permute-start.6 = (bf16[128,768]{1,0:T(8,128)(2,1)S(1)}, bf16[128,768]{1,0:T(8,128)(2,1)S(1)}, u32[]{:S(2)}, u32[]{:S(2)}) collective-permute-start(bf16[128,768]{1,0:T(8,128)(2,1)S(1)} %copy-done.4), channel_id=1, source_target_pairs={{0,1},{1,0},{2,3},{3,2},{4,5},{5,4},{6,7},{7,6},{8,9},{9,8},{10,11... | collective-permute-start | bytes 589832 | tf_op jit(solution)/shard_map/ppermute | solution.py:24
  34.7 1.4 %collective-permute-start.7 = (bf16[128,768]{1,0:T(8,128)(2,1)S(1)}, bf16[128,768]{1,0:T(8,128)(2,1)S(1)}, u32[]{:S(2)}, u32[]{:S(2)}) collective-permute-start(bf16[128,768]{1,0:T(8,128)(2,1)S(1)} %collective-permute-done.3.refs_1_), channel_id=1, source_target_pairs={{0,1},{1,0},{2,3},{3,2},{4,5},{5,4},{6,7},{7,6},{8,9},{9,8},{10,11... | collective-permute-start | bytes 589832 | tf_op jit(solution)/shard_map/ppermute | solution.py:24
  34.8 1.6 %collective-permute-start.8 = (bf16[128,768]{1,0:T(8,128)(2,1)S(1)}, bf16[128,768]{1,0:T(8,128)(2,1)S(1)}, u32[]{:S(2)}, u32[]{:S(2)}) collective-permute-start(bf16[128,768]{1,0:T(8,128)(2,1)S(1)} %collective-permute-done.4.refs_2_), channel_id=1, source_target_pairs={{0,1},{1,0},{2,3},{3,2},{4,5},{5,4},{6,7},{7,6},{8,9},{9,8},{10,11... | collective-permute-start | bytes 589832 | tf_op jit(solution)/shard_map/ppermute | solution.py:24
  35.2 1.5 %collective-permute-start.9 = (bf16[128,768]{1,0:T(8,128)(2,1)S(1)}, bf16[128,768]{1,0:T(8,128)(2,1)S(1)}, u32[]{:S(2)}, u32[]{:S(2)}) collective-permute-start(bf16[128,768]{1,0:T(8,128)(2,1)S(1)} %collective-permute-done.5.refs_3_), channel_id=1, source_target_pairs={{0,1},{1,0},{2,3},{3,2},{4,5},{5,4},{6,7},{7,6},{8,9},{9,8},{10,11... | collective-permute-start | bytes 589832 | tf_op jit(solution)/shard_map/ppermute | solution.py:24
  36.7 17.2 %collective-permute-start.10 = (bf16[1,256,768]{2,1,0:T(8,128)(2,1)S(1)}, bf16[1,256,768]{2,1,0:T(8,128)(2,1)S(1)}, u32[]{:S(2)}, u32[]{:S(2)}) collective-permute-start(bf16[1,256,768]{2,1,0:T(8,128)(2,1)S(1)} %get-tuple-element.69), channel_id=1, source_target_pairs={{0,15},{1,2},{2,1},{3,4},{4,3},{5,6},{6,5},{7,8},{8,7},{9,10},{10,... | collective-permute-start | bytes 1179656 | tf_op jit(solution)/shard_map/ppermute | solution.py:510
  60.0 1.3 %collective-permute-start.11 = (f32[12,768]{1,0:T(8,128)S(1)}, f32[12,768]{1,0:T(8,128)S(1)}, u32[]{:S(2)}, u32[]{:S(2)}) collective-permute-start(f32[12,768]{1,0:T(8,128)S(1)} %stack.1.refs_0_), channel_id=1, source_target_pairs={{0,1},{1,0},{2,3},{3,2},{4,5},{5,4},{6,7},{7,6},{8,9},{9,8},{10,11... | collective-permute-start | bytes 110600 | tf_op jit(solution)/shard_map/ppermute | solution.py:24
  61.4 6.1 %collective-permute-start.14 = (f32[12,768]{1,0:T(8,128)S(1)}, f32[12,768]{1,0:T(8,128)S(1)}, u32[]{:S(2)}, u32[]{:S(2)}) collective-permute-start(f32[12,768]{1,0:T(8,128)S(1)} %add.3.refs_0_), channel_id=1, source_target_pairs={{12,0},{13,1},{14,2},{15,3},{0,4},{1,5},{2,6},{3,7},{4,8},{5,9},{6... | collective-permute-start | bytes 110600 | tf_op jit(solution)/shard_map/ppermute | solution.py:29
  61.4 6.0 %collective-permute-start.13 = (f32[12,768]{1,0:T(8,128)S(1)}, f32[12,768]{1,0:T(8,128)S(1)}, u32[]{:S(2)}, u32[]{:S(2)}) collective-permute-start(f32[12,768]{1,0:T(8,128)S(1)} %add.3.refs_0_), channel_id=1, source_target_pairs={{8,0},{9,1},{10,2},{11,3},{12,4},{13,5},{14,6},{15,7},{0,8},{1,9},... | collective-permute-start | bytes 110600 | tf_op jit(solution)/shard_map/ppermute | solution.py:29
  63.7 4.4 %collective-permute-start.12 = (f32[12,768]{1,0:T(8,128)S(1)}, f32[12,768]{1,0:T(8,128)S(1)}, u32[]{:S(2)}, u32[]{:S(2)}) collective-permute-start(f32[12,768]{1,0:T(8,128)S(1)} %add.3.refs_0_), channel_id=1, source_target_pairs={{4,0},{5,1},{6,2},{7,3},{8,4},{9,5},{10,6},{11,7},{12,8},{13,9},{1... | collective-permute-start | bytes 110600 | tf_op jit(solution)/shard_map/ppermute | solution.py:29
  68.1 5.4 %collective-permute-start.17 = (f32[12,768]{1,0:T(8,128)S(1)}, f32[12,768]{1,0:T(8,128)S(1)}, u32[]{:S(2)}, u32[]{:S(2)}) collective-permute-start(f32[12,768]{1,0:T(8,128)S(1)} %add.4.s0), channel_id=1, source_target_pairs={{66,0},{67,1},{64,2},{65,3},{70,4},{71,5},{68,6},{69,7},{74,8},{75... | collective-permute-start | bytes 110600 | tf_op jit(solution)/shard_map/ppermute | solution.py:43
  69.2 5.6 %collective-permute-start.16 = (f32[12,768]{1,0:T(8,128)S(1)}, f32[12,768]{1,0:T(8,128)S(1)}, u32[]{:S(2)}, u32[]{:S(2)}) collective-permute-start(f32[12,768]{1,0:T(8,128)S(1)} %add.4.s0), channel_id=1, source_target_pairs={{2,0},{3,1},{0,2},{1,3},{6,4},{7,5},{4,6},{5,7},{10,8},{11,9},{8,1... | collective-permute-start | bytes 110600 | tf_op jit(solution)/shard_map/ppermute | solution.py:43
  70.8 4.1 %collective-permute-start.15 = (f32[12,768]{1,0:T(8,128)S(1)}, f32[12,768]{1,0:T(8,128)S(1)}, u32[]{:S(2)}, u32[]{:S(2)}) collective-permute-start(f32[12,768]{1,0:T(8,128)S(1)} %add.4.s0), channel_id=1, source_target_pairs={{64,0},{65,1},{66,2},{67,3},{68,4},{69,5},{70,6},{71,7},{72,8},{73... | collective-permute-start | bytes 110600 | tf_op jit(solution)/shard_map/ppermute | solution.py:43
  75.0 5.0 %collective-permute-start.20 = (f32[8,768]{1,0:T(8,128)S(1)}, f32[8,768]{1,0:T(8,128)S(1)}, u32[]{:S(2)}, u32[]{:S(2)}) collective-permute-start(f32[8,768]{1,0:T(8,128)S(1)} %get-tuple-element.84.e0.emb), channel_id=1, source_target_pairs={{48,0},{0,16},{16,32},{32,48},{112,64},{64,80},{80,96},{96,112},{4... | collective-permute-start | bytes 73736 | tf_op jit(solution)/shard_map/ppermute | solution.py:33
  76.0 5.3 %collective-permute-start.19 = (f32[8,768]{1,0:T(8,128)S(1)}, f32[8,768]{1,0:T(8,128)S(1)}, u32[]{:S(2)}, u32[]{:S(2)}) collective-permute-start(f32[8,768]{1,0:T(8,128)S(1)} %get-tuple-element.84.e0.emb), channel_id=1, source_target_pairs={{32,0},{48,16},{0,32},{16,48},{96,64},{112,80},{64,96},{80,112},{3... | collective-permute-start | bytes 73736 | tf_op jit(solution)/shard_map/ppermute | solution.py:33
  76.8 4.5 %collective-permute-start.18 = (f32[8,768]{1,0:T(8,128)S(1)}, f32[8,768]{1,0:T(8,128)S(1)}, u32[]{:S(2)}, u32[]{:S(2)}) collective-permute-start(f32[8,768]{1,0:T(8,128)S(1)} %get-tuple-element.84.e0.emb), channel_id=1, source_target_pairs={{16,0},{32,16},{48,32},{0,48},{80,64},{96,80},{112,96},{64,112},{1... | collective-permute-start | bytes 73736 | tf_op jit(solution)/shard_map/ppermute | solution.py:33
  83.0 5.5 %collective-permute-start.23 = (f32[16,1024]{1,0:T(8,128)S(1)}, f32[16,1024]{1,0:T(8,128)S(1)}, u32[]{:S(2)}, u32[]{:S(2)}) collective-permute-start(f32[16,1024]{1,0:T(8,128)S(1)} %get-tuple-element.89.refs_0_), channel_id=1, source_target_pairs={{12,0},{13,1},{14,2},{15,3},{0,4},{1,5},{2,6},{3,7},{4,8},{5,9},{6... | collective-permute-start | bytes 196616 | tf_op jit(solution)/shard_map/ppermute | solution.py:29
  84.6 5.8 %collective-permute-start.22 = (f32[16,1024]{1,0:T(8,128)S(1)}, f32[16,1024]{1,0:T(8,128)S(1)}, u32[]{:S(2)}, u32[]{:S(2)}) collective-permute-start(f32[16,1024]{1,0:T(8,128)S(1)} %get-tuple-element.89.refs_0_), channel_id=1, source_target_pairs={{8,0},{9,1},{10,2},{11,3},{12,4},{13,5},{14,6},{15,7},{0,8},{1,9},... | collective-permute-start | bytes 196616 | tf_op jit(solution)/shard_map/ppermute | solution.py:29
  87.2 4.3 %collective-permute-start.21 = (f32[16,1024]{1,0:T(8,128)S(1)}, f32[16,1024]{1,0:T(8,128)S(1)}, u32[]{:S(2)}, u32[]{:S(2)}) collective-permute-start(f32[16,1024]{1,0:T(8,128)S(1)} %get-tuple-element.89.refs_0_), channel_id=1, source_target_pairs={{4,0},{5,1},{6,2},{7,3},{8,4},{9,5},{10,6},{11,7},{12,8},{13,9},{1... | collective-permute-start | bytes 196616 | tf_op jit(solution)/shard_map/ppermute | solution.py:29
  91.6 8.6 %collective-permute-start.26 = (f32[16,1024]{1,0:T(8,128)S(1)}, f32[16,1024]{1,0:T(8,128)S(1)}, u32[]{:S(2)}, u32[]{:S(2)}) collective-permute-start(f32[16,1024]{1,0:T(8,128)S(1)} %merge.1.s0), channel_id=1, source_target_pairs={{66,0},{67,1},{64,2},{65,3},{70,4},{71,5},{68,6},{69,7},{74,8},{75... | collective-permute-start | bytes 196616 | tf_op jit(solution)/shard_map/ppermute | solution.py:43
  93.1 7.1 %collective-permute-start.25 = (f32[16,1024]{1,0:T(8,128)S(1)}, f32[16,1024]{1,0:T(8,128)S(1)}, u32[]{:S(2)}, u32[]{:S(2)}) collective-permute-start(f32[16,1024]{1,0:T(8,128)S(1)} %merge.1.s0), channel_id=1, source_target_pairs={{2,0},{3,1},{0,2},{1,3},{6,4},{7,5},{4,6},{5,7},{10,8},{11,9},{8,1... | collective-permute-start | bytes 196616 | tf_op jit(solution)/shard_map/ppermute | solution.py:43
  95.8 4.4 %collective-permute-start.24 = (f32[16,1024]{1,0:T(8,128)S(1)}, f32[16,1024]{1,0:T(8,128)S(1)}, u32[]{:S(2)}, u32[]{:S(2)}) collective-permute-start(f32[16,1024]{1,0:T(8,128)S(1)} %merge.1.s0), channel_id=1, source_target_pairs={{64,0},{65,1},{66,2},{67,3},{68,4},{69,5},{70,6},{71,7},{72,8},{73... | collective-permute-start | bytes 196616 | tf_op jit(solution)/shard_map/ppermute | solution.py:43
  103.2 2.9 %collective-permute-start.27 = (f32[384,768]{1,0:T(8,128)S(1)}, f32[384,768]{1,0:T(8,128)S(1)}, u32[]{:S(2)}, u32[]{:S(2)}) collective-permute-start(f32[384,768]{1,0:T(8,128)S(1)} %get-tuple-element.100), channel_id=1, source_target_pairs={{0,1},{1,0},{2,3},{3,2},{4,5},{5,4},{6,7},{7,6},{8,9},{9,8},{10,11... | collective-permute-start | bytes 3538952 | tf_op jit(solution)/shard_map/ppermute | solution.py:24
  106.3 6.4 %collective-permute-start.28 = (bf16[96,768]{1,0:T(8,128)(2,1)S(1)}, bf16[96,768]{1,0:T(8,128)(2,1)S(1)}, u32[]{:S(2)}, u32[]{:S(2)}) collective-permute-start(bf16[96,768]{1,0:T(8,128)(2,1)S(1)} %get-tuple-element.102), channel_id=1, source_target_pairs={{48,0},{13,1},{50,2},{15,3},{52,4},{1,5},{54,6},{3,7},{56,8},{5,9}... | collective-permute-start | bytes 442376 | tf_op jit(solution)/shard_map/ppermute | solution.py:54
  108.0 7.6 %collective-permute-start.29 = (bf16[96,768]{1,0:T(8,128)(2,1)S(1)}, bf16[96,768]{1,0:T(8,128)(2,1)S(1)}, u32[]{:S(2)}, u32[]{:S(2)}) collective-permute-start(bf16[96,768]{1,0:T(8,128)(2,1)S(1)} %get-tuple-element.103), channel_id=1, source_target_pairs={{32,0},{9,1},{34,2},{11,3},{36,4},{13,5},{38,6},{15,7},{40,8},{1,9... | collective-permute-start | bytes 442376 | tf_op jit(solution)/shard_map/ppermute | solution.py:54
  110.9 5.1 %collective-permute-start.30 = (bf16[96,768]{1,0:T(8,128)(2,1)S(1)}, bf16[96,768]{1,0:T(8,128)(2,1)S(1)}, u32[]{:S(2)}, u32[]{:S(2)}) collective-permute-start(bf16[96,768]{1,0:T(8,128)(2,1)S(1)} %get-tuple-element.104), channel_id=1, source_target_pairs={{16,0},{5,1},{18,2},{7,3},{20,4},{9,5},{22,6},{11,7},{24,8},{13,9}... | collective-permute-start | bytes 442376 | tf_op jit(solution)/shard_map/ppermute | solution.py:54
  116.1 6.4 %collective-permute-start.31 = (f32[24,768]{1,0:T(8,128)S(1)}, f32[24,768]{1,0:T(8,128)S(1)}, u32[]{:S(2)}, u32[]{:S(2)}) collective-permute-start(f32[24,768]{1,0:T(8,128)S(1)} %get-tuple-element.106), channel_id=1, source_target_pairs={{12,0},{49,1},{14,2},{51,3},{0,4},{53,5},{2,6},{55,7},{4,8},{57,9}... | collective-permute-start | bytes 221192 | tf_op jit(solution)/shard_map/ppermute | solution.py:54
  116.2 6.3 %collective-permute-start.32 = (f32[24,768]{1,0:T(8,128)S(1)}, f32[24,768]{1,0:T(8,128)S(1)}, u32[]{:S(2)}, u32[]{:S(2)}) collective-permute-start(f32[24,768]{1,0:T(8,128)S(1)} %get-tuple-element.107), channel_id=1, source_target_pairs={{8,0},{33,1},{10,2},{35,3},{12,4},{37,5},{14,6},{39,7},{0,8},{41,9... | collective-permute-start | bytes 221192 | tf_op jit(solution)/shard_map/ppermute | solution.py:54
  119.0 4.4 %collective-permute-start.33 = (f32[24,768]{1,0:T(8,128)S(1)}, f32[24,768]{1,0:T(8,128)S(1)}, u32[]{:S(2)}, u32[]{:S(2)}) collective-permute-start(f32[24,768]{1,0:T(8,128)S(1)} %get-tuple-element.108), channel_id=1, source_target_pairs={{4,0},{17,1},{6,2},{19,3},{8,4},{21,5},{10,6},{23,7},{12,8},{25,9}... | collective-permute-start | bytes 221192 | tf_op jit(solution)/shard_map/ppermute | solution.py:54
  123.4 5.1 %collective-permute-start.34 = (f32[6,768]{1,0:T(8,128)S(1)}, f32[6,768]{1,0:T(8,128)S(1)}, u32[]{:S(2)}, u32[]{:S(2)}) collective-permute-start(f32[6,768]{1,0:T(8,128)S(1)} %get-tuple-element.110), channel_id=1, source_target_pairs={{66,0},{67,1},{64,2},{65,3},{70,4},{71,5},{68,6},{69,7},{74,8},{75... | collective-permute-start | bytes 55304 | tf_op jit(solution)/shard_map/ppermute | solution.py:43
  125.0 5.3 %collective-permute-start.35 = (f32[6,768]{1,0:T(8,128)S(1)}, f32[6,768]{1,0:T(8,128)S(1)}, u32[]{:S(2)}, u32[]{:S(2)}) collective-permute-start(f32[6,768]{1,0:T(8,128)S(1)} %get-tuple-element.111), channel_id=1, source_target_pairs={{2,0},{3,1},{0,2},{1,3},{6,4},{7,5},{4,6},{5,7},{10,8},{11,9},{8,1... | collective-permute-start | bytes 55304 | tf_op jit(solution)/shard_map/ppermute | solution.py:43
  126.4 4.0 %collective-permute-start.36 = (f32[6,768]{1,0:T(8,128)S(1)}, f32[6,768]{1,0:T(8,128)S(1)}, u32[]{:S(2)}, u32[]{:S(2)}) collective-permute-start(f32[6,768]{1,0:T(8,128)S(1)} %get-tuple-element.112), channel_id=1, source_target_pairs={{64,0},{65,1},{66,2},{67,3},{68,4},{69,5},{70,6},{71,7},{72,8},{73... | collective-permute-start | bytes 55304 | tf_op jit(solution)/shard_map/ppermute | solution.py:43

commit v2 on v1

--- a/solution.py
+++ b/solution.py
@@ -317,13 +317,11 @@
     out[...] = total
 
 
-def turn_kernel(mixed, out):
-    width = out.shape[0]
-    rows = 128
-    lax.fori_loop(0, width // rows, lambda index, _: turn_rows(index * rows, rows, mixed, out), None)
-
-
-def turn_rows(low, rows, mixed, out):
+def choose_kernel(out):
+    lax.fori_loop(0, out.shape[0] // 128, lambda index, _: choose_rows(index * 128, 128, out), None)
+
+
+def choose_rows(low, rows, out):
     width = out.shape[0]
     place = low + lax.broadcasted_iota(jnp.int32, (rows, 1), 0)
     dp, ctx = here()
@@ -335,9 +333,19 @@
     z = ((ctx & 2) + (dp >> 2) + place // each % 4) & 3
     block = ((z & 1) * 4 + y) * 16 + x * 4 + (z >> 1) * 2 + core
     chosen = block * each + place % each == lax.broadcasted_iota(jnp.int32, (rows, width), 1)
-    chosen = jnp.where(chosen, 1.0, 0.0).astype(jnp.bfloat16)
-    here_rows = pl.ds(pl.multiple_of(low, rows), rows)
-    out[here_rows, :] = jnp.dot(chosen, mixed[...], preferred_element_type=jnp.float32).astype(jnp.bfloat16)
+    out[pl.ds(pl.multiple_of(low, rows), rows), :] = jnp.where(chosen, 1.0, 0.0).astype(jnp.bfloat16)
+
+
+def turn_kernel(chosen, mixed, own, other):
+    half, rows = own.shape[0], 192
+
+    def some(index, _):
+        for out, low in ((own, 0), (other, half)):
+            source = chosen[pl.ds(pl.multiple_of(low + index * rows, 64), rows), :]
+            product = jnp.dot(source, mixed[...], preferred_element_type=jnp.float32)
+            out[pl.ds(pl.multiple_of(index * rows, 64), rows), :] = product.astype(jnp.bfloat16)
+
+    lax.fori_loop(0, half // rows, some, None)
 
 
 def norm_kernel(s0, s1, s2, s3, emb_out, rinv_out, target_out):
@@ -432,12 +440,12 @@
 
 
 def grad_kernel(
-    lengths, s0, s1, s2, s3, emb, rinv, everyone, target, product, stats, gain, normed, rstd, turned,
-    send_out, d_summed, loss_out,
+    lengths, s0, s1, s2, s3, emb, rinv, everyone, target, scored, stats, gain, normed, rstd, turned, *refs,
 ):
+    normed_other, rstd_other, turned_other, loss_out, *outs, rows_dy, rows_level, d_summed, product = refs
     docs, tb, width = normed.shape
     all_docs, group = everyone.shape[0], emb.shape[0]
-    dp, _ = here()
+    dp, ctx = here()
     mine = lambda a: jnp.where(dp >= 4, a[docs:group], a[0:docs])
     own, others = mine(emb), everyone[...]
     now = merge(group, width, [s[...] for s in (s0, s1, s2, s3)])
@@ -450,37 +458,45 @@
     first = (dp & 3) * group + (dp >> 2) * docs
     same = column == lax.broadcasted_iota(jnp.int32, (docs, all_docs), 0) + first
     lse = jnp.sum(jnp.where(same, lse_row, 0.0), axis=1, keepdims=True)
-    scores = mine(product)
+    scores = mine(scored)
     g_batch = jnp.where(same, 0.0, jnp.exp(scores - lse) + jnp.exp(scores - lse_row)) / all_docs
     shares = mine(now)
     mix = shares[:, 0:width] * jnp.exp(shares[:, width + 128 : width + 129] - lse)
     from_batch = jnp.dot(g_batch, others, precision=HIGHEST, preferred_element_type=jnp.float32)
     d_emb = ((mix - mine(target)) / all_docs + from_batch) / TAU
     d_pooled = (d_emb - own * jnp.sum(own * d_emb, axis=1, keepdims=True)) * mine(rinv)[:, 0:1]
+    row = lax.broadcasted_iota(jnp.int32, (docs, width), 0)
+    count = jnp.ones((docs, width), jnp.float32)
     for doc in range(docs):
-        dy = d_pooled[doc : doc + 1] / lengths[doc].astype(jnp.float32) * gain[...].reshape(1, width)
-        level = dy - jnp.mean(dy, axis=1, keepdims=True)
-        unit = normed[doc].astype(jnp.float32)
-        along = jnp.mean(unit * dy, axis=1, keepdims=True)
-        keep = lax.axis_index("ctx") * tb + lax.broadcasted_iota(jnp.int32, (tb, 1), 0) < lengths[doc]
-        scale = jnp.where(keep, rstd[doc, :, 0:1], 0.0)
-        d_summed[doc * tb : (doc + 1) * tb, :] = (scale * (level - unit * along)).astype(jnp.bfloat16)
-    product_rows(turned, width // 2, d_summed, send_out)
-
-
-def product_rows(turned, low, d_summed, out):
-    rows = 128
-
-    def some(index, _):
-        source = pl.ds(pl.multiple_of(low + index * rows, rows), rows)
-        here_rows = pl.ds(pl.multiple_of(index * rows, rows), rows)
-        out[here_rows, :] = jnp.dot(turned[source, :], d_summed[...], preferred_element_type=jnp.float32)
-
-    lax.fori_loop(0, out.shape[0] // rows, some, None)
-
-
-def keep_kernel(turned, d_summed, out):
-    product_rows(turned, 0, d_summed, out)
+        count = jnp.where(row == doc, lengths[doc].astype(jnp.float32), count)
+    dy = d_pooled / count * gain[...].reshape(1, width)
+    rows_dy[0:docs, :] = dy
+    rows_level[0:docs, :] = dy - jnp.mean(dy, axis=1, keepdims=True)
+
+    def some(doc, _):
+        dy, level = rows_dy[pl.ds(doc, 1), :], rows_level[pl.ds(doc, 1), :]
+        for index, (units, scales) in enumerate(((normed, rstd), (normed_other, rstd_other))):
+            unit = units[doc].astype(jnp.float32)
+            along = jnp.mean(unit * dy, axis=1, keepdims=True)
+            start = (ctx ^ index) * tb
+            keep = start + lax.broadcasted_iota(jnp.int32, (tb, 1), 0) < lengths[doc]
+            scale = jnp.where(keep, scales[doc, :, 0:1], 0.0)
+            place = pl.ds(pl.multiple_of((index * docs + doc) * tb, tb), tb)
+            d_summed[place, :] = (scale * (level - unit * along)).astype(jnp.bfloat16)
+
+    lax.fori_loop(0, docs, some, None)
+    half = docs * tb
+    rows = 192
+
+    def block(index, _):
+        place = pl.ds(pl.multiple_of(index * rows, 64), rows)
+        total = jnp.dot(turned[place, :], d_summed[0:half], preferred_element_type=jnp.float32)
+        product[place, :] = total + jnp.dot(turned_other[place, :], d_summed[half:], preferred_element_type=jnp.float32)
+
+    lax.fori_loop(0, turned.shape[0] // rows, block, None)
+    rows = outs[0].shape[0]
+    for index, out in enumerate(outs):
+        out[...] = product[index * rows : (index + 1) * rows, :].astype(out.dtype)
 
 
 def sum_kernel(count, *refs):
@@ -521,36 +537,41 @@
         moved=4 * 2**20,
         name="near",
     )(near, w_qkv, w_v_turned)
+    chosen = call(choose_kernel, bf16(width, width), [], VMEM, limit=4, name="choose")()
+    early, chosen = lax.optimization_barrier((early, chosen))
     gain = ln_gain
     fixed = (lengths, tokens, near_k), (near_v, qk, v_turned, w_qkv, w_v_turned, w_out, gain)
     *done, pool = attend(0, None, *fixed[0], early, *fixed[1])
-    pool, after, *tables = lax.optimization_barrier((pool, positive, *tables))
-    others = [swap(table, "ctx", 1) for table in tables]
+    pool, after = lax.optimization_barrier((pool, positive))
     target = call(
         functools.partial(target_kernel, docs), f32(2 * docs, width), [SMEM] + [VMEM] * 4, VMEM, name="target"
     )(after, *tables)
-    middle, late, target, *others = lax.optimization_barrier((middle, late, target, *others))
+    middle, late, target = lax.optimization_barrier((middle, late, target))
     late = fetch(late)
     done = attend(1, [*done, pool], *fixed[0], middle, *fixed[1])
     done = attend(3, done, *fixed[0], late, *fixed[1])
     hidden, mixed, normed, rstd, pool = done
 
-    turned = call(
+    half = width // 2
+    turned, leaving = call(
         turn_kernel,
-        bf16(width, docs * tb),
-        [VMEM],
-        VMEM,
+        (bf16(half, docs * tb),) * 2,
+        [VMEM, VMEM],
+        (VMEM,) * 2,
         flops=2 * docs * tb * width * width,
         moved=4 * 2**20,
         name="turn",
-    )(mixed)
+    )(chosen, mixed)
 
     group = 2 * docs
     sums = call(stack_kernel, f32(docs + group, width), [VMEM, VMEM], VMEM, limit=4, name="stack")(
         pool, target
     )
     sums = add([sums, swap(sums, "ctx", 1)])
+    sums, *tables = lax.optimization_barrier((sums, *tables))
+    others = [swap(table, "ctx", 1) for table in tables]
     sums = add(around(sums, from_x))
+    sums, leaving = lax.optimization_barrier((sums, leaving))
     emb, rinv, target = call(
         norm_kernel,
         (f32(group, width), f32(group, 128), f32(group, width)),
@@ -559,6 +580,8 @@
         limit=4,
         name="norm",
     )(*around(sums, from_z))
+    emb, *others = lax.optimization_barrier((emb, *others))
+    swapped = [swap(value, "ctx", 1) for value in (normed, rstd, leaving)]
     embs = around(emb, from_y)
     everyone, state = call(
         functools.partial(score_kernel, docs),
@@ -577,29 +600,27 @@
         limit=4,
         name="batch",
     )(emb, everyone)
+    state, *swapped = lax.optimization_barrier((state, *swapped))
     state = merged(group, width, around(state, from_x))
-    half = width // 2
-    send, d_summed, loss = call(
+    piece = (half // 4, width)
+    loss, keep, *sends = call(
         grad_kernel,
-        (f32(half, width), bf16(docs * tb, width), f32(8, 128)),
-        [SMEM] + [VMEM] * 14,
-        (VMEM,) * 3,
-        flops=docs * tb * width * width,
+        (f32(8, 128), f32(*piece)) + (bf16(*piece),) * 3,
+        [SMEM] + [VMEM] * 17,
+        (VMEM,) * 5,
+        flops=2 * docs * tb * width * width,
         moved=8 * 2**20,
+        scratch_shapes=[
+            pltpu.VMEM((8, width), jnp.float32),
+            pltpu.VMEM((8, width), jnp.float32),
+            pltpu.VMEM((2 * docs * tb, width), jnp.bfloat16),
+            pltpu.VMEM((half, width), jnp.float32),
+        ],
         name="grad",
     )(
-        lengths, *around(state, from_z), emb, rinv, everyone, target, product, stats, gain, normed, rstd, turned,
+        lengths, *around(state, from_z), emb, rinv, everyone, target, product, stats, gain,
+        normed, rstd, turned, *swapped,
     )
-    keep = call(
-        keep_kernel,
-        f32(half, width),
-        [VMEM, VMEM],
-        VMEM,
-        flops=docs * tb * width * width,
-        moved=2**20,
-        name="keep",
-    )(turned, d_summed)
-    keep, *sends = sum_and_split([keep, swap(send, "ctx", 1)], jnp.bfloat16)
     got = [from_plane(piece, -(k + 1), False) for k, piece in enumerate(sends)]
     keep, *sends = sum_and_split([keep] + got, jnp.float32)
     got = [from_plane(piece, -(k + 1), True) for k, piece in enumerate(sends)]

time: 131 us -> 150 us (1.15)
  waiting for transfers between devices: 25.9 us -> 41.9 us
  starting transfers between devices: 56.5 us -> 58.6 us
    ppermute x9, waiting for transfers between devices: 4.98 us -> 14.3 us  [from_z(): return lax.ppermute(value, ('dp', 'ctx'), pairs)]
    ppermute x6, waiting for transfers between devices: 2 us -> 6.66 us  [from_y(): lax.ppermute(value, 'dp', [(d & 4 | d + k & 3, d) for d in range(lax.axis...]
    ppermute x7 -> x9, starting transfers between devices: 5.87 us -> 10.1 us  [swap(): lax.ppermute(value, axis, [(i, i ^ bits) for i in range(lax.axis_size(axi...]
    ppermute x9, starting transfers between devices: 12.9 us -> 9.67 us  [from_z(): return lax.ppermute(value, ('dp', 'ctx'), pairs)]
    ppermute x6, waiting for transfers between devices: 8.09 us -> 10.4 us  [from_plane(): return lax.ppermute(value, ('dp', 'ctx'), pairs)]
    ppermute x6, waiting for transfers between devices: 7.29 us -> 5.08 us  [from_x(): lax.ppermute(value, 'ctx', [((c + 4 * k) % size, c) for c in range(size)])]
    ppermute x6, starting transfers between devices: 7.88 us -> 10 us  [from_x(): lax.ppermute(value, 'ctx', [((c + 4 * k) % size, c) for c in range(size)])]
    ppermute x7 -> x9, waiting for transfers between devices: 3.54 us -> 5.14 us  [swap(): lax.ppermute(value, axis, [(i, i ^ bits) for i in range(lax.axis_size(axi...]
  transfers between devices with their start and end apart: 37 -> 39, of which waited for: 22 -> 23; matrix products, arithmetic and copies ran while one was open for 1% -> 1% of each run, Pallas kernels for 26% -> 23%
where the time goes in v2:
time: 150 us; the launch traced here: 149 us
  starting transfers between devices  58.6 us (39%)
  Pallas kernels  46.1 us (31%)
  waiting for transfers between devices  41.9 us (28%)
  local copies, waits for them, and re-layouts  1.9 us (1%)
    pallas_call x3, Pallas kernels, attend(): call(functools.partial(attend_kernel, first), out_shape, in_specs, out_sp...  23.9 us
    ppermute x9, waiting for transfers between devices, from_z(): return lax.ppermute(value, ('dp', 'ctx'), pairs)  14.3 us
    ppermute x3, starting transfers between devices, shards(): fetch = lambda part: lax.ppermute(part, 'ctx', ring)  11.7 us
    ppermute x6, waiting for transfers between devices, from_plane(): return lax.ppermute(value, ('dp', 'ctx'), pairs)  10.4 us
    ppermute x9, starting transfers between devices, swap(): lax.ppermute(value, axis, [(i, i ^ bits) for i in range(lax.axis_size(axi...  10.1 us
    ppermute x6, starting transfers between devices, from_x(): lax.ppermute(value, 'ctx', [((c + 4 * k) % size, c) for c in range(size)])  10 us
    ppermute x6, starting transfers between devices, from_y(): lax.ppermute(value, 'dp', [(d & 4 | d + k & 3, d) for d in range(lax.axis...  9.76 us
    ppermute x9, starting transfers between devices, from_z(): return lax.ppermute(value, ('dp', 'ctx'), pairs)  9.67 us
  transfers between devices with their start and end apart: 39, of which 23 were waited for; matrix products, arithmetic and copies ran while one was open for 1% of the time, Pallas kernels for 23%

profile of v2, /device:TPU:0, one launch (start us, length us, event | category | flops | bytes accessed | tf_op | source)
XLA Modules:
  0.0 149.5 jit_solution(6692285593317887954)
XLA Ops:
  0.7 1.3 slice.12
  2.0 6.2 %collective-permute-start.1 = (bf16[2,256,768]{2,1,0:T(8,128)(2,1)S(1)}, bf16[2,256,768]{2,1,0:T(8,128)(2,1)S(1)}, u32[]{:S(2)}, u32[]{:S(2)}) collective-permute-start(bf16[2,256,768]{2,1,0:T(8,128)(2,1)S(1)} %slice.12), channel_id=1, source_target_pairs={{0,15},{1,2},{2,1},{3,4},{4,3},{5,6},{6,5},{7,8},{8,7},{9,10},{10,... | collective-permute-start | bytes 2359304 | tf_op jit(solution)/shard_map/ppermute | solution.py:526
  8.4 1.6 %collective-permute-start.5 = (bf16[128,768]{1,0:T(8,128)(2,1)S(1)}, bf16[128,768]{1,0:T(8,128)(2,1)S(1)}, u32[]{:S(2)}, u32[]{:S(2)}) collective-permute-start(bf16[128,768]{1,0:T(8,128)(2,1)S(1)} %copy-done.4), channel_id=1, source_target_pairs={{48,0},{0,16},{16,32},{32,48},{112,64},{64,80},{80,96},{96,112},{4... | collective-permute-start | bytes 589832 | tf_op jit(solution)/shard_map/ppermute | solution.py:33
  10.1 2.9 %collective-permute-start.4 = (bf16[128,768]{1,0:T(8,128)(2,1)S(1)}, bf16[128,768]{1,0:T(8,128)(2,1)S(1)}, u32[]{:S(2)}, u32[]{:S(2)}) collective-permute-start(bf16[128,768]{1,0:T(8,128)(2,1)S(1)} %copy-done.4), channel_id=1, source_target_pairs={{32,0},{48,16},{0,32},{16,48},{96,64},{112,80},{64,96},{80,112},{3... | collective-permute-start | bytes 589832 | tf_op jit(solution)/shard_map/ppermute | solution.py:33
  13.0 1.7 %choose.1.chosen = bf16[768,768]{1,0:T(8,128)(2,1)S(1)} custom-call(), custom_call_target="tpu_custom_call" | custom-call | tf_op jit(solution)/shard_map/choose/pallas_call | solution.py:540
  14.7 7.2 %prepare.1 = (bf16[4,256,1536]{2,1,0:T(8,128)(2,1)S(1)}, bf16[768,1024]{1,0:T(8,128)(2,1)S(1)}, bf16[768,768]{1,0:T(8,128)(2,1)S(1)}) custom-call(bf16[4,256,768]{2,1,0:T(8,128)(2,1)} %refs_1_.5, bf16[768,2304]{1,0:T(8,128)(2,1)} %refs_7_.5), custom_call_target="tpu_custom_call" | custom-call | flops 3623878656 | bytes 11534336 | tf_op jit(solution)/shard_map/prepare/pallas_call | solution.py:253
  22.3 3.0 %collective-permute-start.3 = (bf16[128,768]{1,0:T(8,128)(2,1)S(1)}, bf16[128,768]{1,0:T(8,128)(2,1)S(1)}, u32[]{:S(2)}, u32[]{:S(2)}) collective-permute-start(bf16[128,768]{1,0:T(8,128)(2,1)S(1)} %copy-done.4), channel_id=1, source_target_pairs={{16,0},{32,16},{48,32},{0,48},{80,64},{96,80},{112,96},{64,112},{1... | collective-permute-start | bytes 589832 | tf_op jit(solution)/shard_map/ppermute | solution.py:33
  25.3 3.1 %near.1 = (bf16[4,256,768]{2,1,0:T(8,128)(2,1)S(1)}, bf16[768,1024]{1,0:T(8,128)(2,1)S(1)}) custom-call(bf16[4,256,768]{2,1,0:T(8,128)(2,1)S(1)} %collective-permute-done.near, bf16[768,2304]{1,0:T(8,128)(2,1)S(1)} %copy-done, bf16[768,768]{1,0:T(8,128)(2,1)S(1)} %get-tuple-element.68.w_v_turned.refs_8_), custom_call_target="tpu_custom_call" | custom-call | flops 2415919104 | bytes 4194304 | tf_op jit(solution)/shard_map/near/pallas_call | solution.py:531
  28.5 6.1 %attend.3 = (bf16[4,256,768]{2,1,0:T(8,128)(2,1)}, bf16[768,1024]{1,0:T(8,128)(2,1)S(1)}, bf16[4,256,768]{2,1,0:T(8,128)(2,1)S(1)}, f32[4,256,128]{2,1,0:T(8,128)S(1)}, f32[4,1,768]{2,1,0:T(1,128)S(1)}) custom-call(s32[4]{0:T(128)S(1)} %copy-done.6, bf16[4,256,768]{2,1,0:T(8,128)(2,1)S(1)} %copy-done.2, bf16[4,256,768]{2,1,0:T(8,128)(2,1)S(1)} %get-tuple-element.69.refs_2_, ...), custom_call_target="tpu_custom_call" | custom-call | flops 1509949440 | bytes 4194304 | tf_op jit(solution)/shard_map/attend/pallas_call | solution.py:205
  35.4 5.4 %collective-permute-start.6 = (bf16[1,256,768]{2,1,0:T(8,128)(2,1)S(1)}, bf16[1,256,768]{2,1,0:T(8,128)(2,1)S(1)}, u32[]{:S(2)}, u32[]{:S(2)}) collective-permute-start(bf16[1,256,768]{2,1,0:T(8,128)(2,1)S(1)} %get-tuple-element.76), channel_id=1, source_target_pairs={{0,15},{1,2},{2,1},{3,4},{4,3},{5,6},{6,5},{7,8},{8,7},{9,10},{10,... | collective-permute-start | bytes 1179656 | tf_op jit(solution)/shard_map/ppermute | solution.py:526
  40.7 11.7 %attend.4 = (bf16[4,256,768]{2,1,0:T(8,128)(2,1)}, bf16[768,1024]{1,0:T(8,128)(2,1)S(1)}, bf16[4,256,768]{2,1,0:T(8,128)(2,1)S(1)}, f32[4,256,128]{2,1,0:T(8,128)S(1)}, f32[4,1,768]{2,1,0:T(1,128)S(1)}) custom-call(s32[4]{0:T(128)S(1)} %copy-done.6, ...), custom_call_target="tpu_custom_call", output_to_operand_aliasing={{0}: (11, {}), {1}: (12, {}), {2}: (13, {}), {3}: (14, {}),... | custom-call | flops 3019898880 | bytes 4194304 | tf_op jit(solution)/shard_map/attend/pallas_call | solution.py:205
  52.5 6.1 %attend.5 = (bf16[4,256,768]{2,1,0:T(8,128)(2,1)}, bf16[768,1024]{1,0:T(8,128)(2,1)S(1)}, bf16[4,256,768]{2,1,0:T(8,128)(2,1)S(1)}, f32[4,256,128]{2,1,0:T(8,128)S(1)}, f32[4,1,768]{2,1,0:T(1,128)S(1)}) custom-call(s32[4]{0:T(128)S(1)} %copy-done.6, ...), custom_call_target="tpu_custom_call", output_to_operand_aliasing={{0}: (11, {}), {1}: (12, {}), {2}: (13, {}), {3}: (14, {}),... | custom-call | flops 1509949440 | bytes 4194304 | tf_op jit(solution)/shard_map/attend/pallas_call | solution.py:205
  58.6 8.7 %collective-permute-start.21 = (bf16[4,256,768]{2,1,0:T(8,128)(2,1)S(1)}, bf16[4,256,768]{2,1,0:T(8,128)(2,1)S(1)}, u32[]{:S(2)}, u32[]{:S(2)}) collective-permute-start(bf16[4,256,768]{2,1,0:T(8,128)(2,1)S(1)} %get-tuple-element.107.normed), channel_id=1, source_target_pairs={{0,1},{1,0},{2,3},{3,2},{4,5},{5,4},{6,7},{7,6},{8,9},{9,8},{10,11... | collective-permute-start | bytes 4718600 | tf_op jit(solution)/shard_map/ppermute | solution.py:24
  67.4 3.0 %collective-permute-done.7.refs_1_ = f32[12,768]{1,0:T(8,128)S(1)} collective-permute-done((f32[12,768]{1,0:T(8,128)S(1)}, f32[12,768]{1,0:T(8,128)S(1)}, u32[]{:S(2)}, u32[]{:S(2)}) %collective-permute-start.7) | collective-permute-done | bytes 36896 | tf_op jit(solution)/shard_map/ppermute | solution.py:24
  70.4 1.5 %collective-permute-start.10 = (f32[12,768]{1,0:T(8,128)S(1)}, f32[12,768]{1,0:T(8,128)S(1)}, u32[]{:S(2)}, u32[]{:S(2)}) collective-permute-start(f32[12,768]{1,0:T(8,128)S(1)} %add.3.refs_0_), channel_id=1, source_target_pairs={{12,0},{13,1},{14,2},{15,3},{0,4},{1,5},{2,6},{3,7},{4,8},{5,9},{6... | collective-permute-start | bytes 110600 | tf_op jit(solution)/shard_map/ppermute | solution.py:29
  71.9 2.7 %collective-permute-start.9 = (f32[12,768]{1,0:T(8,128)S(1)}, f32[12,768]{1,0:T(8,128)S(1)}, u32[]{:S(2)}, u32[]{:S(2)}) collective-permute-start(f32[12,768]{1,0:T(8,128)S(1)} %add.3.refs_0_), channel_id=1, source_target_pairs={{8,0},{9,1},{10,2},{11,3},{12,4},{13,5},{14,6},{15,7},{0,8},{1,9},... | collective-permute-start | bytes 110600 | tf_op jit(solution)/shard_map/ppermute | solution.py:29
  74.6 1.4 collective-permute-start.8
  76.1 1.6 %turn.1 = (bf16[384,1024]{1,0:T(8,128)(2,1)S(1)}, bf16[384,1024]{1,0:T(8,128)(2,1)S(1)}) custom-call(bf16[768,768]{1,0:T(8,128)(2,1)S(1)} %choose.1.chosen, bf16[768,1024]{1,0:T(8,128)(2,1)S(1)} %get-tuple-element.93.mixed), custom_call_target="tpu_custom_call" | custom-call | flops 1207959552 | bytes 4194304 | tf_op jit(solution)/shard_map/turn/pallas_call | solution.py:556
  77.7 1.0 collective-permute-done.8.refs_1_
  79.3 1.0 collective-permute-start.13
  80.3 1.2 collective-permute-start.12
  81.5 3.6 %collective-permute-done.13.s3 = f32[12,768]{1,0:T(8,128)S(1)} collective-permute-done((f32[12,768]{1,0:T(8,128)S(1)}, f32[12,768]{1,0:T(8,128)S(1)}, u32[]{:S(2)}, u32[]{:S(2)}) %collective-permute-start.13) | collective-permute-done | bytes 36896 | tf_op jit(solution)/shard_map/ppermute | solution.py:43
  85.9 3.3 %collective-permute-done.11.s1 = f32[12,768]{1,0:T(8,128)S(1)} collective-permute-done((f32[12,768]{1,0:T(8,128)S(1)}, f32[12,768]{1,0:T(8,128)S(1)}, u32[]{:S(2)}, u32[]{:S(2)}) %collective-permute-start.11) | collective-permute-done | bytes 36896 | tf_op jit(solution)/shard_map/ppermute | solution.py:43
  89.7 0.9 collective-permute-done.15.refs_5_
  90.9 1.2 collective-permute-done.17.refs_7_
  92.1 2.2 %collective-permute-start.19 = (f32[8,768]{1,0:T(8,128)S(1)}, f32[8,768]{1,0:T(8,128)S(1)}, u32[]{:S(2)}, u32[]{:S(2)}) collective-permute-start(f32[8,768]{1,0:T(8,128)S(1)} %get-tuple-element.101.e0.emb), channel_id=1, source_target_pairs={{32,0},{48,16},{0,32},{16,48},{96,64},{112,80},{64,96},{80,112},{3... | collective-permute-start | bytes 73736 | tf_op jit(solution)/shard_map/ppermute | solution.py:33
  94.3 2.8 %collective-permute-done.20.e3 = f32[8,768]{1,0:T(8,128)S(1)} collective-permute-done((f32[8,768]{1,0:T(8,128)S(1)}, f32[8,768]{1,0:T(8,128)S(1)}, u32[]{:S(2)}, u32[]{:S(2)}) %collective-permute-start.20) | collective-permute-done | bytes 24608 | tf_op jit(solution)/shard_map/ppermute | solution.py:33
  97.4 3.5 %collective-permute-done.18.e1 = f32[8,768]{1,0:T(8,128)S(1)} collective-permute-done((f32[8,768]{1,0:T(8,128)S(1)}, f32[8,768]{1,0:T(8,128)S(1)}, u32[]{:S(2)}, u32[]{:S(2)}) %collective-permute-start.18) | collective-permute-done | bytes 24608 | tf_op jit(solution)/shard_map/ppermute | solution.py:33
  101.0 1.7 %score.1 = (f32[32,768]{1,0:T(8,128)S(1)}, f32[16,1024]{1,0:T(8,128)S(1)}) custom-call(s32[32]{0:T(128)S(1)} %copy-done.7, f32[8,768]{1,0:T(8,128)S(1)} %get-tuple-element.101.e0.emb, f32[8,768]{1,0:T(8,128)S(1)} %collective-permute-done.18.e1, f32[8,768]{1,0:T(8,128)S(1)} %collective-permute-done.19.e2, f32[8,768]{1,0:T(8,128)S(1)} %collective-permute-done.20.e3, ...), custom_call_target="tpu_custom_call" | custom-call | bytes 2097152 | tf_op jit(solution)/shard_map/score/pallas_call | solution.py:586
  103.3 3.6 %collective-permute-start.25 = (f32[16,1024]{1,0:T(8,128)S(1)}, f32[16,1024]{1,0:T(8,128)S(1)}, u32[]{:S(2)}, u32[]{:S(2)}) collective-permute-start(f32[16,1024]{1,0:T(8,128)S(1)} %get-tuple-element.110.refs_0_), channel_id=1, source_target_pairs={{8,0},{9,1},{10,2},{11,3},{12,4},{13,5},{14,6},{15,7},{0,8},{1,9},... | collective-permute-start | bytes 196616 | tf_op jit(solution)/shard_map/ppermute | solution.py:29
  107.1 1.2 collective-permute-done.26.refs_3_
  108.3 1.6 %collective-permute-done.25.refs_2_ = f32[16,1024]{1,0:T(8,128)S(1)} collective-permute-done((f32[16,1024]{1,0:T(8,128)S(1)}, f32[16,1024]{1,0:T(8,128)S(1)}, u32[]{:S(2)}, u32[]{:S(2)}) %collective-permute-start.25) | collective-permute-done | bytes 65568 | tf_op jit(solution)/shard_map/ppermute | solution.py:29
  109.9 1.3 collective-permute-done.24.refs_1_
  111.4 2.7 %collective-permute-start.28 = (f32[16,1024]{1,0:T(8,128)S(1)}, f32[16,1024]{1,0:T(8,128)S(1)}, u32[]{:S(2)}, u32[]{:S(2)}) collective-permute-start(f32[16,1024]{1,0:T(8,128)S(1)} %merge.1.s0), channel_id=1, source_target_pairs={{2,0},{3,1},{0,2},{1,3},{6,4},{7,5},{4,6},{5,7},{10,8},{11,9},{8,1... | collective-permute-start | bytes 196616 | tf_op jit(solution)/shard_map/ppermute | solution.py:43
  114.9 2.6 %collective-permute-done.29.s3 = f32[16,1024]{1,0:T(8,128)S(1)} collective-permute-done((f32[16,1024]{1,0:T(8,128)S(1)}, f32[16,1024]{1,0:T(8,128)S(1)}, u32[]{:S(2)}, u32[]{:S(2)}) %collective-permute-start.29) | collective-permute-done | bytes 65568 | tf_op jit(solution)/shard_map/ppermute | solution.py:43
  117.6 0.9 collective-permute-done.27.s1
  118.4 4.8 %grad.1 = (f32[8,128]{1,0:T(8,128)S(1)}, f32[96,768]{1,0:T(8,128)S(1)}, bf16[96,768]{1,0:T(8,128)(2,1)S(1)}, bf16[96,768]{1,0:T(8,128)(2,1)S(1)}, bf16[96,768]{1,0:T(8,128)(2,1)S(1)}) custom-call(s32[4]{0:T(128)S(1)} %copy-done.6, f32[16,1024]{1,0:T(8,128)S(1)} %merge.1.s0, f32[16,1024]{1,0:T(8,128)S(1)} %collective-permute-done.27.s1, ...), custom_call_target="tpu_custom_call" | custom-call | flops 1207959552 | bytes 8388608 | tf_op jit(solution)/shard_map/grad/pallas_call | solution.py:606
  123.3 2.7 %collective-permute-start.31 = (bf16[96,768]{1,0:T(8,128)(2,1)S(1)}, bf16[96,768]{1,0:T(8,128)(2,1)S(1)}, u32[]{:S(2)}, u32[]{:S(2)}) collective-permute-start(bf16[96,768]{1,0:T(8,128)(2,1)S(1)} %get-tuple-element.123), channel_id=1, source_target_pairs={{32,0},{9,1},{34,2},{11,3},{36,4},{13,5},{38,6},{15,7},{40,8},{1,9... | collective-permute-start | bytes 442376 | tf_op jit(solution)/shard_map/ppermute | solution.py:54
  126.5 5.9 %collective-permute-done.30.refs_1_ = bf16[96,768]{1,0:T(8,128)(2,1)S(1)} collective-permute-done((bf16[96,768]{1,0:T(8,128)(2,1)S(1)}, bf16[96,768]{1,0:T(8,128)(2,1)S(1)}, u32[]{:S(2)}, u32[]{:S(2)}) %collective-permute-start.30) | collective-permute-done | bytes 147488 | tf_op jit(solution)/shard_map/ppermute | solution.py:54
  132.4 1.3 collective-permute-done.32.refs_3_
  133.9 2.1 %collective-permute-start.34 = (f32[24,768]{1,0:T(8,128)S(1)}, f32[24,768]{1,0:T(8,128)S(1)}, u32[]{:S(2)}, u32[]{:S(2)}) collective-permute-start(f32[24,768]{1,0:T(8,128)S(1)} %get-tuple-element.127), channel_id=1, source_target_pairs={{8,0},{33,1},{10,2},{35,3},{12,4},{37,5},{14,6},{39,7},{0,8},{41,9... | collective-permute-start | bytes 221192 | tf_op jit(solution)/shard_map/ppermute | solution.py:54
  136.0 1.8 %collective-permute-start.35 = (f32[24,768]{1,0:T(8,128)S(1)}, f32[24,768]{1,0:T(8,128)S(1)}, u32[]{:S(2)}, u32[]{:S(2)}) collective-permute-start(f32[24,768]{1,0:T(8,128)S(1)} %get-tuple-element.128), channel_id=1, source_target_pairs={{4,0},{17,1},{6,2},{19,3},{8,4},{21,5},{10,6},{23,7},{12,8},{25,9}... | collective-permute-start | bytes 221192 | tf_op jit(solution)/shard_map/ppermute | solution.py:54
  137.8 2.4 %collective-permute-done.33.refs_1_ = f32[24,768]{1,0:T(8,128)S(1)} collective-permute-done((f32[24,768]{1,0:T(8,128)S(1)}, f32[24,768]{1,0:T(8,128)S(1)}, u32[]{:S(2)}, u32[]{:S(2)}) %collective-permute-start.33) | collective-permute-done | bytes 73760 | tf_op jit(solution)/shard_map/ppermute | solution.py:54
  140.2 0.9 collective-permute-done.35.refs_3_
  141.1 1.4 collective-permute-start.36
  142.5 2.5 %collective-permute-start.37 = (f32[6,768]{1,0:T(8,128)S(1)}, f32[6,768]{1,0:T(8,128)S(1)}, u32[]{:S(2)}, u32[]{:S(2)}) collective-permute-start(f32[6,768]{1,0:T(8,128)S(1)} %get-tuple-element.131), channel_id=1, source_target_pairs={{2,0},{3,1},{0,2},{1,3},{6,4},{7,5},{4,6},{5,7},{10,8},{11,9},{8,1... | collective-permute-start | bytes 55304 | tf_op jit(solution)/shard_map/ppermute | solution.py:43
  146.2 1.6 %collective-permute-done.37.refs_2_ = f32[6,768]{1,0:T(8,128)S(1)} collective-permute-done((f32[6,768]{1,0:T(8,128)S(1)}, f32[6,768]{1,0:T(8,128)S(1)}, u32[]{:S(2)}, u32[]{:S(2)}) %collective-permute-start.37) | collective-permute-done | bytes 18464 | tf_op jit(solution)/shard_map/ppermute | solution.py:43
  147.8 1.0 collective-permute-done.38.refs_3_
  (68 shorter events, 8.4 us)
Async XLA Ops:
  0.6 7.6 %copy-start.1 = (bf16[4,256,768]{2,1,0:T(8,128)(2,1)S(1)}, bf16[4,256,768]{2,1,0:T(8,128)(2,1)}, u32[]{:S(2)}) copy-start(bf16[4,256,768]{2,1,0:T(8,128)(2,1)} %refs_1_.5) | copy-start | bytes 4718596
  0.6 7.8 %copy-start.4 = (bf16[128,768]{1,0:T(8,128)(2,1)S(1)}, bf16[128,768]{1,0:T(8,128)(2,1)}, u32[]{:S(2)}) copy-start(bf16[128,768]{1,0:T(8,128)(2,1)} %refs_0_.8) | copy-start | bytes 589828
  0.7 24.6 %collective-permute-start = (bf16[4,256,768]{2,1,0:T(8,128)(2,1)}, bf16[4,256,768]{2,1,0:T(8,128)(2,1)S(1)}, u32[]{:S(2)}, u32[]{:S(2)}) collective-permute-start(bf16[4,256,768]{2,1,0:T(8,128)(2,1)} %refs_1_.5), channel_id=1, source_target_pairs={{0,1},{1,0},{2,3},{3,2},{4,5},{5,4},{6,7},{7,6},{8,9},{9,8},{10,11... | collective-permute-start | bytes 4718600 | tf_op jit(solution)/shard_map/ppermute | solution.py:24
  2.0 33.3 %collective-permute-start.1 = (bf16[2,256,768]{2,1,0:T(8,128)(2,1)S(1)}, bf16[2,256,768]{2,1,0:T(8,128)(2,1)S(1)}, u32[]{:S(2)}, u32[]{:S(2)}) collective-permute-start(bf16[2,256,768]{2,1,0:T(8,128)(2,1)S(1)} %slice.12), channel_id=1, source_target_pairs={{0,15},{1,2},{2,1},{3,4},{4,3},{5,6},{6,5},{7,8},{8,7},{9,10},{10,... | collective-permute-start | bytes 2359304 | tf_op jit(solution)/shard_map/ppermute | solution.py:526
  8.3 13.9 %collective-permute-start.2 = (bf16[1,256,768]{2,1,0:T(8,128)(2,1)S(1)}, bf16[1,256,768]{2,1,0:T(8,128)(2,1)S(1)}, u32[]{:S(2)}, u32[]{:S(2)}) collective-permute-start(bf16[1,256,768]{2,1,0:T(8,128)(2,1)S(1)} %get-tuple-element.133), channel_id=1, source_target_pairs={{0,15},{1,2},{2,1},{3,4},{4,3},{5,6},{6,5},{7,8},{8,7},{9,10},{10,... | collective-permute-start | bytes 1179656 | tf_op jit(solution)/shard_map/ppermute | solution.py:526
  8.4 26.2 %collective-permute-start.5 = (bf16[128,768]{1,0:T(8,128)(2,1)S(1)}, bf16[128,768]{1,0:T(8,128)(2,1)S(1)}, u32[]{:S(2)}, u32[]{:S(2)}) collective-permute-start(bf16[128,768]{1,0:T(8,128)(2,1)S(1)} %copy-done.4), channel_id=1, source_target_pairs={{48,0},{0,16},{16,32},{32,48},{112,64},{64,80},{80,96},{96,112},{4... | collective-permute-start | bytes 589832 | tf_op jit(solution)/shard_map/ppermute | solution.py:33
  10.1 24.6 %collective-permute-start.4 = (bf16[128,768]{1,0:T(8,128)(2,1)S(1)}, bf16[128,768]{1,0:T(8,128)(2,1)S(1)}, u32[]{:S(2)}, u32[]{:S(2)}) collective-permute-start(bf16[128,768]{1,0:T(8,128)(2,1)S(1)} %copy-done.4), channel_id=1, source_target_pairs={{32,0},{48,16},{0,32},{16,48},{96,64},{112,80},{64,96},{80,112},{3... | collective-permute-start | bytes 589832 | tf_op jit(solution)/shard_map/ppermute | solution.py:33
  14.7 10.6 %copy-start = (bf16[768,2304]{1,0:T(8,128)(2,1)S(1)}, bf16[768,2304]{1,0:T(8,128)(2,1)}, u32[]{:S(2)}) copy-start(bf16[768,2304]{1,0:T(8,128)(2,1)} %refs_7_.5) | copy-start | bytes 10616836
  22.3 12.4 %collective-permute-start.3 = (bf16[128,768]{1,0:T(8,128)(2,1)S(1)}, bf16[128,768]{1,0:T(8,128)(2,1)S(1)}, u32[]{:S(2)}, u32[]{:S(2)}) collective-permute-start(bf16[128,768]{1,0:T(8,128)(2,1)S(1)} %copy-done.4), channel_id=1, source_target_pairs={{16,0},{32,16},{48,32},{0,48},{80,64},{96,80},{112,96},{64,112},{1... | collective-permute-start | bytes 589832 | tf_op jit(solution)/shard_map/ppermute | solution.py:33
  25.3 3.2 %copy-start.2 = (bf16[4,256,768]{2,1,0:T(8,128)(2,1)S(1)}, bf16[4,256,768]{2,1,0:T(8,128)(2,1)}, u32[]{:S(2)}) copy-start(bf16[4,256,768]{2,1,0:T(8,128)(2,1)} %refs_1_.5) | copy-start | bytes 4718596
  25.3 3.2 %copy-start.3 = (bf16[768,768]{1,0:T(8,128)(2,1)S(1)}, bf16[768,768]{1,0:T(8,128)(2,1)}, u32[]{:S(2)}) copy-start(bf16[768,768]{1,0:T(8,128)(2,1)} %refs_9_.5) | copy-start | bytes 3538948
  25.3 3.2 %copy-start.5 = (f32[768]{0:T(1024)S(1)}, f32[768]{0:T(1024)}, u32[]{:S(2)}) copy-start(f32[768]{0:T(1024)} %gain.1) | copy-start | bytes 9220
  25.3 3.2 %copy-start.6 = (s32[4]{0:T(128)S(1)}, s32[4]{0:T(128)}, u32[]{:S(2)}) copy-start(s32[4]{0:T(128)} %lengths.1) | copy-start | bytes 52
  28.5 6.2 %copy-start.7 = (s32[32]{0:T(128)S(1)}, s32[32]{0:T(128)}, u32[]{:S(2)}) copy-start(s32[32]{0:T(128)} %positive.2) | copy-start | bytes 388
  35.4 17.1 %collective-permute-start.6 = (bf16[1,256,768]{2,1,0:T(8,128)(2,1)S(1)}, bf16[1,256,768]{2,1,0:T(8,128)(2,1)S(1)}, u32[]{:S(2)}, u32[]{:S(2)}) collective-permute-start(bf16[1,256,768]{2,1,0:T(8,128)(2,1)S(1)} %get-tuple-element.76), channel_id=1, source_target_pairs={{0,15},{1,2},{2,1},{3,4},{4,3},{5,6},{6,5},{7,8},{8,7},{9,10},{10,... | collective-permute-start | bytes 1179656 | tf_op jit(solution)/shard_map/ppermute | solution.py:526
  58.6 44.2 %collective-permute-start.21 = (bf16[4,256,768]{2,1,0:T(8,128)(2,1)S(1)}, bf16[4,256,768]{2,1,0:T(8,128)(2,1)S(1)}, u32[]{:S(2)}, u32[]{:S(2)}) collective-permute-start(bf16[4,256,768]{2,1,0:T(8,128)(2,1)S(1)} %get-tuple-element.107.normed), channel_id=1, source_target_pairs={{0,1},{1,0},{2,3},{3,2},{4,5},{5,4},{6,7},{7,6},{8,9},{9,8},{10,11... | collective-permute-start | bytes 4718600 | tf_op jit(solution)/shard_map/ppermute | solution.py:24
  67.3 3.1 %collective-permute-start.7 = (f32[12,768]{1,0:T(8,128)S(1)}, f32[12,768]{1,0:T(8,128)S(1)}, u32[]{:S(2)}, u32[]{:S(2)}) collective-permute-start(f32[12,768]{1,0:T(8,128)S(1)} %stack.1.refs_0_), channel_id=1, source_target_pairs={{0,1},{1,0},{2,3},{3,2},{4,5},{5,4},{6,7},{7,6},{8,9},{9,8},{10,11... | collective-permute-start | bytes 110600 | tf_op jit(solution)/shard_map/ppermute | solution.py:24
  70.4 7.3 %collective-permute-start.10 = (f32[12,768]{1,0:T(8,128)S(1)}, f32[12,768]{1,0:T(8,128)S(1)}, u32[]{:S(2)}, u32[]{:S(2)}) collective-permute-start(f32[12,768]{1,0:T(8,128)S(1)} %add.3.refs_0_), channel_id=1, source_target_pairs={{12,0},{13,1},{14,2},{15,3},{0,4},{1,5},{2,6},{3,7},{4,8},{5,9},{6... | collective-permute-start | bytes 110600 | tf_op jit(solution)/shard_map/ppermute | solution.py:29
  71.9 5.8 %collective-permute-start.9 = (f32[12,768]{1,0:T(8,128)S(1)}, f32[12,768]{1,0:T(8,128)S(1)}, u32[]{:S(2)}, u32[]{:S(2)}) collective-permute-start(f32[12,768]{1,0:T(8,128)S(1)} %add.3.refs_0_), channel_id=1, source_target_pairs={{8,0},{9,1},{10,2},{11,3},{12,4},{13,5},{14,6},{15,7},{0,8},{1,9},... | collective-permute-start | bytes 110600 | tf_op jit(solution)/shard_map/ppermute | solution.py:29
  74.6 4.1 %collective-permute-start.8 = (f32[12,768]{1,0:T(8,128)S(1)}, f32[12,768]{1,0:T(8,128)S(1)}, u32[]{:S(2)}, u32[]{:S(2)}) collective-permute-start(f32[12,768]{1,0:T(8,128)S(1)} %add.3.refs_0_), channel_id=1, source_target_pairs={{4,0},{5,1},{6,2},{7,3},{8,4},{9,5},{10,6},{11,7},{12,8},{13,9},{1... | collective-permute-start | bytes 110600 | tf_op jit(solution)/shard_map/ppermute | solution.py:29
  78.7 24.0 %collective-permute-start.23 = (bf16[384,1024]{1,0:T(8,128)(2,1)S(1)}, bf16[384,1024]{1,0:T(8,128)(2,1)S(1)}, u32[]{:S(2)}, u32[]{:S(2)}) collective-permute-start(bf16[384,1024]{1,0:T(8,128)(2,1)S(1)} %get-tuple-element.109), channel_id=1, source_target_pairs={{0,1},{1,0},{2,3},{3,2},{4,5},{5,4},{6,7},{7,6},{8,9},{9,8},{10,11... | collective-permute-start | bytes 2359304 | tf_op jit(solution)/shard_map/ppermute | solution.py:24
  78.8 23.9 %collective-permute-start.22 = (f32[4,256,128]{2,1,0:T(8,128)S(1)}, f32[4,256,128]{2,1,0:T(8,128)S(1)}, u32[]{:S(2)}, u32[]{:S(2)}) collective-permute-start(f32[4,256,128]{2,1,0:T(8,128)S(1)} %get-tuple-element.108.rstd), channel_id=1, source_target_pairs={{0,1},{1,0},{2,3},{3,2},{4,5},{5,4},{6,7},{7,6},{8,9},{9,8},{10,11... | collective-permute-start | bytes 1572872 | tf_op jit(solution)/shard_map/ppermute | solution.py:24
  79.3 5.8 %collective-permute-start.13 = (f32[12,768]{1,0:T(8,128)S(1)}, f32[12,768]{1,0:T(8,128)S(1)}, u32[]{:S(2)}, u32[]{:S(2)}) collective-permute-start(f32[12,768]{1,0:T(8,128)S(1)} %add.4.s0), channel_id=1, source_target_pairs={{66,0},{67,1},{64,2},{65,3},{70,4},{71,5},{68,6},{69,7},{74,8},{75... | collective-permute-start | bytes 110600 | tf_op jit(solution)/shard_map/ppermute | solution.py:43
  80.3 5.6 %collective-permute-start.12 = (f32[12,768]{1,0:T(8,128)S(1)}, f32[12,768]{1,0:T(8,128)S(1)}, u32[]{:S(2)}, u32[]{:S(2)}) collective-permute-start(f32[12,768]{1,0:T(8,128)S(1)} %add.4.s0), channel_id=1, source_target_pairs={{2,0},{3,1},{0,2},{1,3},{6,4},{7,5},{4,6},{5,7},{10,8},{11,9},{8,1... | collective-permute-start | bytes 110600 | tf_op jit(solution)/shard_map/ppermute | solution.py:43
  85.1 4.1 %collective-permute-start.11 = (f32[12,768]{1,0:T(8,128)S(1)}, f32[12,768]{1,0:T(8,128)S(1)}, u32[]{:S(2)}, u32[]{:S(2)}) collective-permute-start(f32[12,768]{1,0:T(8,128)S(1)} %add.4.s0), channel_id=1, source_target_pairs={{64,0},{65,1},{66,2},{67,3},{68,4},{69,5},{70,6},{71,7},{72,8},{73... | collective-permute-start | bytes 110600 | tf_op jit(solution)/shard_map/ppermute | solution.py:43
  85.9 3.3 %collective-permute-start.14 = (bf16[128,768]{1,0:T(8,128)(2,1)S(1)}, bf16[128,768]{1,0:T(8,128)(2,1)S(1)}, u32[]{:S(2)}, u32[]{:S(2)}) collective-permute-start(bf16[128,768]{1,0:T(8,128)(2,1)S(1)} %copy-done.4), channel_id=1, source_target_pairs={{0,1},{1,0},{2,3},{3,2},{4,5},{5,4},{6,7},{7,6},{8,9},{9,8},{10,11... | collective-permute-start | bytes 589832 | tf_op jit(solution)/shard_map/ppermute | solution.py:24
  89.2 1.4 collective-permute-start.15
  89.2 1.7 %collective-permute-start.16 = (bf16[128,768]{1,0:T(8,128)(2,1)S(1)}, bf16[128,768]{1,0:T(8,128)(2,1)S(1)}, u32[]{:S(2)}, u32[]{:S(2)}) collective-permute-start(bf16[128,768]{1,0:T(8,128)(2,1)S(1)} %collective-permute-done.4.refs_2_), channel_id=1, source_target_pairs={{0,1},{1,0},{2,3},{3,2},{4,5},{5,4},{6,7},{7,6},{8,9},{9,8},{10,11... | collective-permute-start | bytes 589832 | tf_op jit(solution)/shard_map/ppermute | solution.py:24
  90.7 1.4 collective-permute-start.17
  92.1 5.0 %collective-permute-start.20 = (f32[8,768]{1,0:T(8,128)S(1)}, f32[8,768]{1,0:T(8,128)S(1)}, u32[]{:S(2)}, u32[]{:S(2)}) collective-permute-start(f32[8,768]{1,0:T(8,128)S(1)} %get-tuple-element.101.e0.emb), channel_id=1, source_target_pairs={{48,0},{0,16},{16,32},{32,48},{112,64},{64,80},{80,96},{96,112},{4... | collective-permute-start | bytes 73736 | tf_op jit(solution)/shard_map/ppermute | solution.py:33
  92.1 5.3 %collective-permute-start.19 = (f32[8,768]{1,0:T(8,128)S(1)}, f32[8,768]{1,0:T(8,128)S(1)}, u32[]{:S(2)}, u32[]{:S(2)}) collective-permute-start(f32[8,768]{1,0:T(8,128)S(1)} %get-tuple-element.101.e0.emb), channel_id=1, source_target_pairs={{32,0},{48,16},{0,32},{16,48},{96,64},{112,80},{64,96},{80,112},{3... | collective-permute-start | bytes 73736 | tf_op jit(solution)/shard_map/ppermute | solution.py:33
  97.1 3.8 %collective-permute-start.18 = (f32[8,768]{1,0:T(8,128)S(1)}, f32[8,768]{1,0:T(8,128)S(1)}, u32[]{:S(2)}, u32[]{:S(2)}) collective-permute-start(f32[8,768]{1,0:T(8,128)S(1)} %get-tuple-element.101.e0.emb), channel_id=1, source_target_pairs={{16,0},{32,16},{48,32},{0,48},{80,64},{96,80},{112,96},{64,112},{1... | collective-permute-start | bytes 73736 | tf_op jit(solution)/shard_map/ppermute | solution.py:33
  102.7 5.5 %collective-permute-start.26 = (f32[16,1024]{1,0:T(8,128)S(1)}, f32[16,1024]{1,0:T(8,128)S(1)}, u32[]{:S(2)}, u32[]{:S(2)}) collective-permute-start(f32[16,1024]{1,0:T(8,128)S(1)} %get-tuple-element.110.refs_0_), channel_id=1, source_target_pairs={{12,0},{13,1},{14,2},{15,3},{0,4},{1,5},{2,6},{3,7},{4,8},{5,9},{6... | collective-permute-start | bytes 196616 | tf_op jit(solution)/shard_map/ppermute | solution.py:29
  103.3 6.5 %collective-permute-start.25 = (f32[16,1024]{1,0:T(8,128)S(1)}, f32[16,1024]{1,0:T(8,128)S(1)}, u32[]{:S(2)}, u32[]{:S(2)}) collective-permute-start(f32[16,1024]{1,0:T(8,128)S(1)} %get-tuple-element.110.refs_0_), channel_id=1, source_target_pairs={{8,0},{9,1},{10,2},{11,3},{12,4},{13,5},{14,6},{15,7},{0,8},{1,9},... | collective-permute-start | bytes 196616 | tf_op jit(solution)/shard_map/ppermute | solution.py:29
  106.9 4.3 %collective-permute-start.24 = (f32[16,1024]{1,0:T(8,128)S(1)}, f32[16,1024]{1,0:T(8,128)S(1)}, u32[]{:S(2)}, u32[]{:S(2)}) collective-permute-start(f32[16,1024]{1,0:T(8,128)S(1)} %get-tuple-element.110.refs_0_), channel_id=1, source_target_pairs={{4,0},{5,1},{6,2},{7,3},{8,4},{9,5},{10,6},{11,7},{12,8},{13,9},{1... | collective-permute-start | bytes 196616 | tf_op jit(solution)/shard_map/ppermute | solution.py:29
  111.3 6.2 %collective-permute-start.29 = (f32[16,1024]{1,0:T(8,128)S(1)}, f32[16,1024]{1,0:T(8,128)S(1)}, u32[]{:S(2)}, u32[]{:S(2)}) collective-permute-start(f32[16,1024]{1,0:T(8,128)S(1)} %merge.1.s0), channel_id=1, source_target_pairs={{66,0},{67,1},{64,2},{65,3},{70,4},{71,5},{68,6},{69,7},{74,8},{75... | collective-permute-start | bytes 196616 | tf_op jit(solution)/shard_map/ppermute | solution.py:43
  111.4 6.2 %collective-permute-start.28 = (f32[16,1024]{1,0:T(8,128)S(1)}, f32[16,1024]{1,0:T(8,128)S(1)}, u32[]{:S(2)}, u32[]{:S(2)}) collective-permute-start(f32[16,1024]{1,0:T(8,128)S(1)} %merge.1.s0), channel_id=1, source_target_pairs={{2,0},{3,1},{0,2},{1,3},{6,4},{7,5},{4,6},{5,7},{10,8},{11,9},{8,1... | collective-permute-start | bytes 196616 | tf_op jit(solution)/shard_map/ppermute | solution.py:43
  114.1 4.4 %collective-permute-start.27 = (f32[16,1024]{1,0:T(8,128)S(1)}, f32[16,1024]{1,0:T(8,128)S(1)}, u32[]{:S(2)}, u32[]{:S(2)}) collective-permute-start(f32[16,1024]{1,0:T(8,128)S(1)} %merge.1.s0), channel_id=1, source_target_pairs={{64,0},{65,1},{66,2},{67,3},{68,4},{69,5},{70,6},{71,7},{72,8},{73... | collective-permute-start | bytes 196616 | tf_op jit(solution)/shard_map/ppermute | solution.py:43
  123.2 9.2 %collective-permute-start.30 = (bf16[96,768]{1,0:T(8,128)(2,1)S(1)}, bf16[96,768]{1,0:T(8,128)(2,1)S(1)}, u32[]{:S(2)}, u32[]{:S(2)}) collective-permute-start(bf16[96,768]{1,0:T(8,128)(2,1)S(1)} %get-tuple-element.122), channel_id=1, source_target_pairs={{48,0},{13,1},{50,2},{15,3},{52,4},{1,5},{54,6},{3,7},{56,8},{5,9}... | collective-permute-start | bytes 442376 | tf_op jit(solution)/shard_map/ppermute | solution.py:54
  123.3 9.1 %collective-permute-start.31 = (bf16[96,768]{1,0:T(8,128)(2,1)S(1)}, bf16[96,768]{1,0:T(8,128)(2,1)S(1)}, u32[]{:S(2)}, u32[]{:S(2)}) collective-permute-start(bf16[96,768]{1,0:T(8,128)(2,1)S(1)} %get-tuple-element.123), channel_id=1, source_target_pairs={{32,0},{9,1},{34,2},{11,3},{36,4},{13,5},{38,6},{15,7},{40,8},{1,9... | collective-permute-start | bytes 442376 | tf_op jit(solution)/shard_map/ppermute | solution.py:54
  126.0 7.7 %collective-permute-start.32 = (bf16[96,768]{1,0:T(8,128)(2,1)S(1)}, bf16[96,768]{1,0:T(8,128)(2,1)S(1)}, u32[]{:S(2)}, u32[]{:S(2)}) collective-permute-start(bf16[96,768]{1,0:T(8,128)(2,1)S(1)} %get-tuple-element.124), channel_id=1, source_target_pairs={{16,0},{5,1},{18,2},{7,3},{20,4},{9,5},{22,6},{11,7},{24,8},{13,9}... | collective-permute-start | bytes 442376 | tf_op jit(solution)/shard_map/ppermute | solution.py:54
  133.8 6.4 %collective-permute-start.33 = (f32[24,768]{1,0:T(8,128)S(1)}, f32[24,768]{1,0:T(8,128)S(1)}, u32[]{:S(2)}, u32[]{:S(2)}) collective-permute-start(f32[24,768]{1,0:T(8,128)S(1)} %get-tuple-element.126), channel_id=1, source_target_pairs={{12,0},{49,1},{14,2},{51,3},{0,4},{53,5},{2,6},{55,7},{4,8},{57,9}... | collective-permute-start | bytes 221192 | tf_op jit(solution)/shard_map/ppermute | solution.py:54
  133.9 6.3 %collective-permute-start.34 = (f32[24,768]{1,0:T(8,128)S(1)}, f32[24,768]{1,0:T(8,128)S(1)}, u32[]{:S(2)}, u32[]{:S(2)}) collective-permute-start(f32[24,768]{1,0:T(8,128)S(1)} %get-tuple-element.127), channel_id=1, source_target_pairs={{8,0},{33,1},{10,2},{35,3},{12,4},{37,5},{14,6},{39,7},{0,8},{41,9... | collective-permute-start | bytes 221192 | tf_op jit(solution)/shard_map/ppermute | solution.py:54
  136.0 5.0 %collective-permute-start.35 = (f32[24,768]{1,0:T(8,128)S(1)}, f32[24,768]{1,0:T(8,128)S(1)}, u32[]{:S(2)}, u32[]{:S(2)}) collective-permute-start(f32[24,768]{1,0:T(8,128)S(1)} %get-tuple-element.128), channel_id=1, source_target_pairs={{4,0},{17,1},{6,2},{19,3},{8,4},{21,5},{10,6},{23,7},{12,8},{25,9}... | collective-permute-start | bytes 221192 | tf_op jit(solution)/shard_map/ppermute | solution.py:54
  141.1 5.1 %collective-permute-start.36 = (f32[6,768]{1,0:T(8,128)S(1)}, f32[6,768]{1,0:T(8,128)S(1)}, u32[]{:S(2)}, u32[]{:S(2)}) collective-permute-start(f32[6,768]{1,0:T(8,128)S(1)} %get-tuple-element.130), channel_id=1, source_target_pairs={{66,0},{67,1},{64,2},{65,3},{70,4},{71,5},{68,6},{69,7},{74,8},{75... | collective-permute-start | bytes 55304 | tf_op jit(solution)/shard_map/ppermute | solution.py:43
  142.5 5.3 %collective-permute-start.37 = (f32[6,768]{1,0:T(8,128)S(1)}, f32[6,768]{1,0:T(8,128)S(1)}, u32[]{:S(2)}, u32[]{:S(2)}) collective-permute-start(f32[6,768]{1,0:T(8,128)S(1)} %get-tuple-element.131), channel_id=1, source_target_pairs={{2,0},{3,1},{0,2},{1,3},{6,4},{7,5},{4,6},{5,7},{10,8},{11,9},{8,1... | collective-permute-start | bytes 55304 | tf_op jit(solution)/shard_map/ppermute | solution.py:43
  145.0 3.8 %collective-permute-start.38 = (f32[6,768]{1,0:T(8,128)S(1)}, f32[6,768]{1,0:T(8,128)S(1)}, u32[]{:S(2)}, u32[]{:S(2)}) collective-permute-start(f32[6,768]{1,0:T(8,128)S(1)} %get-tuple-element.132), channel_id=1, source_target_pairs={{64,0},{65,1},{66,2},{67,3},{68,4},{69,5},{70,6},{71,7},{72,8},{73... | collective-permute-start | bytes 55304 | tf_op jit(solution)/shard_map/ppermute | solution.py:43

commit v3 on v1

--- a/solution.py
+++ b/solution.py
@@ -19,6 +19,8 @@
 SMEM = pl.BlockSpec(memory_space=pltpu.SMEM)
 ANY = pl.BlockSpec(memory_space=pl.ANY)
 
+ORDER = (0, 1, 3, 2)
+
 
 def swap(value, axis, bits):
     return lax.ppermute(value, axis, [(i, i ^ bits) for i in range(lax.axis_size(axis))])
@@ -55,7 +57,7 @@
 
 
 def around(value, fetch):
-    return [value] + [fetch(value, k) for k in (1, 2, 3)]
+    return [value] + [fetch(value, k) for k in ORDER[1:]]
 
 
 def here():
@@ -64,6 +66,10 @@
 
 def in_hbm(value):
     return pltpu.with_memory_space_constraint(value, pltpu.HBM)
+
+
+def dealt(pieces, fetch):
+    return [fetch(pieces[k - 1], -k) for k in (2, 1, 3)]
 
 
 def call(kernel, out_shape, in_specs, out_specs, limit=16, flops=0, moved=0, **keywords):
@@ -285,7 +291,7 @@
 def add_kernel(*refs):
     terms = [ref[...] for ref in refs[:-1]]
     if len(terms) == 4:
-        terms = [terms[0] + terms[2], terms[1] + terms[3]]
+        terms = [terms[0] + terms[3], terms[1] + terms[2]]
     refs[-1][...] = terms[0] + terms[1]
 
 
@@ -306,7 +312,7 @@
     pieces, out = refs[:4], refs[4]
     dp, _ = here()
     total = jnp.zeros(out.shape, jnp.float32)
-    for k, piece in enumerate(pieces):
+    for k, piece in zip(ORDER, pieces):
         shape = (out.shape[0], piece.shape[0])
         doc = lax.broadcasted_iota(jnp.int32, shape, 0)
         wanted = jnp.zeros(shape, jnp.int32)
@@ -319,7 +325,7 @@
 
 def turn_kernel(mixed, out):
     width = out.shape[0]
-    rows = 128
+    rows = 192
     lax.fori_loop(0, width // rows, lambda index, _: turn_rows(index * rows, rows, mixed, out), None)
 
 
@@ -336,11 +342,11 @@
     block = ((z & 1) * 4 + y) * 16 + x * 4 + (z >> 1) * 2 + core
     chosen = block * each + place % each == lax.broadcasted_iota(jnp.int32, (rows, width), 1)
     chosen = jnp.where(chosen, 1.0, 0.0).astype(jnp.bfloat16)
-    here_rows = pl.ds(pl.multiple_of(low, rows), rows)
+    here_rows = pl.ds(pl.multiple_of(low, 64), rows)
     out[here_rows, :] = jnp.dot(chosen, mixed[...], preferred_element_type=jnp.float32).astype(jnp.bfloat16)
 
 
-def norm_kernel(s0, s1, s2, s3, emb_out, rinv_out, target_out):
+def norm_kernel(s0, s1, s3, s2, emb_out, rinv_out, target_out):
     docs = s0.shape[0] // 3
     dp, _ = here()
     own, other = s0[0:docs] + s2[0:docs], s1[0:docs] + s3[0:docs]
@@ -358,13 +364,13 @@
     return jnp.sum(jnp.where(same, column, 0.0), axis=0, keepdims=True)
 
 
-def score_kernel(docs, positive, e0, e1, e2, e3, *refs):
-    tables, (everyone, state, expos) = refs[:8], refs[8:]
+def score_kernel(docs, positive, *refs):
+    embs, tables, (everyone, state, expos) = refs[:4], refs[4:12], refs[12:]
     all_docs, width = everyone.shape
     dp, _ = here()
     y = dp & 3
-    group = e0.shape[0]
-    for k, piece in enumerate((e0, e1, e2, e3)):
+    group = embs[0].shape[0]
+    for k, piece in zip(ORDER, embs):
         everyone[pl.ds(pl.multiple_of(((y + k) & 3) * group, group), group), :] = piece[...]
     rows = tables[0].shape[0]
     emb = thirds(everyone[...])
@@ -380,10 +386,10 @@
         expo = jnp.exp(s - top)
         expos[:, k * rows : (k + 1) * rows] = expo
         totals.append(jnp.sum(expo, axis=1, keepdims=True))
-        hit = row_ids(k, (all_docs, rows), 1) == wanted
+        hit = row_ids(ORDER[k % 4] + k // 4 * 4, (all_docs, rows), 1) == wanted
         found = found + jnp.sum(jnp.where(hit, s, 0.0), axis=1, keepdims=True)
     totals = [totals[k] + totals[k + 4] for k in range(4)]
-    total = (totals[0] + totals[2]) + (totals[1] + totals[3])
+    total = (totals[0] + totals[3]) + (totals[1] + totals[2])
     mine = thirds(expos[pl.ds(pl.multiple_of(y * group, group), group), :])
     mix = jnp.zeros((group, width), jnp.float32)
     for k, t in enumerate(tables):
@@ -412,7 +418,7 @@
         s * jnp.exp(jnp.where(row == docs, b - top_lane, a - top_row)) for s, a, b in zip(states, by_row, by_lane)
     ]
     if len(terms) == 4:
-        terms = [terms[0] + terms[2], terms[1] + terms[3]]
+        terms = [terms[0] + terms[3], terms[1] + terms[2]]
     joined = jnp.where((row < docs) & (column >= place), top_row, terms[0] + terms[1])
     return jnp.where(row == docs + 1, top_lane, joined)
 
@@ -469,11 +475,11 @@
 
 
 def product_rows(turned, low, d_summed, out):
-    rows = 128
+    rows = 192
 
     def some(index, _):
-        source = pl.ds(pl.multiple_of(low + index * rows, rows), rows)
-        here_rows = pl.ds(pl.multiple_of(index * rows, rows), rows)
+        source = pl.ds(pl.multiple_of(low + index * rows, 64), rows)
+        here_rows = pl.ds(pl.multiple_of(index * rows, 64), rows)
         out[here_rows, :] = jnp.dot(turned[source, :], d_summed[...], preferred_element_type=jnp.float32)
 
     lax.fori_loop(0, out.shape[0] // rows, some, None)
@@ -551,6 +557,7 @@
     )
     sums = add([sums, swap(sums, "ctx", 1)])
     sums = add(around(sums, from_x))
+    sums, turned = lax.optimization_barrier((sums, turned))
     emb, rinv, target = call(
         norm_kernel,
         (f32(group, width), f32(group, 128), f32(group, width)),
@@ -600,11 +607,11 @@
         name="keep",
     )(turned, d_summed)
     keep, *sends = sum_and_split([keep, swap(send, "ctx", 1)], jnp.bfloat16)
-    got = [from_plane(piece, -(k + 1), False) for k, piece in enumerate(sends)]
+    got = dealt(sends, lambda piece, k: from_plane(piece, k, False))
     keep, *sends = sum_and_split([keep] + got, jnp.float32)
-    got = [from_plane(piece, -(k + 1), True) for k, piece in enumerate(sends)]
+    got = dealt(sends, lambda piece, k: from_plane(piece, k, True))
     keep, *sends = sum_and_split([keep] + got, jnp.float32)
-    got = [from_z(piece, -(k + 1)) for k, piece in enumerate(sends)]
+    got = dealt(sends, from_z)
     return (hidden, loss[0, 0], add([keep] + got))
 
 

time: 131 us -> 132 us (level)
  starting transfers between devices: 56.5 us -> 59.7 us
  waiting for transfers between devices: 25.9 us -> 23.8 us
    ppermute x6, waiting for transfers between devices: 7.29 us -> 3.05 us  [from_x(): lax.ppermute(value, 'ctx', [((c + 4 * k) % size, c) for c in range(size)])]
    ppermute x9, starting transfers between devices: 12.9 us -> 15.3 us  [from_z(): return lax.ppermute(value, ('dp', 'ctx'), pairs)]
    ppermute x9, waiting for transfers between devices: 4.98 us -> 7.11 us  [from_z(): return lax.ppermute(value, ('dp', 'ctx'), pairs)]
  transfers between devices with their start and end apart: 37 -> 37, of which waited for: 22 -> 23; matrix products, arithmetic and copies ran while one was open for 1% -> 1% of each run, Pallas kernels for 26% -> 25%
where the time goes in v3:
time: 132 us; the launch traced here: 131 us
  starting transfers between devices  59.7 us (45%)
  Pallas kernels  45.1 us (34%)
  waiting for transfers between devices  23.8 us (18%)
  local copies, waits for them, and re-layouts  1.77 us (1%)
    pallas_call x3, Pallas kernels, attend(): call(functools.partial(attend_kernel, first), out_shape, in_specs, out_sp...  23.9 us
    ppermute x9, starting transfers between devices, from_z(): return lax.ppermute(value, ('dp', 'ctx'), pairs)  15.3 us
    ppermute x3, starting transfers between devices, shards(): fetch = lambda part: lax.ppermute(part, 'ctx', ring)  11.3 us
    ppermute x6, starting transfers between devices, from_y(): lax.ppermute(value, 'dp', [(d & 4 | d + k & 3, d) for d in range(lax.axis...  10.8 us
    ppermute x6, starting transfers between devices, from_plane(): return lax.ppermute(value, ('dp', 'ctx'), pairs)  9.12 us
    ppermute x6, starting transfers between devices, from_x(): lax.ppermute(value, 'ctx', [((c + 4 * k) % size, c) for c in range(size)])  8.33 us
    ppermute x6, waiting for transfers between devices, from_plane(): return lax.ppermute(value, ('dp', 'ctx'), pairs)  8.11 us
    pallas_call x1, Pallas kernels, prepare(): call(prepare_kernel, (bf16(docs, tb, 2 * width), bf16(width, docs * tb),...  7.17 us
  transfers between devices with their start and end apart: 37, of which 23 were waited for; matrix products, arithmetic and copies ran while one was open for 1% of the time, Pallas kernels for 25%

profile of v3, /device:TPU:0, one launch (start us, length us, event | category | flops | bytes accessed | tf_op | source)
XLA Modules:
  0.0 131.4 jit_solution(2546642507586879731)
XLA Ops:
  0.7 1.7 %collective-permute-start.4 = (bf16[128,768]{1,0:T(8,128)(2,1)}, bf16[128,768]{1,0:T(8,128)(2,1)S(1)}, u32[]{:S(2)}, u32[]{:S(2)}) collective-permute-start(bf16[128,768]{1,0:T(8,128)(2,1)} %refs_4_), channel_id=1, source_target_pairs={{48,0},{0,16},{16,32},{32,48},{112,64},{64,80},{80,96},{96,112},{4... | collective-permute-start | bytes 589832 | tf_op jit(solution)/shard_map/ppermute | solution.py:35
  2.5 1.6 %collective-permute-start.3 = (bf16[128,768]{1,0:T(8,128)(2,1)}, bf16[128,768]{1,0:T(8,128)(2,1)S(1)}, u32[]{:S(2)}, u32[]{:S(2)}) collective-permute-start(bf16[128,768]{1,0:T(8,128)(2,1)} %refs_4_), channel_id=1, source_target_pairs={{16,0},{32,16},{48,32},{0,48},{80,64},{96,80},{112,96},{64,112},{1... | collective-permute-start | bytes 589832 | tf_op jit(solution)/shard_map/ppermute | solution.py:35
  4.0 1.2 fusion
  5.2 5.8 %collective-permute-start.2 = (bf16[1,256,768]{2,1,0:T(8,128)(2,1)S(1)}, bf16[1,256,768]{2,1,0:T(8,128)(2,1)S(1)}, u32[]{:S(2)}, u32[]{:S(2)}) collective-permute-start(bf16[1,256,768]{2,1,0:T(8,128)(2,1)S(1)} %get-tuple-element.117), channel_id=1, source_target_pairs={{0,15},{1,2},{2,1},{3,4},{4,3},{5,6},{6,5},{7,8},{8,7},{9,10},{10,... | collective-permute-start | bytes 1179656 | tf_op jit(solution)/shard_map/ppermute | solution.py:516
  11.2 7.2 %prepare.1 = (bf16[4,256,1536]{2,1,0:T(8,128)(2,1)S(1)}, bf16[768,1024]{1,0:T(8,128)(2,1)S(1)}, bf16[768,768]{1,0:T(8,128)(2,1)S(1)}) custom-call(bf16[4,256,768]{2,1,0:T(8,128)(2,1)} %refs_1_.5, bf16[768,2304]{1,0:T(8,128)(2,1)} %refs_7_.5), custom_call_target="tpu_custom_call" | custom-call | flops 3623878656 | bytes 11534336 | tf_op jit(solution)/shard_map/prepare/pallas_call | solution.py:259
  18.4 2.0 %collective-permute-start.5 = (bf16[128,768]{1,0:T(8,128)(2,1)S(1)}, bf16[128,768]{1,0:T(8,128)(2,1)S(1)}, u32[]{:S(2)}, u32[]{:S(2)}) collective-permute-start(bf16[128,768]{1,0:T(8,128)(2,1)S(1)} %copy-done.4), channel_id=1, source_target_pairs={{32,0},{48,16},{0,32},{16,48},{96,64},{112,80},{64,96},{80,112},{3... | collective-permute-start | bytes 589832 | tf_op jit(solution)/shard_map/ppermute | solution.py:35
  20.4 3.1 %near.1 = (bf16[4,256,768]{2,1,0:T(8,128)(2,1)S(1)}, bf16[768,1024]{1,0:T(8,128)(2,1)S(1)}) custom-call(bf16[4,256,768]{2,1,0:T(8,128)(2,1)S(1)} %collective-permute-done.near, bf16[768,2304]{1,0:T(8,128)(2,1)S(1)} %copy-done, bf16[768,768]{1,0:T(8,128)(2,1)S(1)} %get-tuple-element.60.w_v_turned.refs_8_), custom_call_target="tpu_custom_call" | custom-call | flops 2415919104 | bytes 4194304 | tf_op jit(solution)/shard_map/near/pallas_call | solution.py:521
  23.6 6.1 %attend.3 = (bf16[4,256,768]{2,1,0:T(8,128)(2,1)}, bf16[768,1024]{1,0:T(8,128)(2,1)S(1)}, bf16[4,256,768]{2,1,0:T(8,128)(2,1)S(1)}, f32[4,256,128]{2,1,0:T(8,128)S(1)}, f32[4,1,768]{2,1,0:T(1,128)S(1)}) custom-call(s32[4]{0:T(128)S(1)} %copy-done.6, bf16[4,256,768]{2,1,0:T(8,128)(2,1)S(1)} %copy-done.2, bf16[4,256,768]{2,1,0:T(8,128)(2,1)S(1)} %get-tuple-element.61.refs_2_, ...), custom_call_target="tpu_custom_call" | custom-call | flops 1509949440 | bytes 4194304 | tf_op jit(solution)/shard_map/attend/pallas_call | solution.py:211
  29.7 4.0 %collective-permute-start.6 = (bf16[128,768]{1,0:T(8,128)(2,1)S(1)}, bf16[128,768]{1,0:T(8,128)(2,1)S(1)}, u32[]{:S(2)}, u32[]{:S(2)}) collective-permute-start(bf16[128,768]{1,0:T(8,128)(2,1)S(1)} %copy-done.4), channel_id=1, source_target_pairs={{0,1},{1,0},{2,3},{3,2},{4,5},{5,4},{6,7},{7,6},{8,9},{9,8},{10,11... | collective-permute-start | bytes 589832 | tf_op jit(solution)/shard_map/ppermute | solution.py:26
  35.7 5.4 %collective-permute-start.10 = (bf16[1,256,768]{2,1,0:T(8,128)(2,1)S(1)}, bf16[1,256,768]{2,1,0:T(8,128)(2,1)S(1)}, u32[]{:S(2)}, u32[]{:S(2)}) collective-permute-start(bf16[1,256,768]{2,1,0:T(8,128)(2,1)S(1)} %get-tuple-element.71), channel_id=1, source_target_pairs={{0,15},{1,2},{2,1},{3,4},{4,3},{5,6},{6,5},{7,8},{8,7},{9,10},{10,... | collective-permute-start | bytes 1179656 | tf_op jit(solution)/shard_map/ppermute | solution.py:516
  41.2 11.7 %attend.4 = (bf16[4,256,768]{2,1,0:T(8,128)(2,1)}, bf16[768,1024]{1,0:T(8,128)(2,1)S(1)}, bf16[4,256,768]{2,1,0:T(8,128)(2,1)S(1)}, f32[4,256,128]{2,1,0:T(8,128)S(1)}, f32[4,1,768]{2,1,0:T(1,128)S(1)}) custom-call(s32[4]{0:T(128)S(1)} %copy-done.6, ...), custom_call_target="tpu_custom_call", output_to_operand_aliasing={{0}: (11, {}), {1}: (12, {}), {2}: (13, {}), {3}: (14, {}),... | custom-call | flops 3019898880 | bytes 4194304 | tf_op jit(solution)/shard_map/attend/pallas_call | solution.py:211
  52.9 6.1 %attend.5 = (bf16[4,256,768]{2,1,0:T(8,128)(2,1)}, bf16[768,1024]{1,0:T(8,128)(2,1)S(1)}, bf16[4,256,768]{2,1,0:T(8,128)(2,1)S(1)}, f32[4,256,128]{2,1,0:T(8,128)S(1)}, f32[4,1,768]{2,1,0:T(1,128)S(1)}) custom-call(s32[4]{0:T(128)S(1)} %copy-done.6, ...), custom_call_target="tpu_custom_call", output_to_operand_aliasing={{0}: (11, {}), {1}: (12, {}), {2}: (13, {}), {3}: (14, {}),... | custom-call | flops 1509949440 | bytes 4194304 | tf_op jit(solution)/shard_map/attend/pallas_call | solution.py:211
  59.1 1.2 collective-permute-done.11.refs_1_
  60.3 0.9 collective-permute-start.14
  62.1 2.4 %collective-permute-start.12 = (f32[12,768]{1,0:T(8,128)S(1)}, f32[12,768]{1,0:T(8,128)S(1)}, u32[]{:S(2)}, u32[]{:S(2)}) collective-permute-start(f32[12,768]{1,0:T(8,128)S(1)} %add.3.refs_0_), channel_id=1, source_target_pairs={{4,0},{5,1},{6,2},{7,3},{8,4},{9,5},{10,6},{11,7},{12,8},{13,9},{1... | collective-permute-start | bytes 110600 | tf_op jit(solution)/shard_map/ppermute | solution.py:31
  64.5 3.3 %turn.1.turned = bf16[768,1024]{1,0:T(8,128)(2,1)S(1)} custom-call(bf16[768,1024]{1,0:T(8,128)(2,1)S(1)} %get-tuple-element.86.mixed), custom_call_target="tpu_custom_call" | custom-call | flops 1207959552 | bytes 4194304 | tf_op jit(solution)/shard_map/turn/pallas_call | solution.py:544
  67.8 1.6 %collective-permute-start.17 = (f32[12,768]{1,0:T(8,128)S(1)}, f32[12,768]{1,0:T(8,128)S(1)}, u32[]{:S(2)}, u32[]{:S(2)}) collective-permute-start(f32[12,768]{1,0:T(8,128)S(1)} %add.4.s0), channel_id=1, source_target_pairs={{2,0},{3,1},{0,2},{1,3},{6,4},{7,5},{4,6},{5,7},{10,8},{11,9},{8,1... | collective-permute-start | bytes 110600 | tf_op jit(solution)/shard_map/ppermute | solution.py:45
  69.4 1.0 collective-permute-start.16
  70.4 2.2 %collective-permute-start.15 = (f32[12,768]{1,0:T(8,128)S(1)}, f32[12,768]{1,0:T(8,128)S(1)}, u32[]{:S(2)}, u32[]{:S(2)}) collective-permute-start(f32[12,768]{1,0:T(8,128)S(1)} %add.4.s0), channel_id=1, source_target_pairs={{64,0},{65,1},{66,2},{67,3},{68,4},{69,5},{70,6},{71,7},{72,8},{73... | collective-permute-start | bytes 110600 | tf_op jit(solution)/shard_map/ppermute | solution.py:45
  72.6 1.4 %collective-permute-done.17.s2 = f32[12,768]{1,0:T(8,128)S(1)} collective-permute-done((f32[12,768]{1,0:T(8,128)S(1)}, f32[12,768]{1,0:T(8,128)S(1)}, u32[]{:S(2)}, u32[]{:S(2)}) %collective-permute-start.17) | collective-permute-done | bytes 36896 | tf_op jit(solution)/shard_map/ppermute | solution.py:45
  74.8 2.2 %collective-permute-start.20 = (f32[8,768]{1,0:T(8,128)S(1)}, f32[8,768]{1,0:T(8,128)S(1)}, u32[]{:S(2)}, u32[]{:S(2)}) collective-permute-start(f32[8,768]{1,0:T(8,128)S(1)} %get-tuple-element.88.refs_0_.emb), channel_id=1, source_target_pairs={{32,0},{48,16},{0,32},{16,48},{96,64},{112,80},{64,96},{80,112},{3... | collective-permute-start | bytes 73736 | tf_op jit(solution)/shard_map/ppermute | solution.py:35
  77.7 2.6 %collective-permute-start.18 = (f32[8,768]{1,0:T(8,128)S(1)}, f32[8,768]{1,0:T(8,128)S(1)}, u32[]{:S(2)}, u32[]{:S(2)}) collective-permute-start(f32[8,768]{1,0:T(8,128)S(1)} %get-tuple-element.88.refs_0_.emb), channel_id=1, source_target_pairs={{16,0},{32,16},{48,32},{0,48},{80,64},{96,80},{112,96},{64,112},{1... | collective-permute-start | bytes 73736 | tf_op jit(solution)/shard_map/ppermute | solution.py:35
  80.4 1.7 %collective-permute-done.19.refs_2_ = f32[8,768]{1,0:T(8,128)S(1)} collective-permute-done((f32[8,768]{1,0:T(8,128)S(1)}, f32[8,768]{1,0:T(8,128)S(1)}, u32[]{:S(2)}, u32[]{:S(2)}) %collective-permute-start.19) | collective-permute-done | bytes 24608 | tf_op jit(solution)/shard_map/ppermute | solution.py:35
  82.1 1.7 %score.1 = (f32[32,768]{1,0:T(8,128)S(1)}, f32[16,1024]{1,0:T(8,128)S(1)}) custom-call(s32[32]{0:T(128)S(1)} %copy-done.7, f32[8,768]{1,0:T(8,128)S(1)} %get-tuple-element.88.refs_0_.emb, f32[8,768]{1,0:T(8,128)S(1)} %collective-permute-done.18.refs_1_, f32[8,768]{1,0:T(8,128)S(1)} %collective-permute-done.19.refs_2_, ...), custom_call_target="tpu_custom_call" | custom-call | bytes 2097152 | tf_op jit(solution)/shard_map/score/pallas_call | solution.py:570
  83.8 0.9 collective-permute-start.23
  84.7 2.0 %collective-permute-start.22 = (f32[16,1024]{1,0:T(8,128)S(1)}, f32[16,1024]{1,0:T(8,128)S(1)}, u32[]{:S(2)}, u32[]{:S(2)}) collective-permute-start(f32[16,1024]{1,0:T(8,128)S(1)} %get-tuple-element.93.refs_0_), channel_id=1, source_target_pairs={{12,0},{13,1},{14,2},{15,3},{0,4},{1,5},{2,6},{3,7},{4,8},{5,9},{6... | collective-permute-start | bytes 196616 | tf_op jit(solution)/shard_map/ppermute | solution.py:31
  86.7 1.2 collective-permute-start.21
  87.9 1.7 %collective-permute-done.23.refs_3_ = f32[16,1024]{1,0:T(8,128)S(1)} collective-permute-done((f32[16,1024]{1,0:T(8,128)S(1)}, f32[16,1024]{1,0:T(8,128)S(1)}, u32[]{:S(2)}, u32[]{:S(2)}) %collective-permute-start.23) | collective-permute-done | bytes 65568 | tf_op jit(solution)/shard_map/ppermute | solution.py:31
  91.1 2.5 %collective-permute-start.26 = (f32[16,1024]{1,0:T(8,128)S(1)}, f32[16,1024]{1,0:T(8,128)S(1)}, u32[]{:S(2)}, u32[]{:S(2)}) collective-permute-start(f32[16,1024]{1,0:T(8,128)S(1)} %merge.1.s0), channel_id=1, source_target_pairs={{2,0},{3,1},{0,2},{1,3},{6,4},{7,5},{4,6},{5,7},{10,8},{11,9},{8,1... | collective-permute-start | bytes 196616 | tf_op jit(solution)/shard_map/ppermute | solution.py:45
  93.6 1.6 %collective-permute-start.25 = (f32[16,1024]{1,0:T(8,128)S(1)}, f32[16,1024]{1,0:T(8,128)S(1)}, u32[]{:S(2)}, u32[]{:S(2)}) collective-permute-start(f32[16,1024]{1,0:T(8,128)S(1)} %merge.1.s0), channel_id=1, source_target_pairs={{66,0},{67,1},{64,2},{65,3},{70,4},{71,5},{68,6},{69,7},{74,8},{75... | collective-permute-start | bytes 196616 | tf_op jit(solution)/shard_map/ppermute | solution.py:45
  95.3 1.6 %collective-permute-start.24 = (f32[16,1024]{1,0:T(8,128)S(1)}, f32[16,1024]{1,0:T(8,128)S(1)}, u32[]{:S(2)}, u32[]{:S(2)}) collective-permute-start(f32[16,1024]{1,0:T(8,128)S(1)} %merge.1.s0), channel_id=1, source_target_pairs={{64,0},{65,1},{66,2},{67,3},{68,4},{69,5},{70,6},{71,7},{72,8},{73... | collective-permute-start | bytes 196616 | tf_op jit(solution)/shard_map/ppermute | solution.py:45
  97.2 1.9 %collective-permute-done.25.s2 = f32[16,1024]{1,0:T(8,128)S(1)} collective-permute-done((f32[16,1024]{1,0:T(8,128)S(1)}, f32[16,1024]{1,0:T(8,128)S(1)}, u32[]{:S(2)}, u32[]{:S(2)}) %collective-permute-start.25) | collective-permute-done | bytes 65568 | tf_op jit(solution)/shard_map/ppermute | solution.py:45
  99.5 2.8 %grad.1 = (f32[384,768]{1,0:T(8,128)S(1)}, bf16[1024,768]{1,0:T(8,128)(2,1)S(1)}, f32[8,128]{1,0:T(8,128)S(1)}) custom-call(s32[4]{0:T(128)S(1)} %copy-done.6, f32[16,1024]{1,0:T(8,128)S(1)} %merge.1.s0, f32[16,1024]{1,0:T(8,128)S(1)} %collective-permute-done.24.s1, f32[16,1024]{1,0:T(8,128)S(1)} %collective-permute-done.25.s2, ...), custom_call_target="tpu_custom_call" | custom-call | flops 603979776 | bytes 8388608 | tf_op jit(solution)/shard_map/grad/pallas_call | solution.py:589
  102.4 1.0 keep.1.refs_0_
  103.4 1.8 %collective-permute-done.27.refs_1_ = f32[384,768]{1,0:T(8,128)S(1)} collective-permute-done((f32[384,768]{1,0:T(8,128)S(1)}, f32[384,768]{1,0:T(8,128)S(1)}, u32[]{:S(2)}, u32[]{:S(2)}) %collective-permute-start.27) | collective-permute-done | bytes 1179680 | tf_op jit(solution)/shard_map/ppermute | solution.py:26
  105.4 1.5 %collective-permute-start.28 = (bf16[96,768]{1,0:T(8,128)(2,1)S(1)}, bf16[96,768]{1,0:T(8,128)(2,1)S(1)}, u32[]{:S(2)}, u32[]{:S(2)}) collective-permute-start(bf16[96,768]{1,0:T(8,128)(2,1)S(1)} %get-tuple-element.106), channel_id=1, source_target_pairs={{32,0},{9,1},{34,2},{11,3},{36,4},{13,5},{38,6},{15,7},{40,8},{1,9... | collective-permute-start | bytes 442376 | tf_op jit(solution)/shard_map/ppermute | solution.py:56
  107.0 2.6 %collective-permute-start.29 = (bf16[96,768]{1,0:T(8,128)(2,1)S(1)}, bf16[96,768]{1,0:T(8,128)(2,1)S(1)}, u32[]{:S(2)}, u32[]{:S(2)}) collective-permute-start(bf16[96,768]{1,0:T(8,128)(2,1)S(1)} %get-tuple-element.107), channel_id=1, source_target_pairs={{48,0},{13,1},{50,2},{15,3},{52,4},{1,5},{54,6},{3,7},{56,8},{5,9}... | collective-permute-start | bytes 442376 | tf_op jit(solution)/shard_map/ppermute | solution.py:56
  110.2 2.0 %collective-permute-done.28.refs_1_ = bf16[96,768]{1,0:T(8,128)(2,1)S(1)} collective-permute-done((bf16[96,768]{1,0:T(8,128)(2,1)S(1)}, bf16[96,768]{1,0:T(8,128)(2,1)S(1)}, u32[]{:S(2)}, u32[]{:S(2)}) %collective-permute-start.28) | collective-permute-done | bytes 147488 | tf_op jit(solution)/shard_map/ppermute | solution.py:56
  112.2 1.5 %collective-permute-done.29.refs_2_ = bf16[96,768]{1,0:T(8,128)(2,1)S(1)} collective-permute-done((bf16[96,768]{1,0:T(8,128)(2,1)S(1)}, bf16[96,768]{1,0:T(8,128)(2,1)S(1)}, u32[]{:S(2)}, u32[]{:S(2)}) %collective-permute-start.29) | collective-permute-done | bytes 147488 | tf_op jit(solution)/shard_map/ppermute | solution.py:56
  113.7 1.0 collective-permute-done.30.refs_3_
  114.8 1.1 collective-permute-start.31
  115.9 2.5 %collective-permute-start.32 = (f32[24,768]{1,0:T(8,128)S(1)}, f32[24,768]{1,0:T(8,128)S(1)}, u32[]{:S(2)}, u32[]{:S(2)}) collective-permute-start(f32[24,768]{1,0:T(8,128)S(1)} %get-tuple-element.111), channel_id=1, source_target_pairs={{12,0},{49,1},{14,2},{51,3},{0,4},{53,5},{2,6},{55,7},{4,8},{57,9}... | collective-permute-start | bytes 221192 | tf_op jit(solution)/shard_map/ppermute | solution.py:56
  119.2 1.6 %collective-permute-done.31.refs_1_ = f32[24,768]{1,0:T(8,128)S(1)} collective-permute-done((f32[24,768]{1,0:T(8,128)S(1)}, f32[24,768]{1,0:T(8,128)S(1)}, u32[]{:S(2)}, u32[]{:S(2)}) %collective-permute-start.31) | collective-permute-done | bytes 73760 | tf_op jit(solution)/shard_map/ppermute | solution.py:56
  121.5 1.2 collective-permute-done.33.refs_3_
  122.8 1.5 %collective-permute-start.34 = (f32[6,768]{1,0:T(8,128)S(1)}, f32[6,768]{1,0:T(8,128)S(1)}, u32[]{:S(2)}, u32[]{:S(2)}) collective-permute-start(f32[6,768]{1,0:T(8,128)S(1)} %get-tuple-element.114), channel_id=1, source_target_pairs={{2,0},{3,1},{0,2},{1,3},{6,4},{7,5},{4,6},{5,7},{10,8},{11,9},{8,1... | collective-permute-start | bytes 55304 | tf_op jit(solution)/shard_map/ppermute | solution.py:45
  124.3 2.6 %collective-permute-start.35 = (f32[6,768]{1,0:T(8,128)S(1)}, f32[6,768]{1,0:T(8,128)S(1)}, u32[]{:S(2)}, u32[]{:S(2)}) collective-permute-start(f32[6,768]{1,0:T(8,128)S(1)} %get-tuple-element.115), channel_id=1, source_target_pairs={{66,0},{67,1},{64,2},{65,3},{70,4},{71,5},{68,6},{69,7},{74,8},{75... | collective-permute-start | bytes 55304 | tf_op jit(solution)/shard_map/ppermute | solution.py:45
  128.2 1.2 collective-permute-done.35.refs_2_
  129.4 1.4 %collective-permute-done.36.refs_3_ = f32[6,768]{1,0:T(8,128)S(1)} collective-permute-done((f32[6,768]{1,0:T(8,128)S(1)}, f32[6,768]{1,0:T(8,128)S(1)}, u32[]{:S(2)}, u32[]{:S(2)}) %collective-permute-start.36) | collective-permute-done | bytes 18464 | tf_op jit(solution)/shard_map/ppermute | solution.py:45
  (65 shorter events, 11.4 us)
Async XLA Ops:
  0.6 10.3 %copy-start.1 = (bf16[4,256,768]{2,1,0:T(8,128)(2,1)S(1)}, bf16[4,256,768]{2,1,0:T(8,128)(2,1)}, u32[]{:S(2)}) copy-start(bf16[4,256,768]{2,1,0:T(8,128)(2,1)} %refs_1_.5) | copy-start | bytes 4718596
  0.6 17.7 %collective-permute-start = (bf16[4,256,768]{2,1,0:T(8,128)(2,1)}, bf16[4,256,768]{2,1,0:T(8,128)(2,1)S(1)}, u32[]{:S(2)}, u32[]{:S(2)}) collective-permute-start(bf16[4,256,768]{2,1,0:T(8,128)(2,1)} %refs_1_.5), channel_id=1, source_target_pairs={{0,1},{1,0},{2,3},{3,2},{4,5},{5,4},{6,7},{7,6},{8,9},{9,8},{10,11... | collective-permute-start | bytes 4718600 | tf_op jit(solution)/shard_map/ppermute | solution.py:26
  0.7 29.0 %collective-permute-start.4 = (bf16[128,768]{1,0:T(8,128)(2,1)}, bf16[128,768]{1,0:T(8,128)(2,1)S(1)}, u32[]{:S(2)}, u32[]{:S(2)}) collective-permute-start(bf16[128,768]{1,0:T(8,128)(2,1)} %refs_4_), channel_id=1, source_target_pairs={{48,0},{0,16},{16,32},{32,48},{112,64},{64,80},{80,96},{96,112},{4... | collective-permute-start | bytes 589832 | tf_op jit(solution)/shard_map/ppermute | solution.py:35
  2.5 27.3 %collective-permute-start.3 = (bf16[128,768]{1,0:T(8,128)(2,1)}, bf16[128,768]{1,0:T(8,128)(2,1)S(1)}, u32[]{:S(2)}, u32[]{:S(2)}) collective-permute-start(bf16[128,768]{1,0:T(8,128)(2,1)} %refs_4_), channel_id=1, source_target_pairs={{16,0},{32,16},{48,32},{0,48},{80,64},{96,80},{112,96},{64,112},{1... | collective-permute-start | bytes 589832 | tf_op jit(solution)/shard_map/ppermute | solution.py:35
  5.2 18.3 %collective-permute-start.2 = (bf16[1,256,768]{2,1,0:T(8,128)(2,1)S(1)}, bf16[1,256,768]{2,1,0:T(8,128)(2,1)S(1)}, u32[]{:S(2)}, u32[]{:S(2)}) collective-permute-start(bf16[1,256,768]{2,1,0:T(8,128)(2,1)S(1)} %get-tuple-element.117), channel_id=1, source_target_pairs={{0,15},{1,2},{2,1},{3,4},{4,3},{5,6},{6,5},{7,8},{8,7},{9,10},{10,... | collective-permute-start | bytes 1179656 | tf_op jit(solution)/shard_map/ppermute | solution.py:516
  11.0 7.3 %copy-start.4 = (bf16[128,768]{1,0:T(8,128)(2,1)S(1)}, bf16[128,768]{1,0:T(8,128)(2,1)}, u32[]{:S(2)}) copy-start(bf16[128,768]{1,0:T(8,128)(2,1)} %refs_4_) | copy-start | bytes 589828
  11.0 9.3 %copy-start = (bf16[768,2304]{1,0:T(8,128)(2,1)S(1)}, bf16[768,2304]{1,0:T(8,128)(2,1)}, u32[]{:S(2)}) copy-start(bf16[768,2304]{1,0:T(8,128)(2,1)} %refs_7_.5) | copy-start | bytes 10616836
  11.1 24.0 %collective-permute-start.1 = (bf16[2,256,768]{2,1,0:T(8,128)(2,1)S(1)}, bf16[2,256,768]{2,1,0:T(8,128)(2,1)S(1)}, u32[]{:S(2)}, u32[]{:S(2)}) collective-permute-start(bf16[2,256,768]{2,1,0:T(8,128)(2,1)S(1)} %slice.12), channel_id=1, source_target_pairs={{0,15},{1,2},{2,1},{3,4},{4,3},{5,6},{6,5},{7,8},{8,7},{9,10},{10,... | collective-permute-start | bytes 2359304 | tf_op jit(solution)/shard_map/ppermute | solution.py:516
  18.4 11.4 %collective-permute-start.5 = (bf16[128,768]{1,0:T(8,128)(2,1)S(1)}, bf16[128,768]{1,0:T(8,128)(2,1)S(1)}, u32[]{:S(2)}, u32[]{:S(2)}) collective-permute-start(bf16[128,768]{1,0:T(8,128)(2,1)S(1)} %copy-done.4), channel_id=1, source_target_pairs={{32,0},{48,16},{0,32},{16,48},{96,64},{112,80},{64,96},{80,112},{3... | collective-permute-start | bytes 589832 | tf_op jit(solution)/shard_map/ppermute | solution.py:35
  20.4 3.2 %copy-start.2 = (bf16[4,256,768]{2,1,0:T(8,128)(2,1)S(1)}, bf16[4,256,768]{2,1,0:T(8,128)(2,1)}, u32[]{:S(2)}) copy-start(bf16[4,256,768]{2,1,0:T(8,128)(2,1)} %refs_1_.5) | copy-start | bytes 4718596
  20.4 3.2 %copy-start.3 = (bf16[768,768]{1,0:T(8,128)(2,1)S(1)}, bf16[768,768]{1,0:T(8,128)(2,1)}, u32[]{:S(2)}) copy-start(bf16[768,768]{1,0:T(8,128)(2,1)} %refs_9_.5) | copy-start | bytes 3538948
  20.4 3.2 %copy-start.5 = (f32[768]{0:T(1024)S(1)}, f32[768]{0:T(1024)}, u32[]{:S(2)}) copy-start(f32[768]{0:T(1024)} %gain.1) | copy-start | bytes 9220
  20.4 3.2 %copy-start.6 = (s32[4]{0:T(128)S(1)}, s32[4]{0:T(128)}, u32[]{:S(2)}) copy-start(s32[4]{0:T(128)} %lengths.1) | copy-start | bytes 52
  23.6 10.7 %copy-start.7 = (s32[32]{0:T(128)S(1)}, s32[32]{0:T(128)}, u32[]{:S(2)}) copy-start(s32[32]{0:T(128)} %positive.2) | copy-start | bytes 388
  29.7 5.3 %collective-permute-start.6 = (bf16[128,768]{1,0:T(8,128)(2,1)S(1)}, bf16[128,768]{1,0:T(8,128)(2,1)S(1)}, u32[]{:S(2)}, u32[]{:S(2)}) collective-permute-start(bf16[128,768]{1,0:T(8,128)(2,1)S(1)} %copy-done.4), channel_id=1, source_target_pairs={{0,1},{1,0},{2,3},{3,2},{4,5},{5,4},{6,7},{7,6},{8,9},{9,8},{10,11... | collective-permute-start | bytes 589832 | tf_op jit(solution)/shard_map/ppermute | solution.py:26
  33.7 1.4 %collective-permute-start.7 = (bf16[128,768]{1,0:T(8,128)(2,1)S(1)}, bf16[128,768]{1,0:T(8,128)(2,1)S(1)}, u32[]{:S(2)}, u32[]{:S(2)}) collective-permute-start(bf16[128,768]{1,0:T(8,128)(2,1)S(1)} %collective-permute-done.3.refs_1_.refs_5_), channel_id=1, source_target_pairs={{0,1},{1,0},{2,3},{3,2},{4,5},{5,4},{6,7},{7,6},{8,9},{9,8},{10,11... | collective-permute-start | bytes 589832 | tf_op jit(solution)/shard_map/ppermute | solution.py:26
  33.8 1.6 %collective-permute-start.8 = (bf16[128,768]{1,0:T(8,128)(2,1)S(1)}, bf16[128,768]{1,0:T(8,128)(2,1)S(1)}, u32[]{:S(2)}, u32[]{:S(2)}) collective-permute-start(bf16[128,768]{1,0:T(8,128)(2,1)S(1)} %collective-permute-done.4.refs_2_.refs_6_), channel_id=1, source_target_pairs={{0,1},{1,0},{2,3},{3,2},{4,5},{5,4},{6,7},{7,6},{8,9},{9,8},{10,11... | collective-permute-start | bytes 589832 | tf_op jit(solution)/shard_map/ppermute | solution.py:26
  34.2 1.5 %collective-permute-start.9 = (bf16[128,768]{1,0:T(8,128)(2,1)S(1)}, bf16[128,768]{1,0:T(8,128)(2,1)S(1)}, u32[]{:S(2)}, u32[]{:S(2)}) collective-permute-start(bf16[128,768]{1,0:T(8,128)(2,1)S(1)} %collective-permute-done.5.refs_3_.refs_7_), channel_id=1, source_target_pairs={{0,1},{1,0},{2,3},{3,2},{4,5},{5,4},{6,7},{7,6},{8,9},{9,8},{10,11... | collective-permute-start | bytes 589832 | tf_op jit(solution)/shard_map/ppermute | solution.py:26
  35.7 17.1 %collective-permute-start.10 = (bf16[1,256,768]{2,1,0:T(8,128)(2,1)S(1)}, bf16[1,256,768]{2,1,0:T(8,128)(2,1)S(1)}, u32[]{:S(2)}, u32[]{:S(2)}) collective-permute-start(bf16[1,256,768]{2,1,0:T(8,128)(2,1)S(1)} %get-tuple-element.71), channel_id=1, source_target_pairs={{0,15},{1,2},{2,1},{3,4},{4,3},{5,6},{6,5},{7,8},{8,7},{9,10},{10,... | collective-permute-start | bytes 1179656 | tf_op jit(solution)/shard_map/ppermute | solution.py:516
  59.0 1.3 collective-permute-start.11
  60.3 7.5 %collective-permute-start.14 = (f32[12,768]{1,0:T(8,128)S(1)}, f32[12,768]{1,0:T(8,128)S(1)}, u32[]{:S(2)}, u32[]{:S(2)}) collective-permute-start(f32[12,768]{1,0:T(8,128)S(1)} %add.3.refs_0_), channel_id=1, source_target_pairs={{8,0},{9,1},{10,2},{11,3},{12,4},{13,5},{14,6},{15,7},{0,8},{1,9},... | collective-permute-start | bytes 110600 | tf_op jit(solution)/shard_map/ppermute | solution.py:31
  61.3 6.5 %collective-permute-start.13 = (f32[12,768]{1,0:T(8,128)S(1)}, f32[12,768]{1,0:T(8,128)S(1)}, u32[]{:S(2)}, u32[]{:S(2)}) collective-permute-start(f32[12,768]{1,0:T(8,128)S(1)} %add.3.refs_0_), channel_id=1, source_target_pairs={{12,0},{13,1},{14,2},{15,3},{0,4},{1,5},{2,6},{3,7},{4,8},{5,9},{6... | collective-permute-start | bytes 110600 | tf_op jit(solution)/shard_map/ppermute | solution.py:31
  62.1 5.7 %collective-permute-start.12 = (f32[12,768]{1,0:T(8,128)S(1)}, f32[12,768]{1,0:T(8,128)S(1)}, u32[]{:S(2)}, u32[]{:S(2)}) collective-permute-start(f32[12,768]{1,0:T(8,128)S(1)} %add.3.refs_0_), channel_id=1, source_target_pairs={{4,0},{5,1},{6,2},{7,3},{8,4},{9,5},{10,6},{11,7},{12,8},{13,9},{1... | collective-permute-start | bytes 110600 | tf_op jit(solution)/shard_map/ppermute | solution.py:31
  67.8 6.2 %collective-permute-start.17 = (f32[12,768]{1,0:T(8,128)S(1)}, f32[12,768]{1,0:T(8,128)S(1)}, u32[]{:S(2)}, u32[]{:S(2)}) collective-permute-start(f32[12,768]{1,0:T(8,128)S(1)} %add.4.s0), channel_id=1, source_target_pairs={{2,0},{3,1},{0,2},{1,3},{6,4},{7,5},{4,6},{5,7},{10,8},{11,9},{8,1... | collective-permute-start | bytes 110600 | tf_op jit(solution)/shard_map/ppermute | solution.py:45
  69.4 5.3 %collective-permute-start.16 = (f32[12,768]{1,0:T(8,128)S(1)}, f32[12,768]{1,0:T(8,128)S(1)}, u32[]{:S(2)}, u32[]{:S(2)}) collective-permute-start(f32[12,768]{1,0:T(8,128)S(1)} %add.4.s0), channel_id=1, source_target_pairs={{66,0},{67,1},{64,2},{65,3},{70,4},{71,5},{68,6},{69,7},{74,8},{75... | collective-permute-start | bytes 110600 | tf_op jit(solution)/shard_map/ppermute | solution.py:45
  70.4 4.3 %collective-permute-start.15 = (f32[12,768]{1,0:T(8,128)S(1)}, f32[12,768]{1,0:T(8,128)S(1)}, u32[]{:S(2)}, u32[]{:S(2)}) collective-permute-start(f32[12,768]{1,0:T(8,128)S(1)} %add.4.s0), channel_id=1, source_target_pairs={{64,0},{65,1},{66,2},{67,3},{68,4},{69,5},{70,6},{71,7},{72,8},{73... | collective-permute-start | bytes 110600 | tf_op jit(solution)/shard_map/ppermute | solution.py:45
  74.8 5.6 %collective-permute-start.20 = (f32[8,768]{1,0:T(8,128)S(1)}, f32[8,768]{1,0:T(8,128)S(1)}, u32[]{:S(2)}, u32[]{:S(2)}) collective-permute-start(f32[8,768]{1,0:T(8,128)S(1)} %get-tuple-element.88.refs_0_.emb), channel_id=1, source_target_pairs={{32,0},{48,16},{0,32},{16,48},{96,64},{112,80},{64,96},{80,112},{3... | collective-permute-start | bytes 73736 | tf_op jit(solution)/shard_map/ppermute | solution.py:35
  77.0 5.0 %collective-permute-start.19 = (f32[8,768]{1,0:T(8,128)S(1)}, f32[8,768]{1,0:T(8,128)S(1)}, u32[]{:S(2)}, u32[]{:S(2)}) collective-permute-start(f32[8,768]{1,0:T(8,128)S(1)} %get-tuple-element.88.refs_0_.emb), channel_id=1, source_target_pairs={{48,0},{0,16},{16,32},{32,48},{112,64},{64,80},{80,96},{96,112},{4... | collective-permute-start | bytes 73736 | tf_op jit(solution)/shard_map/ppermute | solution.py:35
  77.7 4.4 %collective-permute-start.18 = (f32[8,768]{1,0:T(8,128)S(1)}, f32[8,768]{1,0:T(8,128)S(1)}, u32[]{:S(2)}, u32[]{:S(2)}) collective-permute-start(f32[8,768]{1,0:T(8,128)S(1)} %get-tuple-element.88.refs_0_.emb), channel_id=1, source_target_pairs={{16,0},{32,16},{48,32},{0,48},{80,64},{96,80},{112,96},{64,112},{1... | collective-permute-start | bytes 73736 | tf_op jit(solution)/shard_map/ppermute | solution.py:35
  83.8 5.9 %collective-permute-start.23 = (f32[16,1024]{1,0:T(8,128)S(1)}, f32[16,1024]{1,0:T(8,128)S(1)}, u32[]{:S(2)}, u32[]{:S(2)}) collective-permute-start(f32[16,1024]{1,0:T(8,128)S(1)} %get-tuple-element.93.refs_0_), channel_id=1, source_target_pairs={{8,0},{9,1},{10,2},{11,3},{12,4},{13,5},{14,6},{15,7},{0,8},{1,9},... | collective-permute-start | bytes 196616 | tf_op jit(solution)/shard_map/ppermute | solution.py:31
  84.7 5.6 %collective-permute-start.22 = (f32[16,1024]{1,0:T(8,128)S(1)}, f32[16,1024]{1,0:T(8,128)S(1)}, u32[]{:S(2)}, u32[]{:S(2)}) collective-permute-start(f32[16,1024]{1,0:T(8,128)S(1)} %get-tuple-element.93.refs_0_), channel_id=1, source_target_pairs={{12,0},{13,1},{14,2},{15,3},{0,4},{1,5},{2,6},{3,7},{4,8},{5,9},{6... | collective-permute-start | bytes 196616 | tf_op jit(solution)/shard_map/ppermute | solution.py:31
  86.7 4.3 %collective-permute-start.21 = (f32[16,1024]{1,0:T(8,128)S(1)}, f32[16,1024]{1,0:T(8,128)S(1)}, u32[]{:S(2)}, u32[]{:S(2)}) collective-permute-start(f32[16,1024]{1,0:T(8,128)S(1)} %get-tuple-element.93.refs_0_), channel_id=1, source_target_pairs={{4,0},{5,1},{6,2},{7,3},{8,4},{9,5},{10,6},{11,7},{12,8},{13,9},{1... | collective-permute-start | bytes 196616 | tf_op jit(solution)/shard_map/ppermute | solution.py:31
  91.1 6.1 %collective-permute-start.26 = (f32[16,1024]{1,0:T(8,128)S(1)}, f32[16,1024]{1,0:T(8,128)S(1)}, u32[]{:S(2)}, u32[]{:S(2)}) collective-permute-start(f32[16,1024]{1,0:T(8,128)S(1)} %merge.1.s0), channel_id=1, source_target_pairs={{2,0},{3,1},{0,2},{1,3},{6,4},{7,5},{4,6},{5,7},{10,8},{11,9},{8,1... | collective-permute-start | bytes 196616 | tf_op jit(solution)/shard_map/ppermute | solution.py:45
  93.6 5.5 %collective-permute-start.25 = (f32[16,1024]{1,0:T(8,128)S(1)}, f32[16,1024]{1,0:T(8,128)S(1)}, u32[]{:S(2)}, u32[]{:S(2)}) collective-permute-start(f32[16,1024]{1,0:T(8,128)S(1)} %merge.1.s0), channel_id=1, source_target_pairs={{66,0},{67,1},{64,2},{65,3},{70,4},{71,5},{68,6},{69,7},{74,8},{75... | collective-permute-start | bytes 196616 | tf_op jit(solution)/shard_map/ppermute | solution.py:45
  95.3 4.3 %collective-permute-start.24 = (f32[16,1024]{1,0:T(8,128)S(1)}, f32[16,1024]{1,0:T(8,128)S(1)}, u32[]{:S(2)}, u32[]{:S(2)}) collective-permute-start(f32[16,1024]{1,0:T(8,128)S(1)} %merge.1.s0), channel_id=1, source_target_pairs={{64,0},{65,1},{66,2},{67,3},{68,4},{69,5},{70,6},{71,7},{72,8},{73... | collective-permute-start | bytes 196616 | tf_op jit(solution)/shard_map/ppermute | solution.py:45
  102.3 2.9 %collective-permute-start.27 = (f32[384,768]{1,0:T(8,128)S(1)}, f32[384,768]{1,0:T(8,128)S(1)}, u32[]{:S(2)}, u32[]{:S(2)}) collective-permute-start(f32[384,768]{1,0:T(8,128)S(1)} %get-tuple-element.104), channel_id=1, source_target_pairs={{0,1},{1,0},{2,3},{3,2},{4,5},{5,4},{6,7},{7,6},{8,9},{9,8},{10,11... | collective-permute-start | bytes 3538952 | tf_op jit(solution)/shard_map/ppermute | solution.py:26
  105.4 6.8 %collective-permute-start.28 = (bf16[96,768]{1,0:T(8,128)(2,1)S(1)}, bf16[96,768]{1,0:T(8,128)(2,1)S(1)}, u32[]{:S(2)}, u32[]{:S(2)}) collective-permute-start(bf16[96,768]{1,0:T(8,128)(2,1)S(1)} %get-tuple-element.106), channel_id=1, source_target_pairs={{32,0},{9,1},{34,2},{11,3},{36,4},{13,5},{38,6},{15,7},{40,8},{1,9... | collective-permute-start | bytes 442376 | tf_op jit(solution)/shard_map/ppermute | solution.py:56
  107.0 6.8 %collective-permute-start.29 = (bf16[96,768]{1,0:T(8,128)(2,1)S(1)}, bf16[96,768]{1,0:T(8,128)(2,1)S(1)}, u32[]{:S(2)}, u32[]{:S(2)}) collective-permute-start(bf16[96,768]{1,0:T(8,128)(2,1)S(1)} %get-tuple-element.107), channel_id=1, source_target_pairs={{48,0},{13,1},{50,2},{15,3},{52,4},{1,5},{54,6},{3,7},{56,8},{5,9}... | collective-permute-start | bytes 442376 | tf_op jit(solution)/shard_map/ppermute | solution.py:56
  109.6 5.1 %collective-permute-start.30 = (bf16[96,768]{1,0:T(8,128)(2,1)S(1)}, bf16[96,768]{1,0:T(8,128)(2,1)S(1)}, u32[]{:S(2)}, u32[]{:S(2)}) collective-permute-start(bf16[96,768]{1,0:T(8,128)(2,1)S(1)} %get-tuple-element.108), channel_id=1, source_target_pairs={{16,0},{5,1},{18,2},{7,3},{20,4},{9,5},{22,6},{11,7},{24,8},{13,9}... | collective-permute-start | bytes 442376 | tf_op jit(solution)/shard_map/ppermute | solution.py:56
  114.8 5.9 %collective-permute-start.31 = (f32[24,768]{1,0:T(8,128)S(1)}, f32[24,768]{1,0:T(8,128)S(1)}, u32[]{:S(2)}, u32[]{:S(2)}) collective-permute-start(f32[24,768]{1,0:T(8,128)S(1)} %get-tuple-element.110), channel_id=1, source_target_pairs={{8,0},{33,1},{10,2},{35,3},{12,4},{37,5},{14,6},{39,7},{0,8},{41,9... | collective-permute-start | bytes 221192 | tf_op jit(solution)/shard_map/ppermute | solution.py:56
  115.9 5.6 %collective-permute-start.32 = (f32[24,768]{1,0:T(8,128)S(1)}, f32[24,768]{1,0:T(8,128)S(1)}, u32[]{:S(2)}, u32[]{:S(2)}) collective-permute-start(f32[24,768]{1,0:T(8,128)S(1)} %get-tuple-element.111), channel_id=1, source_target_pairs={{12,0},{49,1},{14,2},{51,3},{0,4},{53,5},{2,6},{55,7},{4,8},{57,9}... | collective-permute-start | bytes 221192 | tf_op jit(solution)/shard_map/ppermute | solution.py:56
  118.4 4.4 %collective-permute-start.33 = (f32[24,768]{1,0:T(8,128)S(1)}, f32[24,768]{1,0:T(8,128)S(1)}, u32[]{:S(2)}, u32[]{:S(2)}) collective-permute-start(f32[24,768]{1,0:T(8,128)S(1)} %get-tuple-element.112), channel_id=1, source_target_pairs={{4,0},{17,1},{6,2},{19,3},{8,4},{21,5},{10,6},{23,7},{12,8},{25,9}... | collective-permute-start | bytes 221192 | tf_op jit(solution)/shard_map/ppermute | solution.py:56
  122.8 5.4 %collective-permute-start.34 = (f32[6,768]{1,0:T(8,128)S(1)}, f32[6,768]{1,0:T(8,128)S(1)}, u32[]{:S(2)}, u32[]{:S(2)}) collective-permute-start(f32[6,768]{1,0:T(8,128)S(1)} %get-tuple-element.114), channel_id=1, source_target_pairs={{2,0},{3,1},{0,2},{1,3},{6,4},{7,5},{4,6},{5,7},{10,8},{11,9},{8,1... | collective-permute-start | bytes 55304 | tf_op jit(solution)/shard_map/ppermute | solution.py:45
  124.3 5.0 %collective-permute-start.35 = (f32[6,768]{1,0:T(8,128)S(1)}, f32[6,768]{1,0:T(8,128)S(1)}, u32[]{:S(2)}, u32[]{:S(2)}) collective-permute-start(f32[6,768]{1,0:T(8,128)S(1)} %get-tuple-element.115), channel_id=1, source_target_pairs={{66,0},{67,1},{64,2},{65,3},{70,4},{71,5},{68,6},{69,7},{74,8},{75... | collective-permute-start | bytes 55304 | tf_op jit(solution)/shard_map/ppermute | solution.py:45
  126.9 3.8 %collective-permute-start.36 = (f32[6,768]{1,0:T(8,128)S(1)}, f32[6,768]{1,0:T(8,128)S(1)}, u32[]{:S(2)}, u32[]{:S(2)}) collective-permute-start(f32[6,768]{1,0:T(8,128)S(1)} %get-tuple-element.116), channel_id=1, source_target_pairs={{64,0},{65,1},{66,2},{67,3},{68,4},{69,5},{70,6},{71,7},{72,8},{73... | collective-permute-start | bytes 55304 | tf_op jit(solution)/shard_map/ppermute | solution.py:45

commit v4 on v3

--- a/solution.py
+++ b/solution.py
@@ -26,38 +26,42 @@
     return lax.ppermute(value, axis, [(i, i ^ bits) for i in range(lax.axis_size(axis))])
 
 
-def from_x(value, k):
-    size = lax.axis_size("ctx")
-    return lax.ppermute(value, "ctx", [((c + 4 * k) % size, c) for c in range(size)])
-
-
-def from_y(value, k):
-    return lax.ppermute(value, "dp", [((d & 4) | ((d + k) & 3), d) for d in range(lax.axis_size("dp"))])
-
-
-def from_z(value, k):
+def fetched(value, source, cores=(0, 1)):
     n_dp, n_ctx = lax.axis_size("dp"), lax.axis_size("ctx")
     pairs = []
     for d in range(n_dp):
         for c in range(n_ctx):
-            z = ((c & 2) + (d >> 2) + k) & 3
-            pairs.append((((z & 1) * 4 + (d & 3)) * n_ctx + (c & ~2) + (z & 2), d * n_ctx + c))
+            where = source(d, c) if c % 2 in cores else (d, c)
+            pairs.append((where[0] * n_ctx + where[1], d * n_ctx + c))
     return lax.ppermute(value, ("dp", "ctx"), pairs)
 
 
-def from_plane(value, k, last):
-    n_dp, n_ctx = lax.axis_size("dp"), lax.axis_size("ctx")
-    pairs = []
-    for d in range(n_dp):
-        for c in range(n_ctx):
-            along_y = (c & 1 == 1) == last
-            source = ((d & 4) | ((d + k) & 3), c) if along_y else (d, (c + 4 * k) % n_ctx)
-            pairs.append((source[0] * n_ctx + source[1], d * n_ctx + c))
-    return lax.ppermute(value, ("dp", "ctx"), pairs)
-
-
-def around(value, fetch):
-    return [value] + [fetch(value, k) for k in ORDER[1:]]
+def at_x(k):
+    return lambda d, c: (d, (c + 4 * k) % 16)
+
+
+def at_y(k):
+    return lambda d, c: ((d & 4) | ((d + k) & 3), c)
+
+
+def at_z(k):
+    def place(d, c):
+        z = ((c & 2) + (d >> 2) + k) & 3
+        return (z & 1) * 4 + (d & 3), (c & ~2) + (z & 2)
+
+    return place
+
+
+def at_plane(k, last):
+    return lambda d, c: (at_y(k) if (c & 1 == 1) == last else at_x(k))(d, c)
+
+
+def around(value, at, cores=(0, 1)):
+    return [value] + [fetched(value, at(k), cores) for k in ORDER[1:]]
+
+
+def dealt(pieces, at):
+    return [fetched(pieces[k - 1], at(-k)) for k in (2, 1, 3)]
 
 
 def here():
@@ -66,10 +70,6 @@
 
 def in_hbm(value):
     return pltpu.with_memory_space_constraint(value, pltpu.HBM)
-
-
-def dealt(pieces, fetch):
-    return [fetch(pieces[k - 1], -k) for k in (2, 1, 3)]
 
 
 def call(kernel, out_shape, in_specs, out_specs, limit=16, flops=0, moved=0, **keywords):
@@ -325,7 +325,7 @@
 
 def turn_kernel(mixed, out):
     width = out.shape[0]
-    rows = 192
+    rows = 384
     lax.fori_loop(0, width // rows, lambda index, _: turn_rows(index * rows, rows, mixed, out), None)
 
 
@@ -437,16 +437,33 @@
     stats[...] = jnp.concatenate([top, total] * 4, axis=0)
 
 
+def pack_kernel(s0, s1, s2, s3, emb, rinv, everyone, target, product, stats, out):
+    group, width = emb.shape
+    all_docs = everyone.shape[0]
+    out[0 : 2 * group, :] = merge(group, width, [s[...] for s in (s0, s1, s2, s3)])
+    for low, rows in ((2 * group, emb), (3 * group, target)):
+        out[low : low + group, 0:width] = rows[...]
+    out[4 * group :, 0:width] = everyone[...]
+    out[2 * group :, width:] = jnp.zeros((2 * group + all_docs, 256), jnp.float32)
+    out[2 * group : 3 * group, width : width + 128] = rinv[...]
+    out[2 * group : 3 * group, width + 128 : width + 128 + all_docs] = product[...]
+    out[3 * group : 4 * group, width + 128 : width + 128 + all_docs] = stats[...]
+
+
 def grad_kernel(
-    lengths, s0, s1, s2, s3, emb, rinv, everyone, target, product, stats, gain, normed, rstd, turned,
-    send_out, d_summed, loss_out,
+    lengths, packed, other, gain, normed, rstd, turned, send_out, d_summed, loss_out,
 ):
     docs, tb, width = normed.shape
-    all_docs, group = everyone.shape[0], emb.shape[0]
-    dp, _ = here()
+    group = 2 * docs
+    all_docs = packed.shape[0] - 4 * group
+    dp, ctx = here()
+    known = jnp.where(lax.rem(ctx, 2) == 1, packed[...], other[...])
+    now, emb, target = known[0 : 2 * group], known[2 * group : 3 * group], known[3 * group : 4 * group]
+    rinv, scored = emb[:, width : width + 128], emb[:, width + 128 : width + 128 + all_docs]
+    stats = target[:, width + 128 : width + 128 + all_docs]
+    emb, target, others = emb[:, 0:width], target[:, 0:width], known[4 * group :, 0:width]
     mine = lambda a: jnp.where(dp >= 4, a[docs:group], a[0:docs])
-    own, others = mine(emb), everyone[...]
-    now = merge(group, width, [s[...] for s in (s0, s1, s2, s3)])
+    own = mine(emb)
     total, top, found = (now[group + k : group + k + 1, 0:all_docs] for k in range(3))
     batch_top, batch_total = stats[0:1], stats[1:2]
     peak = jnp.maximum(top, batch_top)
@@ -456,7 +473,7 @@
     first = (dp & 3) * group + (dp >> 2) * docs
     same = column == lax.broadcasted_iota(jnp.int32, (docs, all_docs), 0) + first
     lse = jnp.sum(jnp.where(same, lse_row, 0.0), axis=1, keepdims=True)
-    scores = mine(product)
+    scores = mine(scored)
     g_batch = jnp.where(same, 0.0, jnp.exp(scores - lse) + jnp.exp(scores - lse_row)) / all_docs
     shares = mine(now)
     mix = shares[:, 0:width] * jnp.exp(shares[:, width + 128 : width + 129] - lse)
@@ -516,7 +533,7 @@
     fetch = lambda part: lax.ppermute(part, "ctx", ring)
     early, middle, late = fetch(tokens[0:1]), fetch(tokens[1:3]), tokens[3:]
     near = swap(tokens, "ctx", 1)
-    tables = around(cache, from_y)
+    tables = around(cache, at_y)
     qk, v_turned, w_v_turned = prepare(in_hbm(tokens), in_hbm(w_qkv))
     near_k, near_v = call(
         near_kernel,
@@ -556,7 +573,7 @@
         pool, target
     )
     sums = add([sums, swap(sums, "ctx", 1)])
-    sums = add(around(sums, from_x))
+    sums = add(around(sums, at_x, (1,)))
     sums, turned = lax.optimization_barrier((sums, turned))
     emb, rinv, target = call(
         norm_kernel,
@@ -565,8 +582,8 @@
         (VMEM,) * 3,
         limit=4,
         name="norm",
-    )(*around(sums, from_z))
-    embs = around(emb, from_y)
+    )(*around(sums, at_z, (1,)))
+    embs = around(emb, at_y, (1,))
     everyone, state = call(
         functools.partial(score_kernel, docs),
         (f32(all_docs, width), f32(2 * group, width + 256)),
@@ -584,18 +601,26 @@
         limit=4,
         name="batch",
     )(emb, everyone)
-    state = merged(group, width, around(state, from_x))
+    state = merged(group, width, around(state, at_x, (1,)))
+    packed = call(
+        pack_kernel,
+        f32(4 * group + all_docs, width + 256),
+        [VMEM] * 10,
+        VMEM,
+        limit=4,
+        name="pack",
+    )(*around(state, at_z, (1,)), emb, rinv, everyone, target, product, stats)
     half = width // 2
     send, d_summed, loss = call(
         grad_kernel,
         (f32(half, width), bf16(docs * tb, width), f32(8, 128)),
-        [SMEM] + [VMEM] * 14,
+        [SMEM] + [VMEM] * 6,
         (VMEM,) * 3,
         flops=docs * tb * width * width,
         moved=8 * 2**20,
         name="grad",
     )(
-        lengths, *around(state, from_z), emb, rinv, everyone, target, product, stats, gain, normed, rstd, turned,
+        lengths, packed, swap(packed, "ctx", 1), gain, normed, rstd, turned,
     )
     keep = call(
         keep_kernel,
@@ -607,11 +632,11 @@
         name="keep",
     )(turned, d_summed)
     keep, *sends = sum_and_split([keep, swap(send, "ctx", 1)], jnp.bfloat16)
-    got = dealt(sends, lambda piece, k: from_plane(piece, k, False))
+    got = dealt(sends, lambda k: at_plane(k, False))
     keep, *sends = sum_and_split([keep] + got, jnp.float32)
-    got = dealt(sends, lambda piece, k: from_plane(piece, k, True))
+    got = dealt(sends, lambda k: at_plane(k, True))
     keep, *sends = sum_and_split([keep] + got, jnp.float32)
-    got = dealt(sends, from_z)
+    got = dealt(sends, at_z)
     return (hidden, loss[0, 0], add([keep] + got))
 
 

time: 132 us -> 154 us (1.17)
  starting transfers between devices: 59.7 us -> 90.7 us
  waiting for transfers between devices: 23.8 us -> 14.7 us
    ppermute x7 -> x8, starting transfers between devices: 4.84 us -> 48.8 us  [swap(): lax.ppermute(value, axis, [(i, i ^ bits) for i in range(lax.axis_size(axi...]
    ppermute x27, starting transfers between devices: 43.6 us -> 30.6 us  [fetched(): return lax.ppermute(value, ('dp', 'ctx'), pairs)]
    ppermute x27, waiting for transfers between devices: 20.1 us -> 10.2 us  [fetched(): return lax.ppermute(value, ('dp', 'ctx'), pairs)]
    ppermute x7 -> x8, waiting for transfers between devices: 3.72 us -> 4.5 us  [swap(): lax.ppermute(value, axis, [(i, i ^ bits) for i in range(lax.axis_size(axi...]
  transfers between devices with their start and end apart: 37 -> 38, of which waited for: 23 -> 14; matrix products, arithmetic and copies ran while one was open for 1% -> 1% of each run, Pallas kernels for 25% -> 22%
where the time goes in v4:
time: 154 us; the launch traced here: 153 us
  starting transfers between devices  90.7 us (59%)
  Pallas kernels  44.7 us (29%)
  waiting for transfers between devices  14.7 us (10%)
  local copies, waits for them, and re-layouts  1.77 us (1%)
    ppermute x8, starting transfers between devices, swap(): lax.ppermute(value, axis, [(i, i ^ bits) for i in range(lax.axis_size(axi...  48.8 us
    ppermute x27, starting transfers between devices, fetched(): return lax.ppermute(value, ('dp', 'ctx'), pairs)  30.6 us
    pallas_call x3, Pallas kernels, attend(): call(functools.partial(attend_kernel, first), out_shape, in_specs, out_sp...  23.9 us
    ppermute x3, starting transfers between devices, shards(): fetch = lambda part: lax.ppermute(part, 'ctx', ring)  11.3 us
    ppermute x27, waiting for transfers between devices, fetched(): return lax.ppermute(value, ('dp', 'ctx'), pairs)  10.2 us
    pallas_call x1, Pallas kernels, prepare(): call(prepare_kernel, (bf16(docs, tb, 2 * width), bf16(width, docs * tb),...  7.17 us
    ppermute x8, waiting for transfers between devices, swap(): lax.ppermute(value, axis, [(i, i ^ bits) for i in range(lax.axis_size(axi...  4.5 us
    pallas_call x1, Pallas kernels, shards(): call(near_kernel, (bf16(docs, tb, width), bf16(width, docs * tb)), [VMEM]...  3.13 us
  transfers between devices with their start and end apart: 38, of which 14 were waited for; matrix products, arithmetic and copies ran while one was open for 1% of the time, Pallas kernels for 22%

profile of v4, /device:TPU:0, one launch (start us, length us, event | category | flops | bytes accessed | tf_op | source)
XLA Modules:
  0.0 153.0 jit_solution(10710897465962839242)
XLA Ops:
  0.7 1.7 %collective-permute-start.4 = (bf16[128,768]{1,0:T(8,128)(2,1)}, bf16[128,768]{1,0:T(8,128)(2,1)S(1)}, u32[]{:S(2)}, u32[]{:S(2)}) collective-permute-start(bf16[128,768]{1,0:T(8,128)(2,1)} %refs_4_), channel_id=1, source_target_pairs={{48,0},{49,1},{50,2},{51,3},{52,4},{53,5},{54,6},{55,7},{56,8},{57... | collective-permute-start | bytes 589832 | tf_op jit(solution)/shard_map/ppermute | solution.py:36
  2.5 1.6 %collective-permute-start.3 = (bf16[128,768]{1,0:T(8,128)(2,1)}, bf16[128,768]{1,0:T(8,128)(2,1)S(1)}, u32[]{:S(2)}, u32[]{:S(2)}) collective-permute-start(bf16[128,768]{1,0:T(8,128)(2,1)} %refs_4_), channel_id=1, source_target_pairs={{16,0},{17,1},{18,2},{19,3},{20,4},{21,5},{22,6},{23,7},{24,8},{25... | collective-permute-start | bytes 589832 | tf_op jit(solution)/shard_map/ppermute | solution.py:36
  4.0 1.2 fusion
  5.2 5.8 %collective-permute-start.2 = (bf16[1,256,768]{2,1,0:T(8,128)(2,1)S(1)}, bf16[1,256,768]{2,1,0:T(8,128)(2,1)S(1)}, u32[]{:S(2)}, u32[]{:S(2)}) collective-permute-start(bf16[1,256,768]{2,1,0:T(8,128)(2,1)S(1)} %get-tuple-element.117), channel_id=1, source_target_pairs={{0,15},{1,2},{2,1},{3,4},{4,3},{5,6},{6,5},{7,8},{8,7},{9,10},{10,... | collective-permute-start | bytes 1179656 | tf_op jit(solution)/shard_map/ppermute | solution.py:533
  11.2 7.2 %prepare.1 = (bf16[4,256,1536]{2,1,0:T(8,128)(2,1)S(1)}, bf16[768,1024]{1,0:T(8,128)(2,1)S(1)}, bf16[768,768]{1,0:T(8,128)(2,1)S(1)}) custom-call(bf16[4,256,768]{2,1,0:T(8,128)(2,1)} %refs_1_.5, bf16[768,2304]{1,0:T(8,128)(2,1)} %refs_7_.5), custom_call_target="tpu_custom_call" | custom-call | flops 3623878656 | bytes 11534336 | tf_op jit(solution)/shard_map/prepare/pallas_call | solution.py:259
  18.4 2.0 %collective-permute-start.5 = (bf16[128,768]{1,0:T(8,128)(2,1)S(1)}, bf16[128,768]{1,0:T(8,128)(2,1)S(1)}, u32[]{:S(2)}, u32[]{:S(2)}) collective-permute-start(bf16[128,768]{1,0:T(8,128)(2,1)S(1)} %copy-done.4), channel_id=1, source_target_pairs={{32,0},{33,1},{34,2},{35,3},{36,4},{37,5},{38,6},{39,7},{40,8},{41... | collective-permute-start | bytes 589832 | tf_op jit(solution)/shard_map/ppermute | solution.py:36
  20.4 3.1 %near.1 = (bf16[4,256,768]{2,1,0:T(8,128)(2,1)S(1)}, bf16[768,1024]{1,0:T(8,128)(2,1)S(1)}) custom-call(bf16[4,256,768]{2,1,0:T(8,128)(2,1)S(1)} %collective-permute-done.near, bf16[768,2304]{1,0:T(8,128)(2,1)S(1)} %copy-done, bf16[768,768]{1,0:T(8,128)(2,1)S(1)} %get-tuple-element.60.w_v_turned.refs_8_), custom_call_target="tpu_custom_call" | custom-call | flops 2415919104 | bytes 4194304 | tf_op jit(solution)/shard_map/near/pallas_call | solution.py:538
  23.6 6.1 %attend.3 = (bf16[4,256,768]{2,1,0:T(8,128)(2,1)}, bf16[768,1024]{1,0:T(8,128)(2,1)S(1)}, bf16[4,256,768]{2,1,0:T(8,128)(2,1)S(1)}, f32[4,256,128]{2,1,0:T(8,128)S(1)}, f32[4,1,768]{2,1,0:T(1,128)S(1)}) custom-call(s32[4]{0:T(128)S(1)} %copy-done.6, bf16[4,256,768]{2,1,0:T(8,128)(2,1)S(1)} %copy-done.2, bf16[4,256,768]{2,1,0:T(8,128)(2,1)S(1)} %get-tuple-element.61.refs_2_, ...), custom_call_target="tpu_custom_call" | custom-call | flops 1509949440 | bytes 4194304 | tf_op jit(solution)/shard_map/attend/pallas_call | solution.py:211
  29.7 4.0 %collective-permute-start.6 = (bf16[128,768]{1,0:T(8,128)(2,1)S(1)}, bf16[128,768]{1,0:T(8,128)(2,1)S(1)}, u32[]{:S(2)}, u32[]{:S(2)}) collective-permute-start(bf16[128,768]{1,0:T(8,128)(2,1)S(1)} %copy-done.4), channel_id=1, source_target_pairs={{0,1},{1,0},{2,3},{3,2},{4,5},{5,4},{6,7},{7,6},{8,9},{9,8},{10,11... | collective-permute-start | bytes 589832 | tf_op jit(solution)/shard_map/ppermute | solution.py:26
  34.3 0.7 target.1
  35.7 5.4 %collective-permute-start.10 = (bf16[1,256,768]{2,1,0:T(8,128)(2,1)S(1)}, bf16[1,256,768]{2,1,0:T(8,128)(2,1)S(1)}, u32[]{:S(2)}, u32[]{:S(2)}) collective-permute-start(bf16[1,256,768]{2,1,0:T(8,128)(2,1)S(1)} %get-tuple-element.71), channel_id=1, source_target_pairs={{0,15},{1,2},{2,1},{3,4},{4,3},{5,6},{6,5},{7,8},{8,7},{9,10},{10,... | collective-permute-start | bytes 1179656 | tf_op jit(solution)/shard_map/ppermute | solution.py:533
  41.2 11.7 %attend.4 = (bf16[4,256,768]{2,1,0:T(8,128)(2,1)}, bf16[768,1024]{1,0:T(8,128)(2,1)S(1)}, bf16[4,256,768]{2,1,0:T(8,128)(2,1)S(1)}, f32[4,256,128]{2,1,0:T(8,128)S(1)}, f32[4,1,768]{2,1,0:T(1,128)S(1)}) custom-call(s32[4]{0:T(128)S(1)} %copy-done.6, ...), custom_call_target="tpu_custom_call", output_to_operand_aliasing={{0}: (11, {}), {1}: (12, {}), {2}: (13, {}), {3}: (14, {}),... | custom-call | flops 3019898880 | bytes 4194304 | tf_op jit(solution)/shard_map/attend/pallas_call | solution.py:211
  52.9 6.1 %attend.5 = (bf16[4,256,768]{2,1,0:T(8,128)(2,1)}, bf16[768,1024]{1,0:T(8,128)(2,1)S(1)}, bf16[4,256,768]{2,1,0:T(8,128)(2,1)S(1)}, f32[4,256,128]{2,1,0:T(8,128)S(1)}, f32[4,1,768]{2,1,0:T(1,128)S(1)}) custom-call(s32[4]{0:T(128)S(1)} %copy-done.6, ...), custom_call_target="tpu_custom_call", output_to_operand_aliasing={{0}: (11, {}), {1}: (12, {}), {2}: (13, {}), {3}: (14, {}),... | custom-call | flops 1509949440 | bytes 4194304 | tf_op jit(solution)/shard_map/attend/pallas_call | solution.py:211
  59.1 1.2 collective-permute-done.11.refs_1_
  61.0 0.7 collective-permute-start.13
  61.7 0.7 collective-permute-start.12
  62.3 2.9 %turn.1.turned = bf16[768,1024]{1,0:T(8,128)(2,1)S(1)} custom-call(bf16[768,1024]{1,0:T(8,128)(2,1)S(1)} %get-tuple-element.86.mixed), custom_call_target="tpu_custom_call" | custom-call | flops 1207959552 | bytes 4194304 | tf_op jit(solution)/shard_map/turn/pallas_call | solution.py:561
  65.3 0.7 collective-permute-start.17
  65.9 0.7 collective-permute-start.16
  69.5 1.7 %score.1 = (f32[32,768]{1,0:T(8,128)S(1)}, f32[16,1024]{1,0:T(8,128)S(1)}) custom-call(s32[32]{0:T(128)S(1)} %copy-done.7, f32[8,768]{1,0:T(8,128)S(1)} %get-tuple-element.88.refs_0_.emb, f32[8,768]{1,0:T(8,128)S(1)} %collective-permute-done.18.refs_1_, f32[8,768]{1,0:T(8,128)S(1)} %collective-permute-done.19.refs_2_, ...), custom_call_target="tpu_custom_call" | custom-call | bytes 2097152 | tf_op jit(solution)/shard_map/score/pallas_call | solution.py:587
  71.2 0.7 collective-permute-start.23
  71.9 0.7 collective-permute-start.22
  72.5 0.7 collective-permute-start.21
  73.4 0.7 collective-permute-start.26
  74.0 0.7 collective-permute-start.25
  74.7 0.9 collective-permute-start.24
  76.1 43.6 %collective-permute-start.27 = (f32[64,1024]{1,0:T(8,128)S(1)}, f32[64,1024]{1,0:T(8,128)S(1)}, u32[]{:S(2)}, u32[]{:S(2)}) collective-permute-start(f32[64,1024]{1,0:T(8,128)S(1)} %pack.1.packed), channel_id=1, source_target_pairs={{0,1},{1,0},{2,3},{3,2},{4,5},{5,4},{6,7},{7,6},{8,9},{9,8},{10,11... | collective-permute-start | bytes 786440 | tf_op jit(solution)/shard_map/ppermute | solution.py:26
  119.6 1.2 collective-permute-done.27.other
  120.8 2.7 %grad.1 = (f32[384,768]{1,0:T(8,128)S(1)}, bf16[1024,768]{1,0:T(8,128)(2,1)S(1)}, f32[8,128]{1,0:T(8,128)S(1)}) custom-call(s32[4]{0:T(128)S(1)} %copy-done.6, f32[64,1024]{1,0:T(8,128)S(1)} %pack.1.packed, f32[64,1024]{1,0:T(8,128)S(1)} %collective-permute-done.27.other, f32[768]{0:T(1024)S(1)} %copy-done.5, ...), custom_call_target="tpu_custom_call" | custom-call | flops 603979776 | bytes 8388608 | tf_op jit(solution)/shard_map/grad/pallas_call | solution.py:614
  124.0 1.0 keep.1.refs_0_
  125.0 1.5 collective-permute-done.28.refs_1_
  126.6 1.8 %collective-permute-start.29 = (bf16[96,768]{1,0:T(8,128)(2,1)S(1)}, bf16[96,768]{1,0:T(8,128)(2,1)S(1)}, u32[]{:S(2)}, u32[]{:S(2)}) collective-permute-start(bf16[96,768]{1,0:T(8,128)(2,1)S(1)} %get-tuple-element.106), channel_id=1, source_target_pairs={{32,0},{9,1},{34,2},{11,3},{36,4},{13,5},{38,6},{15,7},{40,8},{1,9... | collective-permute-start | bytes 442376 | tf_op jit(solution)/shard_map/ppermute | solution.py:36
  128.4 2.3 %collective-permute-start.30 = (bf16[96,768]{1,0:T(8,128)(2,1)S(1)}, bf16[96,768]{1,0:T(8,128)(2,1)S(1)}, u32[]{:S(2)}, u32[]{:S(2)}) collective-permute-start(bf16[96,768]{1,0:T(8,128)(2,1)S(1)} %get-tuple-element.107), channel_id=1, source_target_pairs={{48,0},{13,1},{50,2},{15,3},{52,4},{1,5},{54,6},{3,7},{56,8},{5,9}... | collective-permute-start | bytes 442376 | tf_op jit(solution)/shard_map/ppermute | solution.py:36
  130.7 0.9 collective-permute-start.31
  131.6 1.7 %collective-permute-done.29.refs_1_ = bf16[96,768]{1,0:T(8,128)(2,1)S(1)} collective-permute-done((bf16[96,768]{1,0:T(8,128)(2,1)S(1)}, bf16[96,768]{1,0:T(8,128)(2,1)S(1)}, u32[]{:S(2)}, u32[]{:S(2)}) %collective-permute-start.29) | collective-permute-done | bytes 147488 | tf_op jit(solution)/shard_map/ppermute | solution.py:36
  133.3 1.6 %collective-permute-done.30.refs_2_ = bf16[96,768]{1,0:T(8,128)(2,1)S(1)} collective-permute-done((bf16[96,768]{1,0:T(8,128)(2,1)S(1)}, bf16[96,768]{1,0:T(8,128)(2,1)S(1)}, u32[]{:S(2)}, u32[]{:S(2)}) %collective-permute-start.30) | collective-permute-done | bytes 147488 | tf_op jit(solution)/shard_map/ppermute | solution.py:36
  134.9 1.0 collective-permute-done.31.refs_3_
  135.9 1.7 %collective-permute-start.32 = (f32[24,768]{1,0:T(8,128)S(1)}, f32[24,768]{1,0:T(8,128)S(1)}, u32[]{:S(2)}, u32[]{:S(2)}) collective-permute-start(f32[24,768]{1,0:T(8,128)S(1)} %get-tuple-element.110), channel_id=1, source_target_pairs={{8,0},{33,1},{10,2},{35,3},{12,4},{37,5},{14,6},{39,7},{0,8},{41,9... | collective-permute-start | bytes 221192 | tf_op jit(solution)/shard_map/ppermute | solution.py:36
  137.6 2.3 %collective-permute-start.33 = (f32[24,768]{1,0:T(8,128)S(1)}, f32[24,768]{1,0:T(8,128)S(1)}, u32[]{:S(2)}, u32[]{:S(2)}) collective-permute-start(f32[24,768]{1,0:T(8,128)S(1)} %get-tuple-element.111), channel_id=1, source_target_pairs={{12,0},{49,1},{14,2},{51,3},{0,4},{53,5},{2,6},{55,7},{4,8},{57,9}... | collective-permute-start | bytes 221192 | tf_op jit(solution)/shard_map/ppermute | solution.py:36
  140.0 0.9 collective-permute-start.34
  140.9 1.0 collective-permute-done.32.refs_1_
  141.9 1.3 collective-permute-done.33.refs_2_
  143.2 1.1 collective-permute-done.34.refs_3_
  144.4 1.9 %collective-permute-start.35 = (f32[6,768]{1,0:T(8,128)S(1)}, f32[6,768]{1,0:T(8,128)S(1)}, u32[]{:S(2)}, u32[]{:S(2)}) collective-permute-start(f32[6,768]{1,0:T(8,128)S(1)} %get-tuple-element.114), channel_id=1, source_target_pairs={{2,0},{3,1},{0,2},{1,3},{6,4},{7,5},{4,6},{5,7},{10,8},{11,9},{8,1... | collective-permute-start | bytes 55304 | tf_op jit(solution)/shard_map/ppermute | solution.py:36
  146.2 2.3 %collective-permute-start.36 = (f32[6,768]{1,0:T(8,128)S(1)}, f32[6,768]{1,0:T(8,128)S(1)}, u32[]{:S(2)}, u32[]{:S(2)}) collective-permute-start(f32[6,768]{1,0:T(8,128)S(1)} %get-tuple-element.115), channel_id=1, source_target_pairs={{66,0},{67,1},{64,2},{65,3},{70,4},{71,5},{68,6},{69,7},{74,8},{75... | collective-permute-start | bytes 55304 | tf_op jit(solution)/shard_map/ppermute | solution.py:36
  148.6 0.9 collective-permute-start.37
  150.0 1.3 collective-permute-done.36.refs_2_
  151.3 1.1 collective-permute-done.37.refs_3_
  (68 shorter events, 7.5 us)
Async XLA Ops:
  0.6 10.3 %copy-start.1 = (bf16[4,256,768]{2,1,0:T(8,128)(2,1)S(1)}, bf16[4,256,768]{2,1,0:T(8,128)(2,1)}, u32[]{:S(2)}) copy-start(bf16[4,256,768]{2,1,0:T(8,128)(2,1)} %refs_1_.5) | copy-start | bytes 4718596
  0.6 17.7 %collective-permute-start = (bf16[4,256,768]{2,1,0:T(8,128)(2,1)}, bf16[4,256,768]{2,1,0:T(8,128)(2,1)S(1)}, u32[]{:S(2)}, u32[]{:S(2)}) collective-permute-start(bf16[4,256,768]{2,1,0:T(8,128)(2,1)} %refs_1_.5), channel_id=1, source_target_pairs={{0,1},{1,0},{2,3},{3,2},{4,5},{5,4},{6,7},{7,6},{8,9},{9,8},{10,11... | collective-permute-start | bytes 4718600 | tf_op jit(solution)/shard_map/ppermute | solution.py:26
  0.7 29.0 %collective-permute-start.4 = (bf16[128,768]{1,0:T(8,128)(2,1)}, bf16[128,768]{1,0:T(8,128)(2,1)S(1)}, u32[]{:S(2)}, u32[]{:S(2)}) collective-permute-start(bf16[128,768]{1,0:T(8,128)(2,1)} %refs_4_), channel_id=1, source_target_pairs={{48,0},{49,1},{50,2},{51,3},{52,4},{53,5},{54,6},{55,7},{56,8},{57... | collective-permute-start | bytes 589832 | tf_op jit(solution)/shard_map/ppermute | solution.py:36
  2.5 27.3 %collective-permute-start.3 = (bf16[128,768]{1,0:T(8,128)(2,1)}, bf16[128,768]{1,0:T(8,128)(2,1)S(1)}, u32[]{:S(2)}, u32[]{:S(2)}) collective-permute-start(bf16[128,768]{1,0:T(8,128)(2,1)} %refs_4_), channel_id=1, source_target_pairs={{16,0},{17,1},{18,2},{19,3},{20,4},{21,5},{22,6},{23,7},{24,8},{25... | collective-permute-start | bytes 589832 | tf_op jit(solution)/shard_map/ppermute | solution.py:36
  5.2 18.3 %collective-permute-start.2 = (bf16[1,256,768]{2,1,0:T(8,128)(2,1)S(1)}, bf16[1,256,768]{2,1,0:T(8,128)(2,1)S(1)}, u32[]{:S(2)}, u32[]{:S(2)}) collective-permute-start(bf16[1,256,768]{2,1,0:T(8,128)(2,1)S(1)} %get-tuple-element.117), channel_id=1, source_target_pairs={{0,15},{1,2},{2,1},{3,4},{4,3},{5,6},{6,5},{7,8},{8,7},{9,10},{10,... | collective-permute-start | bytes 1179656 | tf_op jit(solution)/shard_map/ppermute | solution.py:533
  11.0 7.3 %copy-start.4 = (bf16[128,768]{1,0:T(8,128)(2,1)S(1)}, bf16[128,768]{1,0:T(8,128)(2,1)}, u32[]{:S(2)}) copy-start(bf16[128,768]{1,0:T(8,128)(2,1)} %refs_4_) | copy-start | bytes 589828
  11.0 9.3 %copy-start = (bf16[768,2304]{1,0:T(8,128)(2,1)S(1)}, bf16[768,2304]{1,0:T(8,128)(2,1)}, u32[]{:S(2)}) copy-start(bf16[768,2304]{1,0:T(8,128)(2,1)} %refs_7_.5) | copy-start | bytes 10616836
  11.1 24.0 %collective-permute-start.1 = (bf16[2,256,768]{2,1,0:T(8,128)(2,1)S(1)}, bf16[2,256,768]{2,1,0:T(8,128)(2,1)S(1)}, u32[]{:S(2)}, u32[]{:S(2)}) collective-permute-start(bf16[2,256,768]{2,1,0:T(8,128)(2,1)S(1)} %slice.12), channel_id=1, source_target_pairs={{0,15},{1,2},{2,1},{3,4},{4,3},{5,6},{6,5},{7,8},{8,7},{9,10},{10,... | collective-permute-start | bytes 2359304 | tf_op jit(solution)/shard_map/ppermute | solution.py:533
  18.4 11.4 %collective-permute-start.5 = (bf16[128,768]{1,0:T(8,128)(2,1)S(1)}, bf16[128,768]{1,0:T(8,128)(2,1)S(1)}, u32[]{:S(2)}, u32[]{:S(2)}) collective-permute-start(bf16[128,768]{1,0:T(8,128)(2,1)S(1)} %copy-done.4), channel_id=1, source_target_pairs={{32,0},{33,1},{34,2},{35,3},{36,4},{37,5},{38,6},{39,7},{40,8},{41... | collective-permute-start | bytes 589832 | tf_op jit(solution)/shard_map/ppermute | solution.py:36
  20.4 3.2 %copy-start.2 = (bf16[4,256,768]{2,1,0:T(8,128)(2,1)S(1)}, bf16[4,256,768]{2,1,0:T(8,128)(2,1)}, u32[]{:S(2)}) copy-start(bf16[4,256,768]{2,1,0:T(8,128)(2,1)} %refs_1_.5) | copy-start | bytes 4718596
  20.4 3.2 %copy-start.3 = (bf16[768,768]{1,0:T(8,128)(2,1)S(1)}, bf16[768,768]{1,0:T(8,128)(2,1)}, u32[]{:S(2)}) copy-start(bf16[768,768]{1,0:T(8,128)(2,1)} %refs_9_.5) | copy-start | bytes 3538948
  20.4 3.2 %copy-start.5 = (f32[768]{0:T(1024)S(1)}, f32[768]{0:T(1024)}, u32[]{:S(2)}) copy-start(f32[768]{0:T(1024)} %gain.1) | copy-start | bytes 9220
  20.4 3.2 %copy-start.6 = (s32[4]{0:T(128)S(1)}, s32[4]{0:T(128)}, u32[]{:S(2)}) copy-start(s32[4]{0:T(128)} %lengths.1) | copy-start | bytes 52
  23.6 10.7 %copy-start.7 = (s32[32]{0:T(128)S(1)}, s32[32]{0:T(128)}, u32[]{:S(2)}) copy-start(s32[32]{0:T(128)} %positive.2) | copy-start | bytes 388
  29.7 5.3 %collective-permute-start.6 = (bf16[128,768]{1,0:T(8,128)(2,1)S(1)}, bf16[128,768]{1,0:T(8,128)(2,1)S(1)}, u32[]{:S(2)}, u32[]{:S(2)}) collective-permute-start(bf16[128,768]{1,0:T(8,128)(2,1)S(1)} %copy-done.4), channel_id=1, source_target_pairs={{0,1},{1,0},{2,3},{3,2},{4,5},{5,4},{6,7},{7,6},{8,9},{9,8},{10,11... | collective-permute-start | bytes 589832 | tf_op jit(solution)/shard_map/ppermute | solution.py:26
  33.7 1.4 collective-permute-start.7
  33.8 1.6 %collective-permute-start.8 = (bf16[128,768]{1,0:T(8,128)(2,1)S(1)}, bf16[128,768]{1,0:T(8,128)(2,1)S(1)}, u32[]{:S(2)}, u32[]{:S(2)}) collective-permute-start(bf16[128,768]{1,0:T(8,128)(2,1)S(1)} %collective-permute-done.4.refs_2_.refs_6_), channel_id=1, source_target_pairs={{0,1},{1,0},{2,3},{3,2},{4,5},{5,4},{6,7},{7,6},{8,9},{9,8},{10,11... | collective-permute-start | bytes 589832 | tf_op jit(solution)/shard_map/ppermute | solution.py:26
  34.2 1.5 collective-permute-start.9
  35.7 17.1 %collective-permute-start.10 = (bf16[1,256,768]{2,1,0:T(8,128)(2,1)S(1)}, bf16[1,256,768]{2,1,0:T(8,128)(2,1)S(1)}, u32[]{:S(2)}, u32[]{:S(2)}) collective-permute-start(bf16[1,256,768]{2,1,0:T(8,128)(2,1)S(1)} %get-tuple-element.71), channel_id=1, source_target_pairs={{0,15},{1,2},{2,1},{3,4},{4,3},{5,6},{6,5},{7,8},{8,7},{9,10},{10,... | collective-permute-start | bytes 1179656 | tf_op jit(solution)/shard_map/ppermute | solution.py:533
  59.0 1.3 collective-permute-start.11
  60.3 4.9 %collective-permute-start.14 = (f32[12,768]{1,0:T(8,128)S(1)}, f32[12,768]{1,0:T(8,128)S(1)}, u32[]{:S(2)}, u32[]{:S(2)}) collective-permute-start(f32[12,768]{1,0:T(8,128)S(1)} %add.3.refs_0_), channel_id=1, source_target_pairs={{0,0},{9,1},{2,2},{11,3},{4,4},{13,5},{6,6},{15,7},{8,8},{1,9},{10... | collective-permute-start | bytes 110600 | tf_op jit(solution)/shard_map/ppermute | solution.py:36
  61.0 4.2 %collective-permute-start.13 = (f32[12,768]{1,0:T(8,128)S(1)}, f32[12,768]{1,0:T(8,128)S(1)}, u32[]{:S(2)}, u32[]{:S(2)}) collective-permute-start(f32[12,768]{1,0:T(8,128)S(1)} %add.3.refs_0_), channel_id=1, source_target_pairs={{0,0},{13,1},{2,2},{15,3},{4,4},{1,5},{6,6},{3,7},{8,8},{5,9},{10,... | collective-permute-start | bytes 110600 | tf_op jit(solution)/shard_map/ppermute | solution.py:36
  61.7 3.6 %collective-permute-start.12 = (f32[12,768]{1,0:T(8,128)S(1)}, f32[12,768]{1,0:T(8,128)S(1)}, u32[]{:S(2)}, u32[]{:S(2)}) collective-permute-start(f32[12,768]{1,0:T(8,128)S(1)} %add.3.refs_0_), channel_id=1, source_target_pairs={{0,0},{5,1},{2,2},{7,3},{4,4},{9,5},{6,6},{11,7},{8,8},{13,9},{10,... | collective-permute-start | bytes 110600 | tf_op jit(solution)/shard_map/ppermute | solution.py:36
  65.3 2.0 %collective-permute-start.17 = (f32[12,768]{1,0:T(8,128)S(1)}, f32[12,768]{1,0:T(8,128)S(1)}, u32[]{:S(2)}, u32[]{:S(2)}) collective-permute-start(f32[12,768]{1,0:T(8,128)S(1)} %add.4.s0), channel_id=1, source_target_pairs={{0,0},{3,1},{2,2},{1,3},{4,4},{7,5},{6,6},{5,7},{8,8},{11,9},{10,1... | collective-permute-start | bytes 110600 | tf_op jit(solution)/shard_map/ppermute | solution.py:36
  65.9 1.4 collective-permute-start.16
  66.6 0.7 collective-permute-start.15
  67.4 2.0 %collective-permute-start.20 = (f32[8,768]{1,0:T(8,128)S(1)}, f32[8,768]{1,0:T(8,128)S(1)}, u32[]{:S(2)}, u32[]{:S(2)}) collective-permute-start(f32[8,768]{1,0:T(8,128)S(1)} %get-tuple-element.88.refs_0_.emb), channel_id=1, source_target_pairs={{0,0},{33,1},{2,2},{35,3},{4,4},{37,5},{6,6},{39,7},{8,8},{41,9},{... | collective-permute-start | bytes 73736 | tf_op jit(solution)/shard_map/ppermute | solution.py:36
  68.1 1.4 collective-permute-start.19
  68.8 0.7 collective-permute-start.18
  71.2 2.0 %collective-permute-start.23 = (f32[16,1024]{1,0:T(8,128)S(1)}, f32[16,1024]{1,0:T(8,128)S(1)}, u32[]{:S(2)}, u32[]{:S(2)}) collective-permute-start(f32[16,1024]{1,0:T(8,128)S(1)} %get-tuple-element.93.refs_0_), channel_id=1, source_target_pairs={{0,0},{9,1},{2,2},{11,3},{4,4},{13,5},{6,6},{15,7},{8,8},{1,9},{10... | collective-permute-start | bytes 196616 | tf_op jit(solution)/shard_map/ppermute | solution.py:36
  71.9 1.4 collective-permute-start.22
  72.5 0.7 collective-permute-start.21
  73.4 2.6 %collective-permute-start.26 = (f32[16,1024]{1,0:T(8,128)S(1)}, f32[16,1024]{1,0:T(8,128)S(1)}, u32[]{:S(2)}, u32[]{:S(2)}) collective-permute-start(f32[16,1024]{1,0:T(8,128)S(1)} %merge.1.s0), channel_id=1, source_target_pairs={{0,0},{3,1},{2,2},{1,3},{4,4},{7,5},{6,6},{5,7},{8,8},{11,9},{10,1... | collective-permute-start | bytes 196616 | tf_op jit(solution)/shard_map/ppermute | solution.py:36
  74.0 1.9 %collective-permute-start.25 = (f32[16,1024]{1,0:T(8,128)S(1)}, f32[16,1024]{1,0:T(8,128)S(1)}, u32[]{:S(2)}, u32[]{:S(2)}) collective-permute-start(f32[16,1024]{1,0:T(8,128)S(1)} %merge.1.s0), channel_id=1, source_target_pairs={{0,0},{67,1},{2,2},{65,3},{4,4},{71,5},{6,6},{69,7},{8,8},{75,9},{... | collective-permute-start | bytes 196616 | tf_op jit(solution)/shard_map/ppermute | solution.py:36
  74.7 1.2 collective-permute-start.24
  76.1 44.7 %collective-permute-start.27 = (f32[64,1024]{1,0:T(8,128)S(1)}, f32[64,1024]{1,0:T(8,128)S(1)}, u32[]{:S(2)}, u32[]{:S(2)}) collective-permute-start(f32[64,1024]{1,0:T(8,128)S(1)} %pack.1.packed), channel_id=1, source_target_pairs={{0,1},{1,0},{2,3},{3,2},{4,5},{5,4},{6,7},{7,6},{8,9},{9,8},{10,11... | collective-permute-start | bytes 786440 | tf_op jit(solution)/shard_map/ppermute | solution.py:26
  123.5 2.9 %collective-permute-start.28 = (f32[384,768]{1,0:T(8,128)S(1)}, f32[384,768]{1,0:T(8,128)S(1)}, u32[]{:S(2)}, u32[]{:S(2)}) collective-permute-start(f32[384,768]{1,0:T(8,128)S(1)} %get-tuple-element.104), channel_id=1, source_target_pairs={{0,1},{1,0},{2,3},{3,2},{4,5},{5,4},{6,7},{7,6},{8,9},{9,8},{10,11... | collective-permute-start | bytes 3538952 | tf_op jit(solution)/shard_map/ppermute | solution.py:26
  126.6 6.7 %collective-permute-start.29 = (bf16[96,768]{1,0:T(8,128)(2,1)S(1)}, bf16[96,768]{1,0:T(8,128)(2,1)S(1)}, u32[]{:S(2)}, u32[]{:S(2)}) collective-permute-start(bf16[96,768]{1,0:T(8,128)(2,1)S(1)} %get-tuple-element.106), channel_id=1, source_target_pairs={{32,0},{9,1},{34,2},{11,3},{36,4},{13,5},{38,6},{15,7},{40,8},{1,9... | collective-permute-start | bytes 442376 | tf_op jit(solution)/shard_map/ppermute | solution.py:36
  128.4 6.5 %collective-permute-start.30 = (bf16[96,768]{1,0:T(8,128)(2,1)S(1)}, bf16[96,768]{1,0:T(8,128)(2,1)S(1)}, u32[]{:S(2)}, u32[]{:S(2)}) collective-permute-start(bf16[96,768]{1,0:T(8,128)(2,1)S(1)} %get-tuple-element.107), channel_id=1, source_target_pairs={{48,0},{13,1},{50,2},{15,3},{52,4},{1,5},{54,6},{3,7},{56,8},{5,9}... | collective-permute-start | bytes 442376 | tf_op jit(solution)/shard_map/ppermute | solution.py:36
  130.7 5.1 %collective-permute-start.31 = (bf16[96,768]{1,0:T(8,128)(2,1)S(1)}, bf16[96,768]{1,0:T(8,128)(2,1)S(1)}, u32[]{:S(2)}, u32[]{:S(2)}) collective-permute-start(bf16[96,768]{1,0:T(8,128)(2,1)S(1)} %get-tuple-element.108), channel_id=1, source_target_pairs={{16,0},{5,1},{18,2},{7,3},{20,4},{9,5},{22,6},{11,7},{24,8},{13,9}... | collective-permute-start | bytes 442376 | tf_op jit(solution)/shard_map/ppermute | solution.py:36
  135.9 5.9 %collective-permute-start.32 = (f32[24,768]{1,0:T(8,128)S(1)}, f32[24,768]{1,0:T(8,128)S(1)}, u32[]{:S(2)}, u32[]{:S(2)}) collective-permute-start(f32[24,768]{1,0:T(8,128)S(1)} %get-tuple-element.110), channel_id=1, source_target_pairs={{8,0},{33,1},{10,2},{35,3},{12,4},{37,5},{14,6},{39,7},{0,8},{41,9... | collective-permute-start | bytes 221192 | tf_op jit(solution)/shard_map/ppermute | solution.py:36
  137.6 5.6 %collective-permute-start.33 = (f32[24,768]{1,0:T(8,128)S(1)}, f32[24,768]{1,0:T(8,128)S(1)}, u32[]{:S(2)}, u32[]{:S(2)}) collective-permute-start(f32[24,768]{1,0:T(8,128)S(1)} %get-tuple-element.111), channel_id=1, source_target_pairs={{12,0},{49,1},{14,2},{51,3},{0,4},{53,5},{2,6},{55,7},{4,8},{57,9}... | collective-permute-start | bytes 221192 | tf_op jit(solution)/shard_map/ppermute | solution.py:36
  140.0 4.4 %collective-permute-start.34 = (f32[24,768]{1,0:T(8,128)S(1)}, f32[24,768]{1,0:T(8,128)S(1)}, u32[]{:S(2)}, u32[]{:S(2)}) collective-permute-start(f32[24,768]{1,0:T(8,128)S(1)} %get-tuple-element.112), channel_id=1, source_target_pairs={{4,0},{17,1},{6,2},{19,3},{8,4},{21,5},{10,6},{23,7},{12,8},{25,9}... | collective-permute-start | bytes 221192 | tf_op jit(solution)/shard_map/ppermute | solution.py:36
  144.4 5.6 %collective-permute-start.35 = (f32[6,768]{1,0:T(8,128)S(1)}, f32[6,768]{1,0:T(8,128)S(1)}, u32[]{:S(2)}, u32[]{:S(2)}) collective-permute-start(f32[6,768]{1,0:T(8,128)S(1)} %get-tuple-element.114), channel_id=1, source_target_pairs={{2,0},{3,1},{0,2},{1,3},{6,4},{7,5},{4,6},{5,7},{10,8},{11,9},{8,1... | collective-permute-start | bytes 55304 | tf_op jit(solution)/shard_map/ppermute | solution.py:36
  146.2 5.0 %collective-permute-start.36 = (f32[6,768]{1,0:T(8,128)S(1)}, f32[6,768]{1,0:T(8,128)S(1)}, u32[]{:S(2)}, u32[]{:S(2)}) collective-permute-start(f32[6,768]{1,0:T(8,128)S(1)} %get-tuple-element.115), channel_id=1, source_target_pairs={{66,0},{67,1},{64,2},{65,3},{70,4},{71,5},{68,6},{69,7},{74,8},{75... | collective-permute-start | bytes 55304 | tf_op jit(solution)/shard_map/ppermute | solution.py:36
  148.6 3.8 %collective-permute-start.37 = (f32[6,768]{1,0:T(8,128)S(1)}, f32[6,768]{1,0:T(8,128)S(1)}, u32[]{:S(2)}, u32[]{:S(2)}) collective-permute-start(f32[6,768]{1,0:T(8,128)S(1)} %get-tuple-element.116), channel_id=1, source_target_pairs={{64,0},{65,1},{66,2},{67,3},{68,4},{69,5},{70,6},{71,7},{72,8},{73... | collective-permute-start | bytes 55304 | tf_op jit(solution)/shard_map/ppermute | solution.py:36

commit v5 on v3

--- a/solution.py
+++ b/solution.py
@@ -325,7 +325,7 @@
 
 def turn_kernel(mixed, out):
     width = out.shape[0]
-    rows = 192
+    rows = 384
     lax.fori_loop(0, width // rows, lambda index, _: turn_rows(index * rows, rows, mixed, out), None)
 
 
@@ -557,7 +557,6 @@
     )
     sums = add([sums, swap(sums, "ctx", 1)])
     sums = add(around(sums, from_x))
-    sums, turned = lax.optimization_barrier((sums, turned))
     emb, rinv, target = call(
         norm_kernel,
         (f32(group, width), f32(group, 128), f32(group, width)),

time: 132 us -> 130 us (0.985)
    ppermute x6, waiting for transfers between devices: 3.05 us -> 5.96 us  [from_x(): lax.ppermute(value, 'ctx', [((c + 4 * k) % size, c) for c in range(size)])]
    ppermute x9, waiting for transfers between devices: 7.11 us -> 4.79 us  [from_z(): return lax.ppermute(value, ('dp', 'ctx'), pairs)]
  transfers between devices with their start and end apart: 37 -> 37, of which waited for: 23 -> 22; matrix products, arithmetic and copies ran while one was open for 1% -> 1% of each run, Pallas kernels for 25% -> 25%
where the time goes in v5:
time: 130 us
  starting transfers between devices  59.3 us (46%)
  Pallas kernels  44.7 us (34%)
  waiting for transfers between devices  23.2 us (18%)
  local copies, waits for them, and re-layouts  1.77 us (1%)
    pallas_call x3, Pallas kernels, attend(): call(functools.partial(attend_kernel, first), out_shape, in_specs, out_sp...  23.9 us
    ppermute x9, starting transfers between devices, from_z(): return lax.ppermute(value, ('dp', 'ctx'), pairs)  14.1 us
    ppermute x3, starting transfers between devices, shards(): fetch = lambda part: lax.ppermute(part, 'ctx', ring)  11.3 us
    ppermute x6, starting transfers between devices, from_y(): lax.ppermute(value, 'dp', [(d & 4 | d + k & 3, d) for d in range(lax.axis...  10.6 us
    ppermute x6, starting transfers between devices, from_plane(): return lax.ppermute(value, ('dp', 'ctx'), pairs)  9.55 us
    ppermute x6, starting transfers between devices, from_x(): lax.ppermute(value, 'ctx', [((c + 4 * k) % size, c) for c in range(size)])  8.95 us
    pallas_call x1, Pallas kernels, prepare(): call(prepare_kernel, (bf16(docs, tb, 2 * width), bf16(width, docs * tb),...  7.17 us
    ppermute x6, waiting for transfers between devices, from_plane(): return lax.ppermute(value, ('dp', 'ctx'), pairs)  6.87 us
  transfers between devices with their start and end apart: 37, of which 22 were waited for; matrix products, arithmetic and copies ran while one was open for 1% of the time, Pallas kernels for 25%

profile of v5, /device:TPU:0, one launch (start us, length us, event | category | flops | bytes accessed | tf_op | source)
XLA Modules:
  0.0 129.9 jit_solution(141114416313591630)
XLA Ops:
  0.7 1.7 %collective-permute-start.4 = (bf16[128,768]{1,0:T(8,128)(2,1)}, bf16[128,768]{1,0:T(8,128)(2,1)S(1)}, u32[]{:S(2)}, u32[]{:S(2)}) collective-permute-start(bf16[128,768]{1,0:T(8,128)(2,1)} %refs_4_), channel_id=1, source_target_pairs={{48,0},{0,16},{16,32},{32,48},{112,64},{64,80},{80,96},{96,112},{4... | collective-permute-start | bytes 589832 | tf_op jit(solution)/shard_map/ppermute | solution.py:35
  2.5 1.6 %collective-permute-start.3 = (bf16[128,768]{1,0:T(8,128)(2,1)}, bf16[128,768]{1,0:T(8,128)(2,1)S(1)}, u32[]{:S(2)}, u32[]{:S(2)}) collective-permute-start(bf16[128,768]{1,0:T(8,128)(2,1)} %refs_4_), channel_id=1, source_target_pairs={{16,0},{32,16},{48,32},{0,48},{80,64},{96,80},{112,96},{64,112},{1... | collective-permute-start | bytes 589832 | tf_op jit(solution)/shard_map/ppermute | solution.py:35
  4.0 1.2 fusion
  5.2 5.8 %collective-permute-start.2 = (bf16[1,256,768]{2,1,0:T(8,128)(2,1)S(1)}, bf16[1,256,768]{2,1,0:T(8,128)(2,1)S(1)}, u32[]{:S(2)}, u32[]{:S(2)}) collective-permute-start(bf16[1,256,768]{2,1,0:T(8,128)(2,1)S(1)} %get-tuple-element.113), channel_id=1, source_target_pairs={{0,15},{1,2},{2,1},{3,4},{4,3},{5,6},{6,5},{7,8},{8,7},{9,10},{10,... | collective-permute-start | bytes 1179656 | tf_op jit(solution)/shard_map/ppermute | solution.py:516
  11.2 7.2 %prepare.1 = (bf16[4,256,1536]{2,1,0:T(8,128)(2,1)S(1)}, bf16[768,1024]{1,0:T(8,128)(2,1)S(1)}, bf16[768,768]{1,0:T(8,128)(2,1)S(1)}) custom-call(bf16[4,256,768]{2,1,0:T(8,128)(2,1)} %refs_1_.5, bf16[768,2304]{1,0:T(8,128)(2,1)} %refs_7_.5), custom_call_target="tpu_custom_call" | custom-call | flops 3623878656 | bytes 11534336 | tf_op jit(solution)/shard_map/prepare/pallas_call | solution.py:259
  18.4 2.0 %collective-permute-start.5 = (bf16[128,768]{1,0:T(8,128)(2,1)S(1)}, bf16[128,768]{1,0:T(8,128)(2,1)S(1)}, u32[]{:S(2)}, u32[]{:S(2)}) collective-permute-start(bf16[128,768]{1,0:T(8,128)(2,1)S(1)} %copy-done.4), channel_id=1, source_target_pairs={{32,0},{48,16},{0,32},{16,48},{96,64},{112,80},{64,96},{80,112},{3... | collective-permute-start | bytes 589832 | tf_op jit(solution)/shard_map/ppermute | solution.py:35
  20.4 3.1 %near.1 = (bf16[4,256,768]{2,1,0:T(8,128)(2,1)S(1)}, bf16[768,1024]{1,0:T(8,128)(2,1)S(1)}) custom-call(bf16[4,256,768]{2,1,0:T(8,128)(2,1)S(1)} %collective-permute-done.near, bf16[768,2304]{1,0:T(8,128)(2,1)S(1)} %copy-done, bf16[768,768]{1,0:T(8,128)(2,1)S(1)} %get-tuple-element.58.w_v_turned.refs_8_), custom_call_target="tpu_custom_call" | custom-call | flops 2415919104 | bytes 4194304 | tf_op jit(solution)/shard_map/near/pallas_call | solution.py:521
  23.6 6.1 %attend.3 = (bf16[4,256,768]{2,1,0:T(8,128)(2,1)}, bf16[768,1024]{1,0:T(8,128)(2,1)S(1)}, bf16[4,256,768]{2,1,0:T(8,128)(2,1)S(1)}, f32[4,256,128]{2,1,0:T(8,128)S(1)}, f32[4,1,768]{2,1,0:T(1,128)S(1)}) custom-call(s32[4]{0:T(128)S(1)} %copy-done.6, bf16[4,256,768]{2,1,0:T(8,128)(2,1)S(1)} %copy-done.2, bf16[4,256,768]{2,1,0:T(8,128)(2,1)S(1)} %get-tuple-element.59.refs_2_, ...), custom_call_target="tpu_custom_call" | custom-call | flops 1509949440 | bytes 4194304 | tf_op jit(solution)/shard_map/attend/pallas_call | solution.py:211
  29.7 4.0 %collective-permute-start.6 = (bf16[128,768]{1,0:T(8,128)(2,1)S(1)}, bf16[128,768]{1,0:T(8,128)(2,1)S(1)}, u32[]{:S(2)}, u32[]{:S(2)}) collective-permute-start(bf16[128,768]{1,0:T(8,128)(2,1)S(1)} %copy-done.4), channel_id=1, source_target_pairs={{0,1},{1,0},{2,3},{3,2},{4,5},{5,4},{6,7},{7,6},{8,9},{9,8},{10,11... | collective-permute-start | bytes 589832 | tf_op jit(solution)/shard_map/ppermute | solution.py:26
  35.7 5.4 %collective-permute-start.10 = (bf16[1,256,768]{2,1,0:T(8,128)(2,1)S(1)}, bf16[1,256,768]{2,1,0:T(8,128)(2,1)S(1)}, u32[]{:S(2)}, u32[]{:S(2)}) collective-permute-start(bf16[1,256,768]{2,1,0:T(8,128)(2,1)S(1)} %get-tuple-element.69), channel_id=1, source_target_pairs={{0,15},{1,2},{2,1},{3,4},{4,3},{5,6},{6,5},{7,8},{8,7},{9,10},{10,... | collective-permute-start | bytes 1179656 | tf_op jit(solution)/shard_map/ppermute | solution.py:516
  41.2 11.7 %attend.4 = (bf16[4,256,768]{2,1,0:T(8,128)(2,1)}, bf16[768,1024]{1,0:T(8,128)(2,1)S(1)}, bf16[4,256,768]{2,1,0:T(8,128)(2,1)S(1)}, f32[4,256,128]{2,1,0:T(8,128)S(1)}, f32[4,1,768]{2,1,0:T(1,128)S(1)}) custom-call(s32[4]{0:T(128)S(1)} %copy-done.6, ...), custom_call_target="tpu_custom_call", output_to_operand_aliasing={{0}: (11, {}), {1}: (12, {}), {2}: (13, {}), {3}: (14, {}),... | custom-call | flops 3019898880 | bytes 4194304 | tf_op jit(solution)/shard_map/attend/pallas_call | solution.py:211
  52.9 6.1 %attend.5 = (bf16[4,256,768]{2,1,0:T(8,128)(2,1)}, bf16[768,1024]{1,0:T(8,128)(2,1)S(1)}, bf16[4,256,768]{2,1,0:T(8,128)(2,1)S(1)}, f32[4,256,128]{2,1,0:T(8,128)S(1)}, f32[4,1,768]{2,1,0:T(1,128)S(1)}) custom-call(s32[4]{0:T(128)S(1)} %copy-done.6, ...), custom_call_target="tpu_custom_call", output_to_operand_aliasing={{0}: (11, {}), {1}: (12, {}), {2}: (13, {}), {3}: (14, {}),... | custom-call | flops 1509949440 | bytes 4194304 | tf_op jit(solution)/shard_map/attend/pallas_call | solution.py:211
  59.1 1.2 collective-permute-done.11.refs_1_
  62.1 2.4 %collective-permute-start.12 = (f32[12,768]{1,0:T(8,128)S(1)}, f32[12,768]{1,0:T(8,128)S(1)}, u32[]{:S(2)}, u32[]{:S(2)}) collective-permute-start(f32[12,768]{1,0:T(8,128)S(1)} %add.3.refs_0_), channel_id=1, source_target_pairs={{4,0},{5,1},{6,2},{7,3},{8,4},{9,5},{10,6},{11,7},{12,8},{13,9},{1... | collective-permute-start | bytes 110600 | tf_op jit(solution)/shard_map/ppermute | solution.py:31
  64.5 1.7 %collective-permute-done.14.refs_3_ = f32[12,768]{1,0:T(8,128)S(1)} collective-permute-done((f32[12,768]{1,0:T(8,128)S(1)}, f32[12,768]{1,0:T(8,128)S(1)}, u32[]{:S(2)}, u32[]{:S(2)}) %collective-permute-start.14) | collective-permute-done | bytes 36896 | tf_op jit(solution)/shard_map/ppermute | solution.py:31
  66.8 1.3 %collective-permute-start.17 = (f32[12,768]{1,0:T(8,128)S(1)}, f32[12,768]{1,0:T(8,128)S(1)}, u32[]{:S(2)}, u32[]{:S(2)}) collective-permute-start(f32[12,768]{1,0:T(8,128)S(1)} %add.4.s0), channel_id=1, source_target_pairs={{2,0},{3,1},{0,2},{1,3},{6,4},{7,5},{4,6},{5,7},{10,8},{11,9},{8,1... | collective-permute-start | bytes 110600 | tf_op jit(solution)/shard_map/ppermute | solution.py:45
  68.2 1.0 collective-permute-start.16
  69.2 2.2 %collective-permute-start.15 = (f32[12,768]{1,0:T(8,128)S(1)}, f32[12,768]{1,0:T(8,128)S(1)}, u32[]{:S(2)}, u32[]{:S(2)}) collective-permute-start(f32[12,768]{1,0:T(8,128)S(1)} %add.4.s0), channel_id=1, source_target_pairs={{64,0},{65,1},{66,2},{67,3},{68,4},{69,5},{70,6},{71,7},{72,8},{73... | collective-permute-start | bytes 110600 | tf_op jit(solution)/shard_map/ppermute | solution.py:45
  71.4 1.6 %collective-permute-done.17.s2 = f32[12,768]{1,0:T(8,128)S(1)} collective-permute-done((f32[12,768]{1,0:T(8,128)S(1)}, f32[12,768]{1,0:T(8,128)S(1)}, u32[]{:S(2)}, u32[]{:S(2)}) %collective-permute-start.17) | collective-permute-done | bytes 36896 | tf_op jit(solution)/shard_map/ppermute | solution.py:45
  73.6 2.0 %collective-permute-start.20 = (f32[8,768]{1,0:T(8,128)S(1)}, f32[8,768]{1,0:T(8,128)S(1)}, u32[]{:S(2)}, u32[]{:S(2)}) collective-permute-start(f32[8,768]{1,0:T(8,128)S(1)} %get-tuple-element.84.refs_0_.emb), channel_id=1, source_target_pairs={{32,0},{48,16},{0,32},{16,48},{96,64},{112,80},{64,96},{80,112},{3... | collective-permute-start | bytes 73736 | tf_op jit(solution)/shard_map/ppermute | solution.py:35
  76.3 2.6 %collective-permute-start.18 = (f32[8,768]{1,0:T(8,128)S(1)}, f32[8,768]{1,0:T(8,128)S(1)}, u32[]{:S(2)}, u32[]{:S(2)}) collective-permute-start(f32[8,768]{1,0:T(8,128)S(1)} %get-tuple-element.84.refs_0_.emb), channel_id=1, source_target_pairs={{16,0},{32,16},{48,32},{0,48},{80,64},{96,80},{112,96},{64,112},{1... | collective-permute-start | bytes 73736 | tf_op jit(solution)/shard_map/ppermute | solution.py:35
  78.9 1.7 %collective-permute-done.19.refs_2_ = f32[8,768]{1,0:T(8,128)S(1)} collective-permute-done((f32[8,768]{1,0:T(8,128)S(1)}, f32[8,768]{1,0:T(8,128)S(1)}, u32[]{:S(2)}, u32[]{:S(2)}) %collective-permute-start.19) | collective-permute-done | bytes 24608 | tf_op jit(solution)/shard_map/ppermute | solution.py:35
  80.6 1.7 %score.1 = (f32[32,768]{1,0:T(8,128)S(1)}, f32[16,1024]{1,0:T(8,128)S(1)}) custom-call(s32[32]{0:T(128)S(1)} %copy-done.7, f32[8,768]{1,0:T(8,128)S(1)} %get-tuple-element.84.refs_0_.emb, f32[8,768]{1,0:T(8,128)S(1)} %collective-permute-done.18.refs_1_, f32[8,768]{1,0:T(8,128)S(1)} %collective-permute-done.19.refs_2_, ...), custom_call_target="tpu_custom_call" | custom-call | bytes 2097152 | tf_op jit(solution)/shard_map/score/pallas_call | solution.py:569
  82.4 1.5 %collective-permute-start.23 = (f32[16,1024]{1,0:T(8,128)S(1)}, f32[16,1024]{1,0:T(8,128)S(1)}, u32[]{:S(2)}, u32[]{:S(2)}) collective-permute-start(f32[16,1024]{1,0:T(8,128)S(1)} %get-tuple-element.89.refs_0_), channel_id=1, source_target_pairs={{8,0},{9,1},{10,2},{11,3},{12,4},{13,5},{14,6},{15,7},{0,8},{1,9},... | collective-permute-start | bytes 196616 | tf_op jit(solution)/shard_map/ppermute | solution.py:31
  83.9 2.6 %collective-permute-start.22 = (f32[16,1024]{1,0:T(8,128)S(1)}, f32[16,1024]{1,0:T(8,128)S(1)}, u32[]{:S(2)}, u32[]{:S(2)}) collective-permute-start(f32[16,1024]{1,0:T(8,128)S(1)} %get-tuple-element.89.refs_0_), channel_id=1, source_target_pairs={{12,0},{13,1},{14,2},{15,3},{0,4},{1,5},{2,6},{3,7},{4,8},{5,9},{6... | collective-permute-start | bytes 196616 | tf_op jit(solution)/shard_map/ppermute | solution.py:31
  87.1 1.1 collective-permute-done.23.refs_3_
  88.2 1.2 collective-permute-done.22.refs_2_
  89.4 1.4 %collective-permute-done.21.refs_1_ = f32[16,1024]{1,0:T(8,128)S(1)} collective-permute-done((f32[16,1024]{1,0:T(8,128)S(1)}, f32[16,1024]{1,0:T(8,128)S(1)}, u32[]{:S(2)}, u32[]{:S(2)}) %collective-permute-start.21) | collective-permute-done | bytes 65568 | tf_op jit(solution)/shard_map/ppermute | solution.py:31
  90.9 2.5 %collective-permute-start.26 = (f32[16,1024]{1,0:T(8,128)S(1)}, f32[16,1024]{1,0:T(8,128)S(1)}, u32[]{:S(2)}, u32[]{:S(2)}) collective-permute-start(f32[16,1024]{1,0:T(8,128)S(1)} %merge.1.s0), channel_id=1, source_target_pairs={{2,0},{3,1},{0,2},{1,3},{6,4},{7,5},{4,6},{5,7},{10,8},{11,9},{8,1... | collective-permute-start | bytes 196616 | tf_op jit(solution)/shard_map/ppermute | solution.py:45
  93.4 1.6 %collective-permute-start.25 = (f32[16,1024]{1,0:T(8,128)S(1)}, f32[16,1024]{1,0:T(8,128)S(1)}, u32[]{:S(2)}, u32[]{:S(2)}) collective-permute-start(f32[16,1024]{1,0:T(8,128)S(1)} %merge.1.s0), channel_id=1, source_target_pairs={{66,0},{67,1},{64,2},{65,3},{70,4},{71,5},{68,6},{69,7},{74,8},{75... | collective-permute-start | bytes 196616 | tf_op jit(solution)/shard_map/ppermute | solution.py:45
  95.1 1.6 %collective-permute-start.24 = (f32[16,1024]{1,0:T(8,128)S(1)}, f32[16,1024]{1,0:T(8,128)S(1)}, u32[]{:S(2)}, u32[]{:S(2)}) collective-permute-start(f32[16,1024]{1,0:T(8,128)S(1)} %merge.1.s0), channel_id=1, source_target_pairs={{64,0},{65,1},{66,2},{67,3},{68,4},{69,5},{70,6},{71,7},{72,8},{73... | collective-permute-start | bytes 196616 | tf_op jit(solution)/shard_map/ppermute | solution.py:45
  96.7 2.9 %turn.1.turned = bf16[768,1024]{1,0:T(8,128)(2,1)S(1)} custom-call(bf16[768,1024]{1,0:T(8,128)(2,1)S(1)} %get-tuple-element.97.mixed), custom_call_target="tpu_custom_call" | custom-call | flops 1207959552 | bytes 4194304 | tf_op jit(solution)/shard_map/turn/pallas_call | solution.py:544
  99.9 2.8 %grad.1 = (f32[384,768]{1,0:T(8,128)S(1)}, bf16[1024,768]{1,0:T(8,128)(2,1)S(1)}, f32[8,128]{1,0:T(8,128)S(1)}) custom-call(s32[4]{0:T(128)S(1)} %copy-done.6, f32[16,1024]{1,0:T(8,128)S(1)} %merge.1.s0, f32[16,1024]{1,0:T(8,128)S(1)} %collective-permute-done.24.s1, f32[16,1024]{1,0:T(8,128)S(1)} %collective-permute-done.25.s2, ...), custom_call_target="tpu_custom_call" | custom-call | flops 603979776 | bytes 8388608 | tf_op jit(solution)/shard_map/grad/pallas_call | solution.py:588
  102.8 1.0 keep.1.refs_0_
  103.8 1.8 %collective-permute-done.27.refs_1_ = f32[384,768]{1,0:T(8,128)S(1)} collective-permute-done((f32[384,768]{1,0:T(8,128)S(1)}, f32[384,768]{1,0:T(8,128)S(1)}, u32[]{:S(2)}, u32[]{:S(2)}) %collective-permute-start.27) | collective-permute-done | bytes 1179680 | tf_op jit(solution)/shard_map/ppermute | solution.py:26
  105.8 1.5 %collective-permute-start.28 = (bf16[96,768]{1,0:T(8,128)(2,1)S(1)}, bf16[96,768]{1,0:T(8,128)(2,1)S(1)}, u32[]{:S(2)}, u32[]{:S(2)}) collective-permute-start(bf16[96,768]{1,0:T(8,128)(2,1)S(1)} %get-tuple-element.102), channel_id=1, source_target_pairs={{32,0},{9,1},{34,2},{11,3},{36,4},{13,5},{38,6},{15,7},{40,8},{1,9... | collective-permute-start | bytes 442376 | tf_op jit(solution)/shard_map/ppermute | solution.py:56
  107.3 2.6 %collective-permute-start.29 = (bf16[96,768]{1,0:T(8,128)(2,1)S(1)}, bf16[96,768]{1,0:T(8,128)(2,1)S(1)}, u32[]{:S(2)}, u32[]{:S(2)}) collective-permute-start(bf16[96,768]{1,0:T(8,128)(2,1)S(1)} %get-tuple-element.103), channel_id=1, source_target_pairs={{48,0},{13,1},{50,2},{15,3},{52,4},{1,5},{54,6},{3,7},{56,8},{5,9}... | collective-permute-start | bytes 442376 | tf_op jit(solution)/shard_map/ppermute | solution.py:56
  110.6 2.0 %collective-permute-done.28.refs_1_ = bf16[96,768]{1,0:T(8,128)(2,1)S(1)} collective-permute-done((bf16[96,768]{1,0:T(8,128)(2,1)S(1)}, bf16[96,768]{1,0:T(8,128)(2,1)S(1)}, u32[]{:S(2)}, u32[]{:S(2)}) %collective-permute-start.28) | collective-permute-done | bytes 147488 | tf_op jit(solution)/shard_map/ppermute | solution.py:56
  112.6 1.5 %collective-permute-done.29.refs_2_ = bf16[96,768]{1,0:T(8,128)(2,1)S(1)} collective-permute-done((bf16[96,768]{1,0:T(8,128)(2,1)S(1)}, bf16[96,768]{1,0:T(8,128)(2,1)S(1)}, u32[]{:S(2)}, u32[]{:S(2)}) %collective-permute-start.29) | collective-permute-done | bytes 147488 | tf_op jit(solution)/shard_map/ppermute | solution.py:56
  114.1 1.0 collective-permute-done.30.refs_3_
  115.2 1.5 %collective-permute-start.31 = (f32[24,768]{1,0:T(8,128)S(1)}, f32[24,768]{1,0:T(8,128)S(1)}, u32[]{:S(2)}, u32[]{:S(2)}) collective-permute-start(f32[24,768]{1,0:T(8,128)S(1)} %get-tuple-element.106), channel_id=1, source_target_pairs={{8,0},{33,1},{10,2},{35,3},{12,4},{37,5},{14,6},{39,7},{0,8},{41,9... | collective-permute-start | bytes 221192 | tf_op jit(solution)/shard_map/ppermute | solution.py:56
  116.7 1.2 collective-permute-start.32
  117.9 2.0 %collective-permute-start.33 = (f32[24,768]{1,0:T(8,128)S(1)}, f32[24,768]{1,0:T(8,128)S(1)}, u32[]{:S(2)}, u32[]{:S(2)}) collective-permute-start(f32[24,768]{1,0:T(8,128)S(1)} %get-tuple-element.108), channel_id=1, source_target_pairs={{4,0},{17,1},{6,2},{19,3},{8,4},{21,5},{10,6},{23,7},{12,8},{25,9}... | collective-permute-start | bytes 221192 | tf_op jit(solution)/shard_map/ppermute | solution.py:56
  120.0 1.2 collective-permute-done.31.refs_1_
  121.1 1.2 collective-permute-done.32.refs_2_
  122.9 2.6 %collective-permute-start.35 = (f32[6,768]{1,0:T(8,128)S(1)}, f32[6,768]{1,0:T(8,128)S(1)}, u32[]{:S(2)}, u32[]{:S(2)}) collective-permute-start(f32[6,768]{1,0:T(8,128)S(1)} %get-tuple-element.111), channel_id=1, source_target_pairs={{66,0},{67,1},{64,2},{65,3},{70,4},{71,5},{68,6},{69,7},{74,8},{75... | collective-permute-start | bytes 55304 | tf_op jit(solution)/shard_map/ppermute | solution.py:45
  126.6 1.1 collective-permute-done.34.refs_1_
  128.0 1.3 %collective-permute-done.36.refs_3_ = f32[6,768]{1,0:T(8,128)S(1)} collective-permute-done((f32[6,768]{1,0:T(8,128)S(1)}, f32[6,768]{1,0:T(8,128)S(1)}, u32[]{:S(2)}, u32[]{:S(2)}) %collective-permute-start.36) | collective-permute-done | bytes 18464 | tf_op jit(solution)/shard_map/ppermute | solution.py:45
  (65 shorter events, 10.7 us)
Async XLA Ops:
  0.6 10.3 %copy-start.1 = (bf16[4,256,768]{2,1,0:T(8,128)(2,1)S(1)}, bf16[4,256,768]{2,1,0:T(8,128)(2,1)}, u32[]{:S(2)}) copy-start(bf16[4,256,768]{2,1,0:T(8,128)(2,1)} %refs_1_.5) | copy-start | bytes 4718596
  0.6 17.7 %collective-permute-start = (bf16[4,256,768]{2,1,0:T(8,128)(2,1)}, bf16[4,256,768]{2,1,0:T(8,128)(2,1)S(1)}, u32[]{:S(2)}, u32[]{:S(2)}) collective-permute-start(bf16[4,256,768]{2,1,0:T(8,128)(2,1)} %refs_1_.5), channel_id=1, source_target_pairs={{0,1},{1,0},{2,3},{3,2},{4,5},{5,4},{6,7},{7,6},{8,9},{9,8},{10,11... | collective-permute-start | bytes 4718600 | tf_op jit(solution)/shard_map/ppermute | solution.py:26
  0.7 29.0 %collective-permute-start.4 = (bf16[128,768]{1,0:T(8,128)(2,1)}, bf16[128,768]{1,0:T(8,128)(2,1)S(1)}, u32[]{:S(2)}, u32[]{:S(2)}) collective-permute-start(bf16[128,768]{1,0:T(8,128)(2,1)} %refs_4_), channel_id=1, source_target_pairs={{48,0},{0,16},{16,32},{32,48},{112,64},{64,80},{80,96},{96,112},{4... | collective-permute-start | bytes 589832 | tf_op jit(solution)/shard_map/ppermute | solution.py:35
  2.5 27.3 %collective-permute-start.3 = (bf16[128,768]{1,0:T(8,128)(2,1)}, bf16[128,768]{1,0:T(8,128)(2,1)S(1)}, u32[]{:S(2)}, u32[]{:S(2)}) collective-permute-start(bf16[128,768]{1,0:T(8,128)(2,1)} %refs_4_), channel_id=1, source_target_pairs={{16,0},{32,16},{48,32},{0,48},{80,64},{96,80},{112,96},{64,112},{1... | collective-permute-start | bytes 589832 | tf_op jit(solution)/shard_map/ppermute | solution.py:35
  5.2 18.3 %collective-permute-start.2 = (bf16[1,256,768]{2,1,0:T(8,128)(2,1)S(1)}, bf16[1,256,768]{2,1,0:T(8,128)(2,1)S(1)}, u32[]{:S(2)}, u32[]{:S(2)}) collective-permute-start(bf16[1,256,768]{2,1,0:T(8,128)(2,1)S(1)} %get-tuple-element.113), channel_id=1, source_target_pairs={{0,15},{1,2},{2,1},{3,4},{4,3},{5,6},{6,5},{7,8},{8,7},{9,10},{10,... | collective-permute-start | bytes 1179656 | tf_op jit(solution)/shard_map/ppermute | solution.py:516
  11.0 7.3 %copy-start.4 = (bf16[128,768]{1,0:T(8,128)(2,1)S(1)}, bf16[128,768]{1,0:T(8,128)(2,1)}, u32[]{:S(2)}) copy-start(bf16[128,768]{1,0:T(8,128)(2,1)} %refs_4_) | copy-start | bytes 589828
  11.0 9.3 %copy-start = (bf16[768,2304]{1,0:T(8,128)(2,1)S(1)}, bf16[768,2304]{1,0:T(8,128)(2,1)}, u32[]{:S(2)}) copy-start(bf16[768,2304]{1,0:T(8,128)(2,1)} %refs_7_.5) | copy-start | bytes 10616836
  11.1 24.0 %collective-permute-start.1 = (bf16[2,256,768]{2,1,0:T(8,128)(2,1)S(1)}, bf16[2,256,768]{2,1,0:T(8,128)(2,1)S(1)}, u32[]{:S(2)}, u32[]{:S(2)}) collective-permute-start(bf16[2,256,768]{2,1,0:T(8,128)(2,1)S(1)} %slice.12), channel_id=1, source_target_pairs={{0,15},{1,2},{2,1},{3,4},{4,3},{5,6},{6,5},{7,8},{8,7},{9,10},{10,... | collective-permute-start | bytes 2359304 | tf_op jit(solution)/shard_map/ppermute | solution.py:516
  18.4 11.4 %collective-permute-start.5 = (bf16[128,768]{1,0:T(8,128)(2,1)S(1)}, bf16[128,768]{1,0:T(8,128)(2,1)S(1)}, u32[]{:S(2)}, u32[]{:S(2)}) collective-permute-start(bf16[128,768]{1,0:T(8,128)(2,1)S(1)} %copy-done.4), channel_id=1, source_target_pairs={{32,0},{48,16},{0,32},{16,48},{96,64},{112,80},{64,96},{80,112},{3... | collective-permute-start | bytes 589832 | tf_op jit(solution)/shard_map/ppermute | solution.py:35
  20.4 3.2 %copy-start.2 = (bf16[4,256,768]{2,1,0:T(8,128)(2,1)S(1)}, bf16[4,256,768]{2,1,0:T(8,128)(2,1)}, u32[]{:S(2)}) copy-start(bf16[4,256,768]{2,1,0:T(8,128)(2,1)} %refs_1_.5) | copy-start | bytes 4718596
  20.4 3.2 %copy-start.3 = (bf16[768,768]{1,0:T(8,128)(2,1)S(1)}, bf16[768,768]{1,0:T(8,128)(2,1)}, u32[]{:S(2)}) copy-start(bf16[768,768]{1,0:T(8,128)(2,1)} %refs_9_.5) | copy-start | bytes 3538948
  20.4 3.2 %copy-start.5 = (f32[768]{0:T(1024)S(1)}, f32[768]{0:T(1024)}, u32[]{:S(2)}) copy-start(f32[768]{0:T(1024)} %gain.1) | copy-start | bytes 9220
  20.4 3.2 %copy-start.6 = (s32[4]{0:T(128)S(1)}, s32[4]{0:T(128)}, u32[]{:S(2)}) copy-start(s32[4]{0:T(128)} %lengths.1) | copy-start | bytes 52
  23.6 10.7 %copy-start.7 = (s32[32]{0:T(128)S(1)}, s32[32]{0:T(128)}, u32[]{:S(2)}) copy-start(s32[32]{0:T(128)} %positive.2) | copy-start | bytes 388
  29.7 5.3 %collective-permute-start.6 = (bf16[128,768]{1,0:T(8,128)(2,1)S(1)}, bf16[128,768]{1,0:T(8,128)(2,1)S(1)}, u32[]{:S(2)}, u32[]{:S(2)}) collective-permute-start(bf16[128,768]{1,0:T(8,128)(2,1)S(1)} %copy-done.4), channel_id=1, source_target_pairs={{0,1},{1,0},{2,3},{3,2},{4,5},{5,4},{6,7},{7,6},{8,9},{9,8},{10,11... | collective-permute-start | bytes 589832 | tf_op jit(solution)/shard_map/ppermute | solution.py:26
  33.7 1.4 %collective-permute-start.7 = (bf16[128,768]{1,0:T(8,128)(2,1)S(1)}, bf16[128,768]{1,0:T(8,128)(2,1)S(1)}, u32[]{:S(2)}, u32[]{:S(2)}) collective-permute-start(bf16[128,768]{1,0:T(8,128)(2,1)S(1)} %collective-permute-done.3.refs_1_.refs_5_), channel_id=1, source_target_pairs={{0,1},{1,0},{2,3},{3,2},{4,5},{5,4},{6,7},{7,6},{8,9},{9,8},{10,11... | collective-permute-start | bytes 589832 | tf_op jit(solution)/shard_map/ppermute | solution.py:26
  33.8 1.6 %collective-permute-start.8 = (bf16[128,768]{1,0:T(8,128)(2,1)S(1)}, bf16[128,768]{1,0:T(8,128)(2,1)S(1)}, u32[]{:S(2)}, u32[]{:S(2)}) collective-permute-start(bf16[128,768]{1,0:T(8,128)(2,1)S(1)} %collective-permute-done.4.refs_2_.refs_6_), channel_id=1, source_target_pairs={{0,1},{1,0},{2,3},{3,2},{4,5},{5,4},{6,7},{7,6},{8,9},{9,8},{10,11... | collective-permute-start | bytes 589832 | tf_op jit(solution)/shard_map/ppermute | solution.py:26
  34.2 1.5 %collective-permute-start.9 = (bf16[128,768]{1,0:T(8,128)(2,1)S(1)}, bf16[128,768]{1,0:T(8,128)(2,1)S(1)}, u32[]{:S(2)}, u32[]{:S(2)}) collective-permute-start(bf16[128,768]{1,0:T(8,128)(2,1)S(1)} %collective-permute-done.5.refs_3_.refs_7_), channel_id=1, source_target_pairs={{0,1},{1,0},{2,3},{3,2},{4,5},{5,4},{6,7},{7,6},{8,9},{9,8},{10,11... | collective-permute-start | bytes 589832 | tf_op jit(solution)/shard_map/ppermute | solution.py:26
  35.7 17.1 %collective-permute-start.10 = (bf16[1,256,768]{2,1,0:T(8,128)(2,1)S(1)}, bf16[1,256,768]{2,1,0:T(8,128)(2,1)S(1)}, u32[]{:S(2)}, u32[]{:S(2)}) collective-permute-start(bf16[1,256,768]{2,1,0:T(8,128)(2,1)S(1)} %get-tuple-element.69), channel_id=1, source_target_pairs={{0,15},{1,2},{2,1},{3,4},{4,3},{5,6},{6,5},{7,8},{8,7},{9,10},{10,... | collective-permute-start | bytes 1179656 | tf_op jit(solution)/shard_map/ppermute | solution.py:516
  59.0 1.3 %collective-permute-start.11 = (f32[12,768]{1,0:T(8,128)S(1)}, f32[12,768]{1,0:T(8,128)S(1)}, u32[]{:S(2)}, u32[]{:S(2)}) collective-permute-start(f32[12,768]{1,0:T(8,128)S(1)} %stack.1.refs_0_), channel_id=1, source_target_pairs={{0,1},{1,0},{2,3},{3,2},{4,5},{5,4},{6,7},{7,6},{8,9},{9,8},{10,11... | collective-permute-start | bytes 110600 | tf_op jit(solution)/shard_map/ppermute | solution.py:26
  60.3 5.9 %collective-permute-start.14 = (f32[12,768]{1,0:T(8,128)S(1)}, f32[12,768]{1,0:T(8,128)S(1)}, u32[]{:S(2)}, u32[]{:S(2)}) collective-permute-start(f32[12,768]{1,0:T(8,128)S(1)} %add.3.refs_0_), channel_id=1, source_target_pairs={{8,0},{9,1},{10,2},{11,3},{12,4},{13,5},{14,6},{15,7},{0,8},{1,9},... | collective-permute-start | bytes 110600 | tf_op jit(solution)/shard_map/ppermute | solution.py:31
  61.3 5.5 %collective-permute-start.13 = (f32[12,768]{1,0:T(8,128)S(1)}, f32[12,768]{1,0:T(8,128)S(1)}, u32[]{:S(2)}, u32[]{:S(2)}) collective-permute-start(f32[12,768]{1,0:T(8,128)S(1)} %add.3.refs_0_), channel_id=1, source_target_pairs={{12,0},{13,1},{14,2},{15,3},{0,4},{1,5},{2,6},{3,7},{4,8},{5,9},{6... | collective-permute-start | bytes 110600 | tf_op jit(solution)/shard_map/ppermute | solution.py:31
  62.1 4.7 %collective-permute-start.12 = (f32[12,768]{1,0:T(8,128)S(1)}, f32[12,768]{1,0:T(8,128)S(1)}, u32[]{:S(2)}, u32[]{:S(2)}) collective-permute-start(f32[12,768]{1,0:T(8,128)S(1)} %add.3.refs_0_), channel_id=1, source_target_pairs={{4,0},{5,1},{6,2},{7,3},{8,4},{9,5},{10,6},{11,7},{12,8},{13,9},{1... | collective-permute-start | bytes 110600 | tf_op jit(solution)/shard_map/ppermute | solution.py:31
  66.8 6.1 %collective-permute-start.17 = (f32[12,768]{1,0:T(8,128)S(1)}, f32[12,768]{1,0:T(8,128)S(1)}, u32[]{:S(2)}, u32[]{:S(2)}) collective-permute-start(f32[12,768]{1,0:T(8,128)S(1)} %add.4.s0), channel_id=1, source_target_pairs={{2,0},{3,1},{0,2},{1,3},{6,4},{7,5},{4,6},{5,7},{10,8},{11,9},{8,1... | collective-permute-start | bytes 110600 | tf_op jit(solution)/shard_map/ppermute | solution.py:45
  68.2 5.3 %collective-permute-start.16 = (f32[12,768]{1,0:T(8,128)S(1)}, f32[12,768]{1,0:T(8,128)S(1)}, u32[]{:S(2)}, u32[]{:S(2)}) collective-permute-start(f32[12,768]{1,0:T(8,128)S(1)} %add.4.s0), channel_id=1, source_target_pairs={{66,0},{67,1},{64,2},{65,3},{70,4},{71,5},{68,6},{69,7},{74,8},{75... | collective-permute-start | bytes 110600 | tf_op jit(solution)/shard_map/ppermute | solution.py:45
  69.2 4.3 %collective-permute-start.15 = (f32[12,768]{1,0:T(8,128)S(1)}, f32[12,768]{1,0:T(8,128)S(1)}, u32[]{:S(2)}, u32[]{:S(2)}) collective-permute-start(f32[12,768]{1,0:T(8,128)S(1)} %add.4.s0), channel_id=1, source_target_pairs={{64,0},{65,1},{66,2},{67,3},{68,4},{69,5},{70,6},{71,7},{72,8},{73... | collective-permute-start | bytes 110600 | tf_op jit(solution)/shard_map/ppermute | solution.py:45
  73.6 5.3 %collective-permute-start.20 = (f32[8,768]{1,0:T(8,128)S(1)}, f32[8,768]{1,0:T(8,128)S(1)}, u32[]{:S(2)}, u32[]{:S(2)}) collective-permute-start(f32[8,768]{1,0:T(8,128)S(1)} %get-tuple-element.84.refs_0_.emb), channel_id=1, source_target_pairs={{32,0},{48,16},{0,32},{16,48},{96,64},{112,80},{64,96},{80,112},{3... | collective-permute-start | bytes 73736 | tf_op jit(solution)/shard_map/ppermute | solution.py:35
  75.6 5.0 %collective-permute-start.19 = (f32[8,768]{1,0:T(8,128)S(1)}, f32[8,768]{1,0:T(8,128)S(1)}, u32[]{:S(2)}, u32[]{:S(2)}) collective-permute-start(f32[8,768]{1,0:T(8,128)S(1)} %get-tuple-element.84.refs_0_.emb), channel_id=1, source_target_pairs={{48,0},{0,16},{16,32},{32,48},{112,64},{64,80},{80,96},{96,112},{4... | collective-permute-start | bytes 73736 | tf_op jit(solution)/shard_map/ppermute | solution.py:35
  76.3 4.4 %collective-permute-start.18 = (f32[8,768]{1,0:T(8,128)S(1)}, f32[8,768]{1,0:T(8,128)S(1)}, u32[]{:S(2)}, u32[]{:S(2)}) collective-permute-start(f32[8,768]{1,0:T(8,128)S(1)} %get-tuple-element.84.refs_0_.emb), channel_id=1, source_target_pairs={{16,0},{32,16},{48,32},{0,48},{80,64},{96,80},{112,96},{64,112},{1... | collective-permute-start | bytes 73736 | tf_op jit(solution)/shard_map/ppermute | solution.py:35
  82.4 5.8 %collective-permute-start.23 = (f32[16,1024]{1,0:T(8,128)S(1)}, f32[16,1024]{1,0:T(8,128)S(1)}, u32[]{:S(2)}, u32[]{:S(2)}) collective-permute-start(f32[16,1024]{1,0:T(8,128)S(1)} %get-tuple-element.89.refs_0_), channel_id=1, source_target_pairs={{8,0},{9,1},{10,2},{11,3},{12,4},{13,5},{14,6},{15,7},{0,8},{1,9},... | collective-permute-start | bytes 196616 | tf_op jit(solution)/shard_map/ppermute | solution.py:31
  83.9 5.5 %collective-permute-start.22 = (f32[16,1024]{1,0:T(8,128)S(1)}, f32[16,1024]{1,0:T(8,128)S(1)}, u32[]{:S(2)}, u32[]{:S(2)}) collective-permute-start(f32[16,1024]{1,0:T(8,128)S(1)} %get-tuple-element.89.refs_0_), channel_id=1, source_target_pairs={{12,0},{13,1},{14,2},{15,3},{0,4},{1,5},{2,6},{3,7},{4,8},{5,9},{6... | collective-permute-start | bytes 196616 | tf_op jit(solution)/shard_map/ppermute | solution.py:31
  86.5 4.3 %collective-permute-start.21 = (f32[16,1024]{1,0:T(8,128)S(1)}, f32[16,1024]{1,0:T(8,128)S(1)}, u32[]{:S(2)}, u32[]{:S(2)}) collective-permute-start(f32[16,1024]{1,0:T(8,128)S(1)} %get-tuple-element.89.refs_0_), channel_id=1, source_target_pairs={{4,0},{5,1},{6,2},{7,3},{8,4},{9,5},{10,6},{11,7},{12,8},{13,9},{1... | collective-permute-start | bytes 196616 | tf_op jit(solution)/shard_map/ppermute | solution.py:31
  90.9 9.0 %collective-permute-start.26 = (f32[16,1024]{1,0:T(8,128)S(1)}, f32[16,1024]{1,0:T(8,128)S(1)}, u32[]{:S(2)}, u32[]{:S(2)}) collective-permute-start(f32[16,1024]{1,0:T(8,128)S(1)} %merge.1.s0), channel_id=1, source_target_pairs={{2,0},{3,1},{0,2},{1,3},{6,4},{7,5},{4,6},{5,7},{10,8},{11,9},{8,1... | collective-permute-start | bytes 196616 | tf_op jit(solution)/shard_map/ppermute | solution.py:45
  93.4 6.4 %collective-permute-start.25 = (f32[16,1024]{1,0:T(8,128)S(1)}, f32[16,1024]{1,0:T(8,128)S(1)}, u32[]{:S(2)}, u32[]{:S(2)}) collective-permute-start(f32[16,1024]{1,0:T(8,128)S(1)} %merge.1.s0), channel_id=1, source_target_pairs={{66,0},{67,1},{64,2},{65,3},{70,4},{71,5},{68,6},{69,7},{74,8},{75... | collective-permute-start | bytes 196616 | tf_op jit(solution)/shard_map/ppermute | solution.py:45
  95.1 4.8 %collective-permute-start.24 = (f32[16,1024]{1,0:T(8,128)S(1)}, f32[16,1024]{1,0:T(8,128)S(1)}, u32[]{:S(2)}, u32[]{:S(2)}) collective-permute-start(f32[16,1024]{1,0:T(8,128)S(1)} %merge.1.s0), channel_id=1, source_target_pairs={{64,0},{65,1},{66,2},{67,3},{68,4},{69,5},{70,6},{71,7},{72,8},{73... | collective-permute-start | bytes 196616 | tf_op jit(solution)/shard_map/ppermute | solution.py:45
  102.7 2.9 %collective-permute-start.27 = (f32[384,768]{1,0:T(8,128)S(1)}, f32[384,768]{1,0:T(8,128)S(1)}, u32[]{:S(2)}, u32[]{:S(2)}) collective-permute-start(f32[384,768]{1,0:T(8,128)S(1)} %get-tuple-element.100), channel_id=1, source_target_pairs={{0,1},{1,0},{2,3},{3,2},{4,5},{5,4},{6,7},{7,6},{8,9},{9,8},{10,11... | collective-permute-start | bytes 3538952 | tf_op jit(solution)/shard_map/ppermute | solution.py:26
  105.8 6.8 %collective-permute-start.28 = (bf16[96,768]{1,0:T(8,128)(2,1)S(1)}, bf16[96,768]{1,0:T(8,128)(2,1)S(1)}, u32[]{:S(2)}, u32[]{:S(2)}) collective-permute-start(bf16[96,768]{1,0:T(8,128)(2,1)S(1)} %get-tuple-element.102), channel_id=1, source_target_pairs={{32,0},{9,1},{34,2},{11,3},{36,4},{13,5},{38,6},{15,7},{40,8},{1,9... | collective-permute-start | bytes 442376 | tf_op jit(solution)/shard_map/ppermute | solution.py:56
  107.3 6.8 %collective-permute-start.29 = (bf16[96,768]{1,0:T(8,128)(2,1)S(1)}, bf16[96,768]{1,0:T(8,128)(2,1)S(1)}, u32[]{:S(2)}, u32[]{:S(2)}) collective-permute-start(bf16[96,768]{1,0:T(8,128)(2,1)S(1)} %get-tuple-element.103), channel_id=1, source_target_pairs={{48,0},{13,1},{50,2},{15,3},{52,4},{1,5},{54,6},{3,7},{56,8},{5,9}... | collective-permute-start | bytes 442376 | tf_op jit(solution)/shard_map/ppermute | solution.py:56
  110.0 5.1 %collective-permute-start.30 = (bf16[96,768]{1,0:T(8,128)(2,1)S(1)}, bf16[96,768]{1,0:T(8,128)(2,1)S(1)}, u32[]{:S(2)}, u32[]{:S(2)}) collective-permute-start(bf16[96,768]{1,0:T(8,128)(2,1)S(1)} %get-tuple-element.104), channel_id=1, source_target_pairs={{16,0},{5,1},{18,2},{7,3},{20,4},{9,5},{22,6},{11,7},{24,8},{13,9}... | collective-permute-start | bytes 442376 | tf_op jit(solution)/shard_map/ppermute | solution.py:56
  115.2 5.9 %collective-permute-start.31 = (f32[24,768]{1,0:T(8,128)S(1)}, f32[24,768]{1,0:T(8,128)S(1)}, u32[]{:S(2)}, u32[]{:S(2)}) collective-permute-start(f32[24,768]{1,0:T(8,128)S(1)} %get-tuple-element.106), channel_id=1, source_target_pairs={{8,0},{33,1},{10,2},{35,3},{12,4},{37,5},{14,6},{39,7},{0,8},{41,9... | collective-permute-start | bytes 221192 | tf_op jit(solution)/shard_map/ppermute | solution.py:56
  116.7 5.6 %collective-permute-start.32 = (f32[24,768]{1,0:T(8,128)S(1)}, f32[24,768]{1,0:T(8,128)S(1)}, u32[]{:S(2)}, u32[]{:S(2)}) collective-permute-start(f32[24,768]{1,0:T(8,128)S(1)} %get-tuple-element.107), channel_id=1, source_target_pairs={{12,0},{49,1},{14,2},{51,3},{0,4},{53,5},{2,6},{55,7},{4,8},{57,9}... | collective-permute-start | bytes 221192 | tf_op jit(solution)/shard_map/ppermute | solution.py:56
  117.9 4.4 %collective-permute-start.33 = (f32[24,768]{1,0:T(8,128)S(1)}, f32[24,768]{1,0:T(8,128)S(1)}, u32[]{:S(2)}, u32[]{:S(2)}) collective-permute-start(f32[24,768]{1,0:T(8,128)S(1)} %get-tuple-element.108), channel_id=1, source_target_pairs={{4,0},{17,1},{6,2},{19,3},{8,4},{21,5},{10,6},{23,7},{12,8},{25,9}... | collective-permute-start | bytes 221192 | tf_op jit(solution)/shard_map/ppermute | solution.py:56
  122.3 5.4 %collective-permute-start.34 = (f32[6,768]{1,0:T(8,128)S(1)}, f32[6,768]{1,0:T(8,128)S(1)}, u32[]{:S(2)}, u32[]{:S(2)}) collective-permute-start(f32[6,768]{1,0:T(8,128)S(1)} %get-tuple-element.110), channel_id=1, source_target_pairs={{2,0},{3,1},{0,2},{1,3},{6,4},{7,5},{4,6},{5,7},{10,8},{11,9},{8,1... | collective-permute-start | bytes 55304 | tf_op jit(solution)/shard_map/ppermute | solution.py:45
  122.9 5.1 %collective-permute-start.35 = (f32[6,768]{1,0:T(8,128)S(1)}, f32[6,768]{1,0:T(8,128)S(1)}, u32[]{:S(2)}, u32[]{:S(2)}) collective-permute-start(f32[6,768]{1,0:T(8,128)S(1)} %get-tuple-element.111), channel_id=1, source_target_pairs={{66,0},{67,1},{64,2},{65,3},{70,4},{71,5},{68,6},{69,7},{74,8},{75... | collective-permute-start | bytes 55304 | tf_op jit(solution)/shard_map/ppermute | solution.py:45
  125.5 3.8 %collective-permute-start.36 = (f32[6,768]{1,0:T(8,128)S(1)}, f32[6,768]{1,0:T(8,128)S(1)}, u32[]{:S(2)}, u32[]{:S(2)}) collective-permute-start(f32[6,768]{1,0:T(8,128)S(1)} %get-tuple-element.112), channel_id=1, source_target_pairs={{64,0},{65,1},{66,2},{67,3},{68,4},{69,5},{70,6},{71,7},{72,8},{73... | collective-permute-start | bytes 55304 | tf_op jit(solution)/shard_map/ppermute | solution.py:45

commit v6 on v5

--- a/solution.py
+++ b/solution.py
@@ -480,7 +480,8 @@
     def some(index, _):
         source = pl.ds(pl.multiple_of(low + index * rows, 64), rows)
         here_rows = pl.ds(pl.multiple_of(index * rows, 64), rows)
-        out[here_rows, :] = jnp.dot(turned[source, :], d_summed[...], preferred_element_type=jnp.float32)
+        product = jnp.dot(turned[source, :], d_summed[...], preferred_element_type=jnp.float32)
+        out[here_rows, :] = product.astype(out.dtype)
 
     lax.fori_loop(0, out.shape[0] // rows, some, None)
 
@@ -587,7 +588,7 @@
     half = width // 2
     send, d_summed, loss = call(
         grad_kernel,
-        (f32(half, width), bf16(docs * tb, width), f32(8, 128)),
+        (bf16(half, width), bf16(docs * tb, width), f32(8, 128)),
         [SMEM] + [VMEM] * 14,
         (VMEM,) * 3,
         flops=docs * tb * width * width,

time: 130 us -> 130 us (level)
  transfers between devices with their start and end apart: 37 -> 37, of which waited for: 22 -> 22; matrix products, arithmetic and copies ran while one was open for 1% -> 1% of each run, Pallas kernels for 25% -> 26%
where the time goes in v6:
time: 130 us; the launch traced here: 129 us
  starting transfers between devices  59.3 us (46%)
  Pallas kernels  44.6 us (34%)
  waiting for transfers between devices  22.3 us (17%)
  local copies, waits for them, and re-layouts  1.77 us (1%)
    pallas_call x3, Pallas kernels, attend(): call(functools.partial(attend_kernel, first), out_shape, in_specs, out_sp...  23.9 us
    ppermute x9, starting transfers between devices, from_z(): return lax.ppermute(value, ('dp', 'ctx'), pairs)  14.1 us
    ppermute x3, starting transfers between devices, shards(): fetch = lambda part: lax.ppermute(part, 'ctx', ring)  11.3 us
    ppermute x6, starting transfers between devices, from_y(): lax.ppermute(value, 'dp', [(d & 4 | d + k & 3, d) for d in range(lax.axis...  10.6 us
    ppermute x6, starting transfers between devices, from_plane(): return lax.ppermute(value, ('dp', 'ctx'), pairs)  9.55 us
    ppermute x6, starting transfers between devices, from_x(): lax.ppermute(value, 'ctx', [((c + 4 * k) % size, c) for c in range(size)])  8.95 us
    pallas_call x1, Pallas kernels, prepare(): call(prepare_kernel, (bf16(docs, tb, 2 * width), bf16(width, docs * tb),...  7.17 us
    ppermute x6, waiting for transfers between devices, from_plane(): return lax.ppermute(value, ('dp', 'ctx'), pairs)  6.87 us
  transfers between devices with their start and end apart: 37, of which 22 were waited for; matrix products, arithmetic and copies ran while one was open for 1% of the time, Pallas kernels for 26%

profile of v6, /device:TPU:0, one launch (start us, length us, event | category | flops | bytes accessed | tf_op | source)
XLA Modules:
  0.0 129.0 jit_solution(13002188943141417988)
XLA Ops:
  0.7 1.7 %collective-permute-start.4 = (bf16[128,768]{1,0:T(8,128)(2,1)}, bf16[128,768]{1,0:T(8,128)(2,1)S(1)}, u32[]{:S(2)}, u32[]{:S(2)}) collective-permute-start(bf16[128,768]{1,0:T(8,128)(2,1)} %refs_4_), channel_id=1, source_target_pairs={{48,0},{0,16},{16,32},{32,48},{112,64},{64,80},{80,96},{96,112},{4... | collective-permute-start | bytes 589832 | tf_op jit(solution)/shard_map/ppermute | solution.py:35
  2.5 1.6 %collective-permute-start.3 = (bf16[128,768]{1,0:T(8,128)(2,1)}, bf16[128,768]{1,0:T(8,128)(2,1)S(1)}, u32[]{:S(2)}, u32[]{:S(2)}) collective-permute-start(bf16[128,768]{1,0:T(8,128)(2,1)} %refs_4_), channel_id=1, source_target_pairs={{16,0},{32,16},{48,32},{0,48},{80,64},{96,80},{112,96},{64,112},{1... | collective-permute-start | bytes 589832 | tf_op jit(solution)/shard_map/ppermute | solution.py:35
  4.0 1.2 fusion
  5.2 5.8 %collective-permute-start.2 = (bf16[1,256,768]{2,1,0:T(8,128)(2,1)S(1)}, bf16[1,256,768]{2,1,0:T(8,128)(2,1)S(1)}, u32[]{:S(2)}, u32[]{:S(2)}) collective-permute-start(bf16[1,256,768]{2,1,0:T(8,128)(2,1)S(1)} %get-tuple-element.113), channel_id=1, source_target_pairs={{0,15},{1,2},{2,1},{3,4},{4,3},{5,6},{6,5},{7,8},{8,7},{9,10},{10,... | collective-permute-start | bytes 1179656 | tf_op jit(solution)/shard_map/ppermute | solution.py:517
  11.2 7.2 %prepare.1 = (bf16[4,256,1536]{2,1,0:T(8,128)(2,1)S(1)}, bf16[768,1024]{1,0:T(8,128)(2,1)S(1)}, bf16[768,768]{1,0:T(8,128)(2,1)S(1)}) custom-call(bf16[4,256,768]{2,1,0:T(8,128)(2,1)} %refs_1_.5, bf16[768,2304]{1,0:T(8,128)(2,1)} %refs_7_.5), custom_call_target="tpu_custom_call" | custom-call | flops 3623878656 | bytes 11534336 | tf_op jit(solution)/shard_map/prepare/pallas_call | solution.py:259
  18.4 2.0 %collective-permute-start.5 = (bf16[128,768]{1,0:T(8,128)(2,1)S(1)}, bf16[128,768]{1,0:T(8,128)(2,1)S(1)}, u32[]{:S(2)}, u32[]{:S(2)}) collective-permute-start(bf16[128,768]{1,0:T(8,128)(2,1)S(1)} %copy-done.4), channel_id=1, source_target_pairs={{32,0},{48,16},{0,32},{16,48},{96,64},{112,80},{64,96},{80,112},{3... | collective-permute-start | bytes 589832 | tf_op jit(solution)/shard_map/ppermute | solution.py:35
  20.4 3.1 %near.1 = (bf16[4,256,768]{2,1,0:T(8,128)(2,1)S(1)}, bf16[768,1024]{1,0:T(8,128)(2,1)S(1)}) custom-call(bf16[4,256,768]{2,1,0:T(8,128)(2,1)S(1)} %collective-permute-done.near, bf16[768,2304]{1,0:T(8,128)(2,1)S(1)} %copy-done, bf16[768,768]{1,0:T(8,128)(2,1)S(1)} %get-tuple-element.58.w_v_turned.refs_8_), custom_call_target="tpu_custom_call" | custom-call | flops 2415919104 | bytes 4194304 | tf_op jit(solution)/shard_map/near/pallas_call | solution.py:522
  23.6 6.1 %attend.3 = (bf16[4,256,768]{2,1,0:T(8,128)(2,1)}, bf16[768,1024]{1,0:T(8,128)(2,1)S(1)}, bf16[4,256,768]{2,1,0:T(8,128)(2,1)S(1)}, f32[4,256,128]{2,1,0:T(8,128)S(1)}, f32[4,1,768]{2,1,0:T(1,128)S(1)}) custom-call(s32[4]{0:T(128)S(1)} %copy-done.6, bf16[4,256,768]{2,1,0:T(8,128)(2,1)S(1)} %copy-done.2, bf16[4,256,768]{2,1,0:T(8,128)(2,1)S(1)} %get-tuple-element.59.refs_2_, ...), custom_call_target="tpu_custom_call" | custom-call | flops 1509949440 | bytes 4194304 | tf_op jit(solution)/shard_map/attend/pallas_call | solution.py:211
  29.7 4.0 %collective-permute-start.6 = (bf16[128,768]{1,0:T(8,128)(2,1)S(1)}, bf16[128,768]{1,0:T(8,128)(2,1)S(1)}, u32[]{:S(2)}, u32[]{:S(2)}) collective-permute-start(bf16[128,768]{1,0:T(8,128)(2,1)S(1)} %copy-done.4), channel_id=1, source_target_pairs={{0,1},{1,0},{2,3},{3,2},{4,5},{5,4},{6,7},{7,6},{8,9},{9,8},{10,11... | collective-permute-start | bytes 589832 | tf_op jit(solution)/shard_map/ppermute | solution.py:26
  35.7 5.4 %collective-permute-start.10 = (bf16[1,256,768]{2,1,0:T(8,128)(2,1)S(1)}, bf16[1,256,768]{2,1,0:T(8,128)(2,1)S(1)}, u32[]{:S(2)}, u32[]{:S(2)}) collective-permute-start(bf16[1,256,768]{2,1,0:T(8,128)(2,1)S(1)} %get-tuple-element.69), channel_id=1, source_target_pairs={{0,15},{1,2},{2,1},{3,4},{4,3},{5,6},{6,5},{7,8},{8,7},{9,10},{10,... | collective-permute-start | bytes 1179656 | tf_op jit(solution)/shard_map/ppermute | solution.py:517
  41.2 11.7 %attend.4 = (bf16[4,256,768]{2,1,0:T(8,128)(2,1)}, bf16[768,1024]{1,0:T(8,128)(2,1)S(1)}, bf16[4,256,768]{2,1,0:T(8,128)(2,1)S(1)}, f32[4,256,128]{2,1,0:T(8,128)S(1)}, f32[4,1,768]{2,1,0:T(1,128)S(1)}) custom-call(s32[4]{0:T(128)S(1)} %copy-done.6, ...), custom_call_target="tpu_custom_call", output_to_operand_aliasing={{0}: (11, {}), {1}: (12, {}), {2}: (13, {}), {3}: (14, {}),... | custom-call | flops 3019898880 | bytes 4194304 | tf_op jit(solution)/shard_map/attend/pallas_call | solution.py:211
  52.9 6.1 %attend.5 = (bf16[4,256,768]{2,1,0:T(8,128)(2,1)}, bf16[768,1024]{1,0:T(8,128)(2,1)S(1)}, bf16[4,256,768]{2,1,0:T(8,128)(2,1)S(1)}, f32[4,256,128]{2,1,0:T(8,128)S(1)}, f32[4,1,768]{2,1,0:T(1,128)S(1)}) custom-call(s32[4]{0:T(128)S(1)} %copy-done.6, ...), custom_call_target="tpu_custom_call", output_to_operand_aliasing={{0}: (11, {}), {1}: (12, {}), {2}: (13, {}), {3}: (14, {}),... | custom-call | flops 1509949440 | bytes 4194304 | tf_op jit(solution)/shard_map/attend/pallas_call | solution.py:211
  59.1 1.2 collective-permute-done.11.refs_1_
  62.1 2.4 %collective-permute-start.12 = (f32[12,768]{1,0:T(8,128)S(1)}, f32[12,768]{1,0:T(8,128)S(1)}, u32[]{:S(2)}, u32[]{:S(2)}) collective-permute-start(f32[12,768]{1,0:T(8,128)S(1)} %add.3.refs_0_), channel_id=1, source_target_pairs={{4,0},{5,1},{6,2},{7,3},{8,4},{9,5},{10,6},{11,7},{12,8},{13,9},{1... | collective-permute-start | bytes 110600 | tf_op jit(solution)/shard_map/ppermute | solution.py:31
  64.5 1.7 %collective-permute-done.14.refs_3_ = f32[12,768]{1,0:T(8,128)S(1)} collective-permute-done((f32[12,768]{1,0:T(8,128)S(1)}, f32[12,768]{1,0:T(8,128)S(1)}, u32[]{:S(2)}, u32[]{:S(2)}) %collective-permute-start.14) | collective-permute-done | bytes 36896 | tf_op jit(solution)/shard_map/ppermute | solution.py:31
  66.8 1.3 %collective-permute-start.17 = (f32[12,768]{1,0:T(8,128)S(1)}, f32[12,768]{1,0:T(8,128)S(1)}, u32[]{:S(2)}, u32[]{:S(2)}) collective-permute-start(f32[12,768]{1,0:T(8,128)S(1)} %add.4.s0), channel_id=1, source_target_pairs={{2,0},{3,1},{0,2},{1,3},{6,4},{7,5},{4,6},{5,7},{10,8},{11,9},{8,1... | collective-permute-start | bytes 110600 | tf_op jit(solution)/shard_map/ppermute | solution.py:45
  68.2 1.0 collective-permute-start.16
  69.2 2.2 %collective-permute-start.15 = (f32[12,768]{1,0:T(8,128)S(1)}, f32[12,768]{1,0:T(8,128)S(1)}, u32[]{:S(2)}, u32[]{:S(2)}) collective-permute-start(f32[12,768]{1,0:T(8,128)S(1)} %add.4.s0), channel_id=1, source_target_pairs={{64,0},{65,1},{66,2},{67,3},{68,4},{69,5},{70,6},{71,7},{72,8},{73... | collective-permute-start | bytes 110600 | tf_op jit(solution)/shard_map/ppermute | solution.py:45
  71.4 1.6 %collective-permute-done.17.s2 = f32[12,768]{1,0:T(8,128)S(1)} collective-permute-done((f32[12,768]{1,0:T(8,128)S(1)}, f32[12,768]{1,0:T(8,128)S(1)}, u32[]{:S(2)}, u32[]{:S(2)}) %collective-permute-start.17) | collective-permute-done | bytes 36896 | tf_op jit(solution)/shard_map/ppermute | solution.py:45
  73.6 2.0 %collective-permute-start.20 = (f32[8,768]{1,0:T(8,128)S(1)}, f32[8,768]{1,0:T(8,128)S(1)}, u32[]{:S(2)}, u32[]{:S(2)}) collective-permute-start(f32[8,768]{1,0:T(8,128)S(1)} %get-tuple-element.84.refs_0_.emb), channel_id=1, source_target_pairs={{32,0},{48,16},{0,32},{16,48},{96,64},{112,80},{64,96},{80,112},{3... | collective-permute-start | bytes 73736 | tf_op jit(solution)/shard_map/ppermute | solution.py:35
  76.3 2.6 %collective-permute-start.18 = (f32[8,768]{1,0:T(8,128)S(1)}, f32[8,768]{1,0:T(8,128)S(1)}, u32[]{:S(2)}, u32[]{:S(2)}) collective-permute-start(f32[8,768]{1,0:T(8,128)S(1)} %get-tuple-element.84.refs_0_.emb), channel_id=1, source_target_pairs={{16,0},{32,16},{48,32},{0,48},{80,64},{96,80},{112,96},{64,112},{1... | collective-permute-start | bytes 73736 | tf_op jit(solution)/shard_map/ppermute | solution.py:35
  78.9 1.7 %collective-permute-done.19.refs_2_ = f32[8,768]{1,0:T(8,128)S(1)} collective-permute-done((f32[8,768]{1,0:T(8,128)S(1)}, f32[8,768]{1,0:T(8,128)S(1)}, u32[]{:S(2)}, u32[]{:S(2)}) %collective-permute-start.19) | collective-permute-done | bytes 24608 | tf_op jit(solution)/shard_map/ppermute | solution.py:35
  80.6 1.7 %score.1 = (f32[32,768]{1,0:T(8,128)S(1)}, f32[16,1024]{1,0:T(8,128)S(1)}) custom-call(s32[32]{0:T(128)S(1)} %copy-done.7, f32[8,768]{1,0:T(8,128)S(1)} %get-tuple-element.84.refs_0_.emb, f32[8,768]{1,0:T(8,128)S(1)} %collective-permute-done.18.refs_1_, f32[8,768]{1,0:T(8,128)S(1)} %collective-permute-done.19.refs_2_, ...), custom_call_target="tpu_custom_call" | custom-call | bytes 2097152 | tf_op jit(solution)/shard_map/score/pallas_call | solution.py:570
  82.4 1.5 %collective-permute-start.23 = (f32[16,1024]{1,0:T(8,128)S(1)}, f32[16,1024]{1,0:T(8,128)S(1)}, u32[]{:S(2)}, u32[]{:S(2)}) collective-permute-start(f32[16,1024]{1,0:T(8,128)S(1)} %get-tuple-element.89.refs_0_), channel_id=1, source_target_pairs={{8,0},{9,1},{10,2},{11,3},{12,4},{13,5},{14,6},{15,7},{0,8},{1,9},... | collective-permute-start | bytes 196616 | tf_op jit(solution)/shard_map/ppermute | solution.py:31
  83.9 2.6 %collective-permute-start.22 = (f32[16,1024]{1,0:T(8,128)S(1)}, f32[16,1024]{1,0:T(8,128)S(1)}, u32[]{:S(2)}, u32[]{:S(2)}) collective-permute-start(f32[16,1024]{1,0:T(8,128)S(1)} %get-tuple-element.89.refs_0_), channel_id=1, source_target_pairs={{12,0},{13,1},{14,2},{15,3},{0,4},{1,5},{2,6},{3,7},{4,8},{5,9},{6... | collective-permute-start | bytes 196616 | tf_op jit(solution)/shard_map/ppermute | solution.py:31
  87.1 1.1 collective-permute-done.23.refs_3_
  88.2 1.2 collective-permute-done.22.refs_2_
  89.4 1.4 %collective-permute-done.21.refs_1_ = f32[16,1024]{1,0:T(8,128)S(1)} collective-permute-done((f32[16,1024]{1,0:T(8,128)S(1)}, f32[16,1024]{1,0:T(8,128)S(1)}, u32[]{:S(2)}, u32[]{:S(2)}) %collective-permute-start.21) | collective-permute-done | bytes 65568 | tf_op jit(solution)/shard_map/ppermute | solution.py:31
  90.9 2.5 %collective-permute-start.26 = (f32[16,1024]{1,0:T(8,128)S(1)}, f32[16,1024]{1,0:T(8,128)S(1)}, u32[]{:S(2)}, u32[]{:S(2)}) collective-permute-start(f32[16,1024]{1,0:T(8,128)S(1)} %merge.1.s0), channel_id=1, source_target_pairs={{2,0},{3,1},{0,2},{1,3},{6,4},{7,5},{4,6},{5,7},{10,8},{11,9},{8,1... | collective-permute-start | bytes 196616 | tf_op jit(solution)/shard_map/ppermute | solution.py:45
  93.4 1.6 %collective-permute-start.25 = (f32[16,1024]{1,0:T(8,128)S(1)}, f32[16,1024]{1,0:T(8,128)S(1)}, u32[]{:S(2)}, u32[]{:S(2)}) collective-permute-start(f32[16,1024]{1,0:T(8,128)S(1)} %merge.1.s0), channel_id=1, source_target_pairs={{66,0},{67,1},{64,2},{65,3},{70,4},{71,5},{68,6},{69,7},{74,8},{75... | collective-permute-start | bytes 196616 | tf_op jit(solution)/shard_map/ppermute | solution.py:45
  95.1 1.6 %collective-permute-start.24 = (f32[16,1024]{1,0:T(8,128)S(1)}, f32[16,1024]{1,0:T(8,128)S(1)}, u32[]{:S(2)}, u32[]{:S(2)}) collective-permute-start(f32[16,1024]{1,0:T(8,128)S(1)} %merge.1.s0), channel_id=1, source_target_pairs={{64,0},{65,1},{66,2},{67,3},{68,4},{69,5},{70,6},{71,7},{72,8},{73... | collective-permute-start | bytes 196616 | tf_op jit(solution)/shard_map/ppermute | solution.py:45
  96.7 2.9 %turn.1.turned = bf16[768,1024]{1,0:T(8,128)(2,1)S(1)} custom-call(bf16[768,1024]{1,0:T(8,128)(2,1)S(1)} %get-tuple-element.97.mixed), custom_call_target="tpu_custom_call" | custom-call | flops 1207959552 | bytes 4194304 | tf_op jit(solution)/shard_map/turn/pallas_call | solution.py:545
  99.9 2.8 %grad.1 = (bf16[384,768]{1,0:T(8,128)(2,1)S(1)}, bf16[1024,768]{1,0:T(8,128)(2,1)S(1)}, f32[8,128]{1,0:T(8,128)S(1)}) custom-call(s32[4]{0:T(128)S(1)} %copy-done.6, f32[16,1024]{1,0:T(8,128)S(1)} %merge.1.s0, f32[16,1024]{1,0:T(8,128)S(1)} %collective-permute-done.24.s1, f32[16,1024]{1,0:T(8,128)S(1)} %collective-permute-done.25.s2, ...), custom_call_target="tpu_custom_call" | custom-call | flops 603979776 | bytes 8388608 | tf_op jit(solution)/shard_map/grad/pallas_call | solution.py:589
  102.8 1.0 keep.1.refs_0_
  103.8 1.0 collective-permute-done.27.refs_1_
  104.9 1.5 %collective-permute-start.28 = (bf16[96,768]{1,0:T(8,128)(2,1)S(1)}, bf16[96,768]{1,0:T(8,128)(2,1)S(1)}, u32[]{:S(2)}, u32[]{:S(2)}) collective-permute-start(bf16[96,768]{1,0:T(8,128)(2,1)S(1)} %get-tuple-element.102), channel_id=1, source_target_pairs={{32,0},{9,1},{34,2},{11,3},{36,4},{13,5},{38,6},{15,7},{40,8},{1,9... | collective-permute-start | bytes 442376 | tf_op jit(solution)/shard_map/ppermute | solution.py:56
  106.4 2.6 %collective-permute-start.29 = (bf16[96,768]{1,0:T(8,128)(2,1)S(1)}, bf16[96,768]{1,0:T(8,128)(2,1)S(1)}, u32[]{:S(2)}, u32[]{:S(2)}) collective-permute-start(bf16[96,768]{1,0:T(8,128)(2,1)S(1)} %get-tuple-element.103), channel_id=1, source_target_pairs={{48,0},{13,1},{50,2},{15,3},{52,4},{1,5},{54,6},{3,7},{56,8},{5,9}... | collective-permute-start | bytes 442376 | tf_op jit(solution)/shard_map/ppermute | solution.py:56
  109.6 2.0 %collective-permute-done.28.refs_1_ = bf16[96,768]{1,0:T(8,128)(2,1)S(1)} collective-permute-done((bf16[96,768]{1,0:T(8,128)(2,1)S(1)}, bf16[96,768]{1,0:T(8,128)(2,1)S(1)}, u32[]{:S(2)}, u32[]{:S(2)}) %collective-permute-start.28) | collective-permute-done | bytes 147488 | tf_op jit(solution)/shard_map/ppermute | solution.py:56
  111.6 1.5 %collective-permute-done.29.refs_2_ = bf16[96,768]{1,0:T(8,128)(2,1)S(1)} collective-permute-done((bf16[96,768]{1,0:T(8,128)(2,1)S(1)}, bf16[96,768]{1,0:T(8,128)(2,1)S(1)}, u32[]{:S(2)}, u32[]{:S(2)}) %collective-permute-start.29) | collective-permute-done | bytes 147488 | tf_op jit(solution)/shard_map/ppermute | solution.py:56
  113.2 1.0 collective-permute-done.30.refs_3_
  114.3 1.5 %collective-permute-start.31 = (f32[24,768]{1,0:T(8,128)S(1)}, f32[24,768]{1,0:T(8,128)S(1)}, u32[]{:S(2)}, u32[]{:S(2)}) collective-permute-start(f32[24,768]{1,0:T(8,128)S(1)} %get-tuple-element.106), channel_id=1, source_target_pairs={{8,0},{33,1},{10,2},{35,3},{12,4},{37,5},{14,6},{39,7},{0,8},{41,9... | collective-permute-start | bytes 221192 | tf_op jit(solution)/shard_map/ppermute | solution.py:56
  115.8 1.2 collective-permute-start.32
  117.0 2.0 %collective-permute-start.33 = (f32[24,768]{1,0:T(8,128)S(1)}, f32[24,768]{1,0:T(8,128)S(1)}, u32[]{:S(2)}, u32[]{:S(2)}) collective-permute-start(f32[24,768]{1,0:T(8,128)S(1)} %get-tuple-element.108), channel_id=1, source_target_pairs={{4,0},{17,1},{6,2},{19,3},{8,4},{21,5},{10,6},{23,7},{12,8},{25,9}... | collective-permute-start | bytes 221192 | tf_op jit(solution)/shard_map/ppermute | solution.py:56
  119.0 1.2 collective-permute-done.31.refs_1_
  120.2 1.2 collective-permute-done.32.refs_2_
  121.9 2.6 %collective-permute-start.35 = (f32[6,768]{1,0:T(8,128)S(1)}, f32[6,768]{1,0:T(8,128)S(1)}, u32[]{:S(2)}, u32[]{:S(2)}) collective-permute-start(f32[6,768]{1,0:T(8,128)S(1)} %get-tuple-element.111), channel_id=1, source_target_pairs={{66,0},{67,1},{64,2},{65,3},{70,4},{71,5},{68,6},{69,7},{74,8},{75... | collective-permute-start | bytes 55304 | tf_op jit(solution)/shard_map/ppermute | solution.py:45
  125.7 1.1 collective-permute-done.34.refs_1_
  127.1 1.3 %collective-permute-done.36.refs_3_ = f32[6,768]{1,0:T(8,128)S(1)} collective-permute-done((f32[6,768]{1,0:T(8,128)S(1)}, f32[6,768]{1,0:T(8,128)S(1)}, u32[]{:S(2)}, u32[]{:S(2)}) %collective-permute-start.36) | collective-permute-done | bytes 18464 | tf_op jit(solution)/shard_map/ppermute | solution.py:45
  (65 shorter events, 10.6 us)
Async XLA Ops:
  0.6 10.3 %copy-start.1 = (bf16[4,256,768]{2,1,0:T(8,128)(2,1)S(1)}, bf16[4,256,768]{2,1,0:T(8,128)(2,1)}, u32[]{:S(2)}) copy-start(bf16[4,256,768]{2,1,0:T(8,128)(2,1)} %refs_1_.5) | copy-start | bytes 4718596
  0.6 17.7 %collective-permute-start = (bf16[4,256,768]{2,1,0:T(8,128)(2,1)}, bf16[4,256,768]{2,1,0:T(8,128)(2,1)S(1)}, u32[]{:S(2)}, u32[]{:S(2)}) collective-permute-start(bf16[4,256,768]{2,1,0:T(8,128)(2,1)} %refs_1_.5), channel_id=1, source_target_pairs={{0,1},{1,0},{2,3},{3,2},{4,5},{5,4},{6,7},{7,6},{8,9},{9,8},{10,11... | collective-permute-start | bytes 4718600 | tf_op jit(solution)/shard_map/ppermute | solution.py:26
  0.7 29.0 %collective-permute-start.4 = (bf16[128,768]{1,0:T(8,128)(2,1)}, bf16[128,768]{1,0:T(8,128)(2,1)S(1)}, u32[]{:S(2)}, u32[]{:S(2)}) collective-permute-start(bf16[128,768]{1,0:T(8,128)(2,1)} %refs_4_), channel_id=1, source_target_pairs={{48,0},{0,16},{16,32},{32,48},{112,64},{64,80},{80,96},{96,112},{4... | collective-permute-start | bytes 589832 | tf_op jit(solution)/shard_map/ppermute | solution.py:35
  2.5 27.3 %collective-permute-start.3 = (bf16[128,768]{1,0:T(8,128)(2,1)}, bf16[128,768]{1,0:T(8,128)(2,1)S(1)}, u32[]{:S(2)}, u32[]{:S(2)}) collective-permute-start(bf16[128,768]{1,0:T(8,128)(2,1)} %refs_4_), channel_id=1, source_target_pairs={{16,0},{32,16},{48,32},{0,48},{80,64},{96,80},{112,96},{64,112},{1... | collective-permute-start | bytes 589832 | tf_op jit(solution)/shard_map/ppermute | solution.py:35
  5.2 18.3 %collective-permute-start.2 = (bf16[1,256,768]{2,1,0:T(8,128)(2,1)S(1)}, bf16[1,256,768]{2,1,0:T(8,128)(2,1)S(1)}, u32[]{:S(2)}, u32[]{:S(2)}) collective-permute-start(bf16[1,256,768]{2,1,0:T(8,128)(2,1)S(1)} %get-tuple-element.113), channel_id=1, source_target_pairs={{0,15},{1,2},{2,1},{3,4},{4,3},{5,6},{6,5},{7,8},{8,7},{9,10},{10,... | collective-permute-start | bytes 1179656 | tf_op jit(solution)/shard_map/ppermute | solution.py:517
  11.0 7.3 %copy-start.4 = (bf16[128,768]{1,0:T(8,128)(2,1)S(1)}, bf16[128,768]{1,0:T(8,128)(2,1)}, u32[]{:S(2)}) copy-start(bf16[128,768]{1,0:T(8,128)(2,1)} %refs_4_) | copy-start | bytes 589828
  11.0 9.3 %copy-start = (bf16[768,2304]{1,0:T(8,128)(2,1)S(1)}, bf16[768,2304]{1,0:T(8,128)(2,1)}, u32[]{:S(2)}) copy-start(bf16[768,2304]{1,0:T(8,128)(2,1)} %refs_7_.5) | copy-start | bytes 10616836
  11.1 24.0 %collective-permute-start.1 = (bf16[2,256,768]{2,1,0:T(8,128)(2,1)S(1)}, bf16[2,256,768]{2,1,0:T(8,128)(2,1)S(1)}, u32[]{:S(2)}, u32[]{:S(2)}) collective-permute-start(bf16[2,256,768]{2,1,0:T(8,128)(2,1)S(1)} %slice.12), channel_id=1, source_target_pairs={{0,15},{1,2},{2,1},{3,4},{4,3},{5,6},{6,5},{7,8},{8,7},{9,10},{10,... | collective-permute-start | bytes 2359304 | tf_op jit(solution)/shard_map/ppermute | solution.py:517
  18.4 11.4 %collective-permute-start.5 = (bf16[128,768]{1,0:T(8,128)(2,1)S(1)}, bf16[128,768]{1,0:T(8,128)(2,1)S(1)}, u32[]{:S(2)}, u32[]{:S(2)}) collective-permute-start(bf16[128,768]{1,0:T(8,128)(2,1)S(1)} %copy-done.4), channel_id=1, source_target_pairs={{32,0},{48,16},{0,32},{16,48},{96,64},{112,80},{64,96},{80,112},{3... | collective-permute-start | bytes 589832 | tf_op jit(solution)/shard_map/ppermute | solution.py:35
  20.4 3.2 %copy-start.2 = (bf16[4,256,768]{2,1,0:T(8,128)(2,1)S(1)}, bf16[4,256,768]{2,1,0:T(8,128)(2,1)}, u32[]{:S(2)}) copy-start(bf16[4,256,768]{2,1,0:T(8,128)(2,1)} %refs_1_.5) | copy-start | bytes 4718596
  20.4 3.2 %copy-start.3 = (bf16[768,768]{1,0:T(8,128)(2,1)S(1)}, bf16[768,768]{1,0:T(8,128)(2,1)}, u32[]{:S(2)}) copy-start(bf16[768,768]{1,0:T(8,128)(2,1)} %refs_9_.5) | copy-start | bytes 3538948
  20.4 3.2 %copy-start.5 = (f32[768]{0:T(1024)S(1)}, f32[768]{0:T(1024)}, u32[]{:S(2)}) copy-start(f32[768]{0:T(1024)} %gain.1) | copy-start | bytes 9220
  20.4 3.2 %copy-start.6 = (s32[4]{0:T(128)S(1)}, s32[4]{0:T(128)}, u32[]{:S(2)}) copy-start(s32[4]{0:T(128)} %lengths.1) | copy-start | bytes 52
  23.6 10.7 %copy-start.7 = (s32[32]{0:T(128)S(1)}, s32[32]{0:T(128)}, u32[]{:S(2)}) copy-start(s32[32]{0:T(128)} %positive.2) | copy-start | bytes 388
  29.7 5.3 %collective-permute-start.6 = (bf16[128,768]{1,0:T(8,128)(2,1)S(1)}, bf16[128,768]{1,0:T(8,128)(2,1)S(1)}, u32[]{:S(2)}, u32[]{:S(2)}) collective-permute-start(bf16[128,768]{1,0:T(8,128)(2,1)S(1)} %copy-done.4), channel_id=1, source_target_pairs={{0,1},{1,0},{2,3},{3,2},{4,5},{5,4},{6,7},{7,6},{8,9},{9,8},{10,11... | collective-permute-start | bytes 589832 | tf_op jit(solution)/shard_map/ppermute | solution.py:26
  33.7 1.4 %collective-permute-start.7 = (bf16[128,768]{1,0:T(8,128)(2,1)S(1)}, bf16[128,768]{1,0:T(8,128)(2,1)S(1)}, u32[]{:S(2)}, u32[]{:S(2)}) collective-permute-start(bf16[128,768]{1,0:T(8,128)(2,1)S(1)} %collective-permute-done.3.refs_1_.refs_5_), channel_id=1, source_target_pairs={{0,1},{1,0},{2,3},{3,2},{4,5},{5,4},{6,7},{7,6},{8,9},{9,8},{10,11... | collective-permute-start | bytes 589832 | tf_op jit(solution)/shard_map/ppermute | solution.py:26
  33.8 1.6 %collective-permute-start.8 = (bf16[128,768]{1,0:T(8,128)(2,1)S(1)}, bf16[128,768]{1,0:T(8,128)(2,1)S(1)}, u32[]{:S(2)}, u32[]{:S(2)}) collective-permute-start(bf16[128,768]{1,0:T(8,128)(2,1)S(1)} %collective-permute-done.4.refs_2_.refs_6_), channel_id=1, source_target_pairs={{0,1},{1,0},{2,3},{3,2},{4,5},{5,4},{6,7},{7,6},{8,9},{9,8},{10,11... | collective-permute-start | bytes 589832 | tf_op jit(solution)/shard_map/ppermute | solution.py:26
  34.2 1.5 %collective-permute-start.9 = (bf16[128,768]{1,0:T(8,128)(2,1)S(1)}, bf16[128,768]{1,0:T(8,128)(2,1)S(1)}, u32[]{:S(2)}, u32[]{:S(2)}) collective-permute-start(bf16[128,768]{1,0:T(8,128)(2,1)S(1)} %collective-permute-done.5.refs_3_.refs_7_), channel_id=1, source_target_pairs={{0,1},{1,0},{2,3},{3,2},{4,5},{5,4},{6,7},{7,6},{8,9},{9,8},{10,11... | collective-permute-start | bytes 589832 | tf_op jit(solution)/shard_map/ppermute | solution.py:26
  35.7 17.1 %collective-permute-start.10 = (bf16[1,256,768]{2,1,0:T(8,128)(2,1)S(1)}, bf16[1,256,768]{2,1,0:T(8,128)(2,1)S(1)}, u32[]{:S(2)}, u32[]{:S(2)}) collective-permute-start(bf16[1,256,768]{2,1,0:T(8,128)(2,1)S(1)} %get-tuple-element.69), channel_id=1, source_target_pairs={{0,15},{1,2},{2,1},{3,4},{4,3},{5,6},{6,5},{7,8},{8,7},{9,10},{10,... | collective-permute-start | bytes 1179656 | tf_op jit(solution)/shard_map/ppermute | solution.py:517
  59.0 1.3 %collective-permute-start.11 = (f32[12,768]{1,0:T(8,128)S(1)}, f32[12,768]{1,0:T(8,128)S(1)}, u32[]{:S(2)}, u32[]{:S(2)}) collective-permute-start(f32[12,768]{1,0:T(8,128)S(1)} %stack.1.refs_0_), channel_id=1, source_target_pairs={{0,1},{1,0},{2,3},{3,2},{4,5},{5,4},{6,7},{7,6},{8,9},{9,8},{10,11... | collective-permute-start | bytes 110600 | tf_op jit(solution)/shard_map/ppermute | solution.py:26
  60.3 5.9 %collective-permute-start.14 = (f32[12,768]{1,0:T(8,128)S(1)}, f32[12,768]{1,0:T(8,128)S(1)}, u32[]{:S(2)}, u32[]{:S(2)}) collective-permute-start(f32[12,768]{1,0:T(8,128)S(1)} %add.3.refs_0_), channel_id=1, source_target_pairs={{8,0},{9,1},{10,2},{11,3},{12,4},{13,5},{14,6},{15,7},{0,8},{1,9},... | collective-permute-start | bytes 110600 | tf_op jit(solution)/shard_map/ppermute | solution.py:31
  61.3 5.5 %collective-permute-start.13 = (f32[12,768]{1,0:T(8,128)S(1)}, f32[12,768]{1,0:T(8,128)S(1)}, u32[]{:S(2)}, u32[]{:S(2)}) collective-permute-start(f32[12,768]{1,0:T(8,128)S(1)} %add.3.refs_0_), channel_id=1, source_target_pairs={{12,0},{13,1},{14,2},{15,3},{0,4},{1,5},{2,6},{3,7},{4,8},{5,9},{6... | collective-permute-start | bytes 110600 | tf_op jit(solution)/shard_map/ppermute | solution.py:31
  62.1 4.7 %collective-permute-start.12 = (f32[12,768]{1,0:T(8,128)S(1)}, f32[12,768]{1,0:T(8,128)S(1)}, u32[]{:S(2)}, u32[]{:S(2)}) collective-permute-start(f32[12,768]{1,0:T(8,128)S(1)} %add.3.refs_0_), channel_id=1, source_target_pairs={{4,0},{5,1},{6,2},{7,3},{8,4},{9,5},{10,6},{11,7},{12,8},{13,9},{1... | collective-permute-start | bytes 110600 | tf_op jit(solution)/shard_map/ppermute | solution.py:31
  66.8 6.1 %collective-permute-start.17 = (f32[12,768]{1,0:T(8,128)S(1)}, f32[12,768]{1,0:T(8,128)S(1)}, u32[]{:S(2)}, u32[]{:S(2)}) collective-permute-start(f32[12,768]{1,0:T(8,128)S(1)} %add.4.s0), channel_id=1, source_target_pairs={{2,0},{3,1},{0,2},{1,3},{6,4},{7,5},{4,6},{5,7},{10,8},{11,9},{8,1... | collective-permute-start | bytes 110600 | tf_op jit(solution)/shard_map/ppermute | solution.py:45
  68.2 5.3 %collective-permute-start.16 = (f32[12,768]{1,0:T(8,128)S(1)}, f32[12,768]{1,0:T(8,128)S(1)}, u32[]{:S(2)}, u32[]{:S(2)}) collective-permute-start(f32[12,768]{1,0:T(8,128)S(1)} %add.4.s0), channel_id=1, source_target_pairs={{66,0},{67,1},{64,2},{65,3},{70,4},{71,5},{68,6},{69,7},{74,8},{75... | collective-permute-start | bytes 110600 | tf_op jit(solution)/shard_map/ppermute | solution.py:45
  69.2 4.3 %collective-permute-start.15 = (f32[12,768]{1,0:T(8,128)S(1)}, f32[12,768]{1,0:T(8,128)S(1)}, u32[]{:S(2)}, u32[]{:S(2)}) collective-permute-start(f32[12,768]{1,0:T(8,128)S(1)} %add.4.s0), channel_id=1, source_target_pairs={{64,0},{65,1},{66,2},{67,3},{68,4},{69,5},{70,6},{71,7},{72,8},{73... | collective-permute-start | bytes 110600 | tf_op jit(solution)/shard_map/ppermute | solution.py:45
  73.6 5.3 %collective-permute-start.20 = (f32[8,768]{1,0:T(8,128)S(1)}, f32[8,768]{1,0:T(8,128)S(1)}, u32[]{:S(2)}, u32[]{:S(2)}) collective-permute-start(f32[8,768]{1,0:T(8,128)S(1)} %get-tuple-element.84.refs_0_.emb), channel_id=1, source_target_pairs={{32,0},{48,16},{0,32},{16,48},{96,64},{112,80},{64,96},{80,112},{3... | collective-permute-start | bytes 73736 | tf_op jit(solution)/shard_map/ppermute | solution.py:35
  75.6 5.0 %collective-permute-start.19 = (f32[8,768]{1,0:T(8,128)S(1)}, f32[8,768]{1,0:T(8,128)S(1)}, u32[]{:S(2)}, u32[]{:S(2)}) collective-permute-start(f32[8,768]{1,0:T(8,128)S(1)} %get-tuple-element.84.refs_0_.emb), channel_id=1, source_target_pairs={{48,0},{0,16},{16,32},{32,48},{112,64},{64,80},{80,96},{96,112},{4... | collective-permute-start | bytes 73736 | tf_op jit(solution)/shard_map/ppermute | solution.py:35
  76.3 4.4 %collective-permute-start.18 = (f32[8,768]{1,0:T(8,128)S(1)}, f32[8,768]{1,0:T(8,128)S(1)}, u32[]{:S(2)}, u32[]{:S(2)}) collective-permute-start(f32[8,768]{1,0:T(8,128)S(1)} %get-tuple-element.84.refs_0_.emb), channel_id=1, source_target_pairs={{16,0},{32,16},{48,32},{0,48},{80,64},{96,80},{112,96},{64,112},{1... | collective-permute-start | bytes 73736 | tf_op jit(solution)/shard_map/ppermute | solution.py:35
  82.4 5.8 %collective-permute-start.23 = (f32[16,1024]{1,0:T(8,128)S(1)}, f32[16,1024]{1,0:T(8,128)S(1)}, u32[]{:S(2)}, u32[]{:S(2)}) collective-permute-start(f32[16,1024]{1,0:T(8,128)S(1)} %get-tuple-element.89.refs_0_), channel_id=1, source_target_pairs={{8,0},{9,1},{10,2},{11,3},{12,4},{13,5},{14,6},{15,7},{0,8},{1,9},... | collective-permute-start | bytes 196616 | tf_op jit(solution)/shard_map/ppermute | solution.py:31
  83.9 5.5 %collective-permute-start.22 = (f32[16,1024]{1,0:T(8,128)S(1)}, f32[16,1024]{1,0:T(8,128)S(1)}, u32[]{:S(2)}, u32[]{:S(2)}) collective-permute-start(f32[16,1024]{1,0:T(8,128)S(1)} %get-tuple-element.89.refs_0_), channel_id=1, source_target_pairs={{12,0},{13,1},{14,2},{15,3},{0,4},{1,5},{2,6},{3,7},{4,8},{5,9},{6... | collective-permute-start | bytes 196616 | tf_op jit(solution)/shard_map/ppermute | solution.py:31
  86.5 4.3 %collective-permute-start.21 = (f32[16,1024]{1,0:T(8,128)S(1)}, f32[16,1024]{1,0:T(8,128)S(1)}, u32[]{:S(2)}, u32[]{:S(2)}) collective-permute-start(f32[16,1024]{1,0:T(8,128)S(1)} %get-tuple-element.89.refs_0_), channel_id=1, source_target_pairs={{4,0},{5,1},{6,2},{7,3},{8,4},{9,5},{10,6},{11,7},{12,8},{13,9},{1... | collective-permute-start | bytes 196616 | tf_op jit(solution)/shard_map/ppermute | solution.py:31
  90.9 9.0 %collective-permute-start.26 = (f32[16,1024]{1,0:T(8,128)S(1)}, f32[16,1024]{1,0:T(8,128)S(1)}, u32[]{:S(2)}, u32[]{:S(2)}) collective-permute-start(f32[16,1024]{1,0:T(8,128)S(1)} %merge.1.s0), channel_id=1, source_target_pairs={{2,0},{3,1},{0,2},{1,3},{6,4},{7,5},{4,6},{5,7},{10,8},{11,9},{8,1... | collective-permute-start | bytes 196616 | tf_op jit(solution)/shard_map/ppermute | solution.py:45
  93.4 6.4 %collective-permute-start.25 = (f32[16,1024]{1,0:T(8,128)S(1)}, f32[16,1024]{1,0:T(8,128)S(1)}, u32[]{:S(2)}, u32[]{:S(2)}) collective-permute-start(f32[16,1024]{1,0:T(8,128)S(1)} %merge.1.s0), channel_id=1, source_target_pairs={{66,0},{67,1},{64,2},{65,3},{70,4},{71,5},{68,6},{69,7},{74,8},{75... | collective-permute-start | bytes 196616 | tf_op jit(solution)/shard_map/ppermute | solution.py:45
  95.1 4.8 %collective-permute-start.24 = (f32[16,1024]{1,0:T(8,128)S(1)}, f32[16,1024]{1,0:T(8,128)S(1)}, u32[]{:S(2)}, u32[]{:S(2)}) collective-permute-start(f32[16,1024]{1,0:T(8,128)S(1)} %merge.1.s0), channel_id=1, source_target_pairs={{64,0},{65,1},{66,2},{67,3},{68,4},{69,5},{70,6},{71,7},{72,8},{73... | collective-permute-start | bytes 196616 | tf_op jit(solution)/shard_map/ppermute | solution.py:45
  102.7 2.1 %collective-permute-start.27 = (bf16[384,768]{1,0:T(8,128)(2,1)S(1)}, bf16[384,768]{1,0:T(8,128)(2,1)S(1)}, u32[]{:S(2)}, u32[]{:S(2)}) collective-permute-start(bf16[384,768]{1,0:T(8,128)(2,1)S(1)} %get-tuple-element.100), channel_id=1, source_target_pairs={{0,1},{1,0},{2,3},{3,2},{4,5},{5,4},{6,7},{7,6},{8,9},{9,8},{10,11... | collective-permute-start | bytes 1769480 | tf_op jit(solution)/shard_map/ppermute | solution.py:26
  104.9 6.8 %collective-permute-start.28 = (bf16[96,768]{1,0:T(8,128)(2,1)S(1)}, bf16[96,768]{1,0:T(8,128)(2,1)S(1)}, u32[]{:S(2)}, u32[]{:S(2)}) collective-permute-start(bf16[96,768]{1,0:T(8,128)(2,1)S(1)} %get-tuple-element.102), channel_id=1, source_target_pairs={{32,0},{9,1},{34,2},{11,3},{36,4},{13,5},{38,6},{15,7},{40,8},{1,9... | collective-permute-start | bytes 442376 | tf_op jit(solution)/shard_map/ppermute | solution.py:56
  106.4 6.8 %collective-permute-start.29 = (bf16[96,768]{1,0:T(8,128)(2,1)S(1)}, bf16[96,768]{1,0:T(8,128)(2,1)S(1)}, u32[]{:S(2)}, u32[]{:S(2)}) collective-permute-start(bf16[96,768]{1,0:T(8,128)(2,1)S(1)} %get-tuple-element.103), channel_id=1, source_target_pairs={{48,0},{13,1},{50,2},{15,3},{52,4},{1,5},{54,6},{3,7},{56,8},{5,9}... | collective-permute-start | bytes 442376 | tf_op jit(solution)/shard_map/ppermute | solution.py:56
  109.0 5.1 %collective-permute-start.30 = (bf16[96,768]{1,0:T(8,128)(2,1)S(1)}, bf16[96,768]{1,0:T(8,128)(2,1)S(1)}, u32[]{:S(2)}, u32[]{:S(2)}) collective-permute-start(bf16[96,768]{1,0:T(8,128)(2,1)S(1)} %get-tuple-element.104), channel_id=1, source_target_pairs={{16,0},{5,1},{18,2},{7,3},{20,4},{9,5},{22,6},{11,7},{24,8},{13,9}... | collective-permute-start | bytes 442376 | tf_op jit(solution)/shard_map/ppermute | solution.py:56
  114.3 5.9 %collective-permute-start.31 = (f32[24,768]{1,0:T(8,128)S(1)}, f32[24,768]{1,0:T(8,128)S(1)}, u32[]{:S(2)}, u32[]{:S(2)}) collective-permute-start(f32[24,768]{1,0:T(8,128)S(1)} %get-tuple-element.106), channel_id=1, source_target_pairs={{8,0},{33,1},{10,2},{35,3},{12,4},{37,5},{14,6},{39,7},{0,8},{41,9... | collective-permute-start | bytes 221192 | tf_op jit(solution)/shard_map/ppermute | solution.py:56
  115.8 5.6 %collective-permute-start.32 = (f32[24,768]{1,0:T(8,128)S(1)}, f32[24,768]{1,0:T(8,128)S(1)}, u32[]{:S(2)}, u32[]{:S(2)}) collective-permute-start(f32[24,768]{1,0:T(8,128)S(1)} %get-tuple-element.107), channel_id=1, source_target_pairs={{12,0},{49,1},{14,2},{51,3},{0,4},{53,5},{2,6},{55,7},{4,8},{57,9}... | collective-permute-start | bytes 221192 | tf_op jit(solution)/shard_map/ppermute | solution.py:56
  117.0 4.4 %collective-permute-start.33 = (f32[24,768]{1,0:T(8,128)S(1)}, f32[24,768]{1,0:T(8,128)S(1)}, u32[]{:S(2)}, u32[]{:S(2)}) collective-permute-start(f32[24,768]{1,0:T(8,128)S(1)} %get-tuple-element.108), channel_id=1, source_target_pairs={{4,0},{17,1},{6,2},{19,3},{8,4},{21,5},{10,6},{23,7},{12,8},{25,9}... | collective-permute-start | bytes 221192 | tf_op jit(solution)/shard_map/ppermute | solution.py:56
  121.4 5.4 %collective-permute-start.34 = (f32[6,768]{1,0:T(8,128)S(1)}, f32[6,768]{1,0:T(8,128)S(1)}, u32[]{:S(2)}, u32[]{:S(2)}) collective-permute-start(f32[6,768]{1,0:T(8,128)S(1)} %get-tuple-element.110), channel_id=1, source_target_pairs={{2,0},{3,1},{0,2},{1,3},{6,4},{7,5},{4,6},{5,7},{10,8},{11,9},{8,1... | collective-permute-start | bytes 55304 | tf_op jit(solution)/shard_map/ppermute | solution.py:45
  121.9 5.1 %collective-permute-start.35 = (f32[6,768]{1,0:T(8,128)S(1)}, f32[6,768]{1,0:T(8,128)S(1)}, u32[]{:S(2)}, u32[]{:S(2)}) collective-permute-start(f32[6,768]{1,0:T(8,128)S(1)} %get-tuple-element.111), channel_id=1, source_target_pairs={{66,0},{67,1},{64,2},{65,3},{70,4},{71,5},{68,6},{69,7},{74,8},{75... | collective-permute-start | bytes 55304 | tf_op jit(solution)/shard_map/ppermute | solution.py:45
  124.6 3.8 %collective-permute-start.36 = (f32[6,768]{1,0:T(8,128)S(1)}, f32[6,768]{1,0:T(8,128)S(1)}, u32[]{:S(2)}, u32[]{:S(2)}) collective-permute-start(f32[6,768]{1,0:T(8,128)S(1)} %get-tuple-element.112), channel_id=1, source_target_pairs={{64,0},{65,1},{66,2},{67,3},{68,4},{69,5},{70,6},{71,7},{72,8},{73... | collective-permute-start | bytes 55304 | tf_op jit(solution)/shard_map/ppermute | solution.py:45
